TPU v7x, 256 devices: a whole 4x4x8 slice. The times are simulated.
256 devices in a mesh: section: 16 (over x_hi, z), dp: 16 (over y, x_lo, core).
Axes of the slice: x: 4 (x_hi: 2, x_lo: 2; x = x_hi * 2 + x_lo), y: 4, z: 8, core: 2. Of those that a mesh axis runs over, the one named last changes fastest.
Arguments:
- weight: bfloat16 [16, 2048, 2048], P('section', 'dp'), may hold values from -0.125 to 0.125
- gain: float32 [16, 2048], P('section'), may hold values from 0.1 to 1.9
- acts_in: bfloat16 [16, 2048, 2048], P('section', 'dp'), may hold values from -6 to 6
- grads_in: bfloat16 [16, 2048, 2048], P('section', 'dp'), may hold values from -0.59765625 to 0.59765625
- parked: bfloat16 [16, 3, 2048, 2048], P('section', None, 'dp'), may hold values from -6 to 6
- fetch_slot: int32 [16], replicated, may hold values from 0 to 2
- park_slot: int32 [16], replicated, may hold values from 0 to 2
Outputs:
- next_acts: bfloat16 [16, 2048, 2048], P('section', 'dp')
- next_grads: bfloat16 [16, 2048, 2048], P('section', 'dp')
- parked_out: bfloat16 [16, 3, 2048, 2048], P('section', None, 'dp')
- weight_grad: float32 [16, 2048, 2048], P('section', 'dp')
- gain_grad: float32 [16, 2048], P('section', 'dp')
All inputs are finite; a program needn't handle non-finite values.
Results may differ from a plain program's by a relative error of at most 0.02.
Values may be sent and summed in bfloat16 or wider, within the bound.
No kernel may reach another device: no remote copies, remote signals or barrier semaphores. Data moves between devices by JAX's collectives and lax.ppermute only.
A program may use at most 64 MiB of HBM per device.

v0:
```python
import jax
import jax.numpy as jnp
from jax import lax
from jax.sharding import PartitionSpec as P

EPSILON = 1e-05


def partner_2(block, axis, apart):
    count = lax.axis_size(axis)
    route = []
    for low in range(count):
        high = low | 1 << apart
        if high != low and high < count:
            route += [(low, high), (high, low)]
    return lax.ppermute(block, axis, route)


def shifted(block, axis, distance):
    devices = range(lax.axis_size(axis))
    route = [((i - distance) % len(devices), i) for i in devices]
    return lax.ppermute(block, axis, route)


def forward_rows(acts, gain_row, weight_mat):
    values = acts.astype(jnp.float32)
    inv_rms = lax.rsqrt(jnp.mean(values * values, -1, keepdims=True) + EPSILON)
    normed = (values * inv_rms * gain_row).astype(jnp.bfloat16)
    pre_act = jnp.dot(normed, weight_mat, preferred_element_type=jnp.float32)
    return (values + jax.nn.silu(pre_act)).astype(jnp.bfloat16)


def backward_rows(panel, grads, gain_row, weight_mat):
    values = panel.astype(jnp.float32)
    inv_rms = lax.rsqrt(jnp.mean(values * values, -1, keepdims=True) + EPSILON)
    unit_rows = values * inv_rms
    normed = (unit_rows * gain_row).astype(jnp.bfloat16)
    pre_act = jnp.dot(normed, weight_mat, preferred_element_type=jnp.float32)
    sigma = jax.nn.sigmoid(pre_act)
    grad_f = grads.astype(jnp.float32)
    delta = (grad_f * sigma * (1.0 + pre_act * (1.0 - sigma))).astype(jnp.bfloat16)
    back_rows = lax.dot_general(
        delta, weight_mat, (((1,), (1,)), ((), ())), preferred_element_type=jnp.float32
    )
    through = back_rows * gain_row
    grad_acts = (
        grad_f + inv_rms * (through - unit_rows * jnp.mean(through * unit_rows, -1, keepdims=True))
    ).astype(jnp.bfloat16)
    return (grad_acts, normed, delta, jnp.sum(back_rows * unit_rows, 0))


def shards(weight, gain, acts_in, grads_in, parked, fetch_slot, park_slot):
    sections = lax.axis_size("section")
    position = lax.axis_index("section")
    partner = sections - 1 - position
    held = parked[0]
    send_slot = lax.dynamic_index_in_dim(fetch_slot, partner, 0, keepdims=False)
    write_slot = lax.dynamic_index_in_dim(park_slot, partner, 0, keepdims=False)
    outgoing = jnp.stack([lax.dynamic_index_in_dim(held, send_slot, 0, keepdims=False), acts_in[0]])
    levels = sections.bit_length() - 1
    for level in range(levels):
        outgoing = partner_2(outgoing, "section", level)
    full_weight = lax.all_gather(weight[0], "dp", axis=0, tiled=True)
    gain_row = gain[0]
    out_rows = forward_rows(acts_in[0], gain_row, full_weight)
    next_acts = shifted(out_rows, "section", 1)
    grad_acts, normed, delta, gain_local = backward_rows(
        outgoing[0], grads_in[0], gain_row, full_weight
    )
    next_grads = shifted(grad_acts, "section", -1)
    parked_out = lax.dynamic_update_index_in_dim(held, outgoing[1], write_slot, 0)
    weight_local = lax.dot_general(
        normed, delta, (((0,), (0,)), ((), ())), preferred_element_type=jnp.float32
    )
    weight_grad, gain_grad = (
        lax.psum_scatter(
            weight_local.astype(jnp.bfloat16), "dp", scatter_dimension=0, tiled=True
        ).astype(jnp.float32),
        lax.psum_scatter(
            gain_local.astype(jnp.bfloat16), "dp", scatter_dimension=0, tiled=True
        ).astype(jnp.float32),
    )
    return (next_acts[None], next_grads[None], parked_out[None], weight_grad[None], gain_grad[None])


def solution(mesh):
    return jax.shard_map(
        shards,
        mesh=mesh,
        in_specs=(
            P("section", "dp", None),
            P("section", None),
            P("section", "dp", None),
            P("section", "dp", None),
            P("section", None, "dp", None),
            P(),
            P(),
        ),
        out_specs=(
            P("section", "dp", None),
            P("section", "dp", None),
            P("section", None, "dp", None),
            P("section", "dp", None),
            P("section", "dp"),
        ),
        check_vma=False,
    )
```

profile of v0, /device:TPU:1, one launch (start us, length us, event | category | flops | bytes accessed | tf_op | source)
XLA Modules:
  0.0 296.2 jit_solution(14008057013348368079)
XLA Ops:
  7.2 1.4 copy.16
  8.7 1.3 dynamic_slice.13
  12.0 1.1 pad_maximum_fusion
  13.1 2.6 collective-permute-start.1
  15.7 21.8 %collective-permute-done.1 = bf16[2,128,2048]{2,1,0:T(8,128)(2,1)S(1)} collective-permute-done((bf16[2,128,2048]{2,1,0:T(8,128)(2,1)S(1)}, bf16[2,128,2048]{2,1,0:T(8,128)(2,1)S(1)}, u32[]{:S(2)}, u32[]{:S(2)}) %collective-permute-start.1) | collective-permute-done | bytes 1048608 | tf_op jit(solution)/shard_map/ppermute | solution.py:16
  37.5 4.0 %collective-permute-start.2 = (bf16[2,128,2048]{2,1,0:T(8,128)(2,1)S(1)}, bf16[2,128,2048]{2,1,0:T(8,128)(2,1)S(1)}, u32[]{:S(2)}, u32[]{:S(2)}) collective-permute-start(bf16[2,128,2048]{2,1,0:T(8,128)(2,1)S(1)} %collective-permute-done.1), channel_id=1, source_target_pairs={{0,32},{32,0},{16,48},{48,16},{64,96},{96,64},{80,112},{112,80},{1... | collective-permute-start | bytes 3145736 | tf_op jit(solution)/shard_map/ppermute | solution.py:16
  41.5 45.1 %collective-permute-done.2 = bf16[2,128,2048]{2,1,0:T(8,128)(2,1)S(1)} collective-permute-done((bf16[2,128,2048]{2,1,0:T(8,128)(2,1)S(1)}, bf16[2,128,2048]{2,1,0:T(8,128)(2,1)S(1)}, u32[]{:S(2)}, u32[]{:S(2)}) %collective-permute-start.2) | collective-permute-done | bytes 1048608 | tf_op jit(solution)/shard_map/ppermute | solution.py:16
  86.6 6.4 %collective-permute-start.3 = (bf16[2,128,2048]{2,1,0:T(8,128)(2,1)S(1)}, bf16[2,128,2048]{2,1,0:T(8,128)(2,1)S(1)}, u32[]{:S(2)}, u32[]{:S(2)}) collective-permute-start(bf16[2,128,2048]{2,1,0:T(8,128)(2,1)S(1)} %collective-permute-done.2), channel_id=1, source_target_pairs={{0,64},{64,0},{16,80},{80,16},{32,96},{96,32},{48,112},{112,48},{1... | collective-permute-start | bytes 3145736 | tf_op jit(solution)/shard_map/ppermute | solution.py:16
  93.0 45.4 %collective-permute-done.3 = bf16[2,128,2048]{2,1,0:T(8,128)(2,1)S(1)} collective-permute-done((bf16[2,128,2048]{2,1,0:T(8,128)(2,1)S(1)}, bf16[2,128,2048]{2,1,0:T(8,128)(2,1)S(1)}, u32[]{:S(2)}, u32[]{:S(2)}) %collective-permute-start.3) | collective-permute-done | bytes 1048608 | tf_op jit(solution)/shard_map/ppermute | solution.py:16
  138.4 2.7 collective-permute-start.4
  141.1 21.7 %collective-permute-done.4 = bf16[2,128,2048]{2,1,0:T(8,128)(2,1)S(1)} collective-permute-done((bf16[2,128,2048]{2,1,0:T(8,128)(2,1)S(1)}, bf16[2,128,2048]{2,1,0:T(8,128)(2,1)S(1)}, u32[]{:S(2)}, u32[]{:S(2)}) %collective-permute-start.4) | collective-permute-done | bytes 1048608 | tf_op jit(solution)/shard_map/ppermute | solution.py:16
  163.1 4.7 %fusion.2 = f32[128,2048]{1,0:T(8,128)S(1)} fusion(bf16[1,2048,2048]{2,1,0:T(8,128)(2,1)} %all-gather.3.cloned.1.call-done, f32[128]{0:T(128)S(1)} %add_rsqrt_fusion, f32[2048]{0:T(1024)} %bitcast.66, bf16[2,128,2048]{2,1,0:T(8,128)(2,1)S(1)} %collective-permute-done.4), kind=kOutput, calls=%fused_computation.2 | convolution fusion | flops 1074790400 | bytes 9970176 | tf_op jit(solution)/shard_map/dot_general | solution.py:38
  167.9 5.7 %convolution_convert_fusion = bf16[2048,2048]{1,0:T(8,128)(2,1)} fusion(f32[128,2048]{1,0:T(8,128)S(1)} %fusion.2, bf16[1,128,2048]{2,1,0:T(8,128)(2,1)S(1)} %copy-done.1, f32[128]{0:T(128)S(1)} %add_rsqrt_fusion, f32[2048]{0:T(1024)S(1)} %bitcast.67, bf16[2,128,2048]{2,1,0:T(8,128)(2,1)S(1)} %collective-permute-done.4), kind=kOutput, calls=%fused_computation.6 | convolution fusion | flops 1081606144 | bytes 10494464 | tf_op jit(solution)/shard_map/dot_general | solution.py:72
  173.7 0.6 dynamic_slice.16
  177.7 5.6 %fusion.22 = bf16[128,2048]{1,0:T(8,128)(2,1)} fusion(bf16[1,2048,2048]{2,1,0:T(8,128)(2,1)} %all-gather.3.cloned.1.call-done, bf16[1,128,2048]{2,1,0:T(8,128)(2,1)S(1)} %copy-done.2, f32[2048]{0:T(1024)S(1)} %bitcast.68, f32[128]{0:T(128)S(1)} %add_rsqrt_fusion.1), kind=kOutput, calls=%fused_computation.30 | convolution fusion | flops 1076625408 | bytes 9445888 | tf_op jit(solution)/shard_map/dot_general | solution.py:29
  183.3 6.5 %fusion.17 = (bf16[2048]{0:T(1024)(128)(2,1)S(1)}, f32[128]{0:T(128)S(1)}, f32[128,2048]{1,0:T(8,128)S(1)}) fusion(f32[128]{0:T(128)S(1)} %add_rsqrt_fusion, bf16[2,128,2048]{2,1,0:T(8,128)(2,1)S(1)} %collective-permute-done.4, f32[2048]{0:T(1024)S(1)} %bitcast.69, bf16[1,2048,2048]{2,1,0:T(8,128)(2,1)} %all-gather.3.cloned.1.call-done, ...), kind=kOutput, calls=%fused_computation.25 | convolution fusion | flops 1078196096 | bytes 11547648 | tf_op jit(solution)/shard_map/dot_general | solution.py:42
  190.2 7.3 %collective-permute-start.5 = (bf16[128,2048]{1,0:T(8,128)(2,1)S(1)}, bf16[128,2048]{1,0:T(8,128)(2,1)S(1)}, u32[]{:S(2)}, u32[]{:S(2)}) collective-permute-start(bf16[128,2048]{1,0:T(8,128)(2,1)S(1)} %fusion.12), channel_id=1, source_target_pairs={{16,0},{32,16},{48,32},{64,48},{80,64},{96,80},{112,96},{128,112},... | collective-permute-start | bytes 1572872 | tf_op jit(solution)/shard_map/ppermute | solution.py:22
  197.5 0.8 fusion.28
  198.4 29.0 %all-reduce = bf16[2048]{0:T(1024)(128)(2,1)S(1)} all-reduce(bf16[2048]{0:T(1024)(128)(2,1)S(1)} %get-tuple-element.5), channel_id=4, replica_groups=mesh['section'=16,'dp'=16] {'dp'}, use_global_device_ids=true, to_apply=%region_5.6.clone | all-reduce | flops 2048 | bytes 8192
  227.4 0.6 bitcast_convert_fusion.1
  228.0 57.7 %reduce-scatter.2.cloned.1.call-done = bf16[128,2048]{1,0:T(8,128)(2,1)} async-done(((bf16[2048,2048]{1,0:T(8,128)(2,1)}), bf16[128,2048]{1,0:T(8,128)(2,1)}) %reduce-scatter.2.cloned.1.call-update) | async-done | bytes 524304 | tf_op jit(solution)/shard_map/reduce_scatter | solution.py:76
  285.6 2.1 bitcast_convert_fusion
  287.8 0.8 copy.17
  288.6 0.8 copy.18
  (28 shorter events, 1.6 us)
Async XLA Ops:
  7.2 155.9 %all-gather.3.cloned.1.call-start = ((), (), s32[]{:S(2)}) async-start(), calls=%async_computation.2 | async-start | bytes 8912896 | tf_op jit(solution)/shard_map/all_gather | solution.py:63
  8.6 84.4 %copy-start = (bf16[1,3,128,2048]{3,2,1,0:T(8,128)(2,1)}, bf16[1,3,128,2048]{3,2,1,0:T(8,128)(2,1)S(1)}, u32[]{:S(2)}) copy-start(bf16[1,3,128,2048]{3,2,1,0:T(8,128)(2,1)S(1)} %copy.16) | copy-start | bytes 4718596
  8.6 277.0 %reduce-scatter.2.cloned.1.call-start = ((), (), s32[]{:S(2)}) async-start(), calls=%async_computation.1 | async-start | bytes 8912896 | tf_op jit(solution)/shard_map/reduce_scatter | solution.py:76
  13.1 24.4 %collective-permute-start.1 = (bf16[2,128,2048]{2,1,0:T(8,128)(2,1)S(1)}, bf16[2,128,2048]{2,1,0:T(8,128)(2,1)S(1)}, u32[]{:S(2)}, u32[]{:S(2)}) collective-permute-start(bf16[2,128,2048]{2,1,0:T(8,128)(2,1)S(1)} %pad_maximum_fusion), channel_id=1, source_target_pairs={{0,16},{16,0},{32,48},{48,32},{64,80},{80,64},{96,112},{112,96},{1... | collective-permute-start | bytes 3145736 | tf_op jit(solution)/shard_map/ppermute | solution.py:16
  37.5 49.1 %collective-permute-start.2 = (bf16[2,128,2048]{2,1,0:T(8,128)(2,1)S(1)}, bf16[2,128,2048]{2,1,0:T(8,128)(2,1)S(1)}, u32[]{:S(2)}, u32[]{:S(2)}) collective-permute-start(bf16[2,128,2048]{2,1,0:T(8,128)(2,1)S(1)} %collective-permute-done.1), channel_id=1, source_target_pairs={{0,32},{32,0},{16,48},{48,16},{64,96},{96,64},{80,112},{112,80},{1... | collective-permute-start | bytes 3145736 | tf_op jit(solution)/shard_map/ppermute | solution.py:16
  86.6 51.8 %collective-permute-start.3 = (bf16[2,128,2048]{2,1,0:T(8,128)(2,1)S(1)}, bf16[2,128,2048]{2,1,0:T(8,128)(2,1)S(1)}, u32[]{:S(2)}, u32[]{:S(2)}) collective-permute-start(bf16[2,128,2048]{2,1,0:T(8,128)(2,1)S(1)} %collective-permute-done.2), channel_id=1, source_target_pairs={{0,64},{64,0},{16,80},{80,16},{32,96},{96,32},{48,112},{112,48},{1... | collective-permute-start | bytes 3145736 | tf_op jit(solution)/shard_map/ppermute | solution.py:16
  138.4 24.5 %collective-permute-start.4 = (bf16[2,128,2048]{2,1,0:T(8,128)(2,1)S(1)}, bf16[2,128,2048]{2,1,0:T(8,128)(2,1)S(1)}, u32[]{:S(2)}, u32[]{:S(2)}) collective-permute-start(bf16[2,128,2048]{2,1,0:T(8,128)(2,1)S(1)} %collective-permute-done.3), channel_id=1, source_target_pairs={{0,128},{128,0},{16,144},{144,16},{32,160},{160,32},{48,176},{176,... | collective-permute-start | bytes 3145736 | tf_op jit(solution)/shard_map/ppermute | solution.py:16
  163.0 4.8 %copy-start.1 = (bf16[1,128,2048]{2,1,0:T(8,128)(2,1)S(1)}, bf16[1,128,2048]{2,1,0:T(8,128)(2,1)}, u32[]{:S(2)}) copy-start(bf16[1,128,2048]{2,1,0:T(8,128)(2,1)} %param.10) | copy-start | bytes 1572868
  163.0 4.8 %copy-start.3 = (f32[1,2048]{1,0:T(1,128)S(1)}, f32[1,2048]{1,0:T(1,128)}, u32[]{:S(2)}) copy-start(f32[1,2048]{1,0:T(1,128)} %param.8) | copy-start | bytes 24580
  167.9 5.8 %copy-start.4 = (s32[16]{0:T(128)S(1)}, s32[16]{0:T(128)}, u32[]{:S(2)}) copy-start(s32[16]{0:T(128)} %param.13) | copy-start | bytes 196
  167.9 7.7 %copy-start.5 = (u32[256]{0:T(256)S(1)}, u32[256]{0:T(256)}, u32[]{:S(2)}) copy-start(u32[256]{0:T(256)} %constant.47) | copy-start | bytes 3076
  167.9 9.6 %copy-start.2 = (bf16[1,128,2048]{2,1,0:T(8,128)(2,1)S(1)}, bf16[1,128,2048]{2,1,0:T(8,128)(2,1)}, u32[]{:S(2)}) copy-start(bf16[1,128,2048]{2,1,0:T(8,128)(2,1)} %param.9) | copy-start | bytes 1572868
  183.3 44.7 %collective-permute-start = (bf16[128,2048]{1,0:T(8,128)(2,1)}, bf16[128,2048]{1,0:T(8,128)(2,1)S(1)}, u32[]{:S(2)}, u32[]{:S(2)}) collective-permute-start(bf16[128,2048]{1,0:T(8,128)(2,1)} %fusion.22), channel_id=1, source_target_pairs={{240,0},{0,16},{16,32},{32,48},{48,64},{64,80},{80,96},{96,112},{1... | collective-permute-start | bytes 1572872 | tf_op jit(solution)/shard_map/ppermute | solution.py:22
  190.2 37.8 %collective-permute-start.5 = (bf16[128,2048]{1,0:T(8,128)(2,1)S(1)}, bf16[128,2048]{1,0:T(8,128)(2,1)S(1)}, u32[]{:S(2)}, u32[]{:S(2)}) collective-permute-start(bf16[128,2048]{1,0:T(8,128)(2,1)S(1)} %fusion.12), channel_id=1, source_target_pairs={{16,0},{32,16},{48,32},{64,48},{80,64},{96,80},{112,96},{128,112},... | collective-permute-start | bytes 1572872 | tf_op jit(solution)/shard_map/ppermute | solution.py:22
Sparse Core Ops, SparseCore 0:
  9.9 58.8 all-gather.2
  173.8 111.8 reduce-scatter.1
where the time goes:
time: 297 us; the launch traced here: 296 us
  waiting for transfers between devices  192 us (65%)
  blocking collectives  29 us (10%)
  starting transfers between devices  23.2 us (8%)
  matrix products  22.6 us (8%)
  between operations  18.7 us (6%)
  local copies, waits for them, and re-layouts  6.34 us (2%)
  other arithmetic  4.65 us (2%)
    ppermute x4, waiting for transfers between devices, partner_2(): return lax.ppermute(block, axis, route)  134 us
    reduce_scatter x1, waiting for transfers between devices, shards(): lax.psum_scatter(weight_local.astype(jnp.bfloat16), 'dp', scatter_dimensi...  57.7 us
    unnamed x1, blocking collectives  29 us
    ppermute x4, starting transfers between devices, partner_2(): return lax.ppermute(block, axis, route)  15.8 us
    ppermute x2, starting transfers between devices, shifted(): return lax.ppermute(block, axis, route)  7.34 us
    dot_general x1, matrix products, backward_rows(): lax.dot_general(delta, weight_mat, (((1,), (1,)), ((), ())), preferred_el...  6.47 us
  transfers between devices with their start and end apart: 8, of which 5 were waited for; matrix products, arithmetic and copies ran while one was open for 6% of the time, Pallas kernels for 0%

commit v1 on v0

v1 whole, which is shorter than its diff:
```python
import jax
import jax.numpy as jnp
from jax import lax
from jax.sharding import PartitionSpec as P

EPSILON = 1e-05


def mirrored(block, axis):
    count = lax.axis_size(axis)
    return lax.ppermute(block, axis, [(i, count - 1 - i) for i in range(count)])


def shifted(block, axis, distance):
    devices = range(lax.axis_size(axis))
    route = [((i - distance) % len(devices), i) for i in devices]
    return lax.ppermute(block, axis, route)


def forward_rows(acts, gain_row, weight_mat):
    values = acts.astype(jnp.float32)
    inv_rms = lax.rsqrt(jnp.mean(values * values, -1, keepdims=True) + EPSILON)
    normed = (values * inv_rms * gain_row).astype(jnp.bfloat16)
    pre_act = jnp.dot(normed, weight_mat, preferred_element_type=jnp.float32)
    return (values + jax.nn.silu(pre_act)).astype(jnp.bfloat16)


def shards(weight, gain, acts_in, grads_in, parked, fetch_slot, park_slot):
    sections = lax.axis_size("section")
    position = lax.axis_index("section")
    member = lax.axis_index("dp")
    partner = sections - 1 - position
    held = parked[0]
    tokens, width = acts_in.shape[1:]
    own_width = weight.shape[1]
    send_slot = lax.dynamic_index_in_dim(fetch_slot, partner, 0, keepdims=False)
    write_slot = lax.dynamic_index_in_dim(park_slot, partner, 0, keepdims=False)
    gain_row = gain[0]

    panel = mirrored(lax.dynamic_index_in_dim(held, send_slot, 0, keepdims=False), "section")
    full_weight = lax.all_gather(weight[0], "dp", axis=0, tiled=True)
    stashed = mirrored(acts_in[0], "section")

    values = panel.astype(jnp.float32)
    inv_rms = lax.rsqrt(jnp.mean(values * values, -1, keepdims=True) + EPSILON)
    unit_rows = values * inv_rms
    normed = (unit_rows * gain_row).astype(jnp.bfloat16)
    own_units = lax.all_to_all(
        unit_rows.astype(jnp.bfloat16), "dp", split_axis=1, concat_axis=0, tiled=True
    )
    pre_act = jnp.dot(normed, full_weight, preferred_element_type=jnp.float32)
    sigma = jax.nn.sigmoid(pre_act)
    grad_f = grads_in[0].astype(jnp.float32)
    delta = (grad_f * sigma * (1.0 + pre_act * (1.0 - sigma))).astype(jnp.bfloat16)
    all_delta = lax.all_gather(delta, "dp", axis=0, tiled=True)

    out_rows = forward_rows(acts_in[0], gain_row, full_weight)
    next_acts = shifted(out_rows, "section", 1)

    back_rows = lax.dot_general(
        delta, full_weight, (((1,), (1,)), ((), ())), preferred_element_type=jnp.float32
    )
    through = back_rows * gain_row
    grad_acts = (
        grad_f + inv_rms * (through - unit_rows * jnp.mean(through * unit_rows, -1, keepdims=True))
    ).astype(jnp.bfloat16)
    next_grads = shifted(grad_acts, "section", -1)
    parked_out = lax.dynamic_update_index_in_dim(held, stashed, write_slot, 0)

    outer = lax.dot_general(
        own_units, all_delta, (((0,), (0,)), ((), ())), preferred_element_type=jnp.float32
    )
    own_gain = lax.dynamic_slice_in_dim(gain_row, member * own_width, own_width)
    weight_grad = outer * own_gain[:, None]
    gain_grad = jnp.sum(outer * weight[0].astype(jnp.float32), -1)
    return (next_acts[None], next_grads[None], parked_out[None], weight_grad[None], gain_grad[None])


def solution(mesh):
    return jax.shard_map(
        shards,
        mesh=mesh,
        in_specs=(
            P("section", "dp", None),
            P("section", None),
            P("section", "dp", None),
            P("section", "dp", None),
            P("section", None, "dp", None),
            P(),
            P(),
        ),
        out_specs=(
            P("section", "dp", None),
            P("section", "dp", None),
            P("section", None, "dp", None),
            P("section", "dp", None),
            P("section", "dp"),
        ),
        check_vma=False,
    )
```

time: 297 us -> 186 us (0.63)
  waiting for transfers between devices: 192 us -> 115 us
  blocking collectives: 29 us -> 0 us
  matrix products: 22.6 us -> 19.6 us
    ppermute x4 -> x2, waiting for transfers between devices: 134 us -> 40 us  [mirrored(): return lax.ppermute(block, axis, [(i, count - 1 - i) for i in range(count)])]
    reduce_scatter x1 -> x0, waiting for transfers between devices: 57.7 us -> none  [shards(): lax.psum_scatter(weight_local.astype(jnp.bfloat16), 'dp', scatter_dimensi...]
    all_gather x0 -> x1, waiting for transfers between devices: none -> 33.3 us  [shards(): all_delta = lax.all_gather(delta, 'dp', axis=0, tiled=True)]
    unnamed x1 -> x0, blocking collectives: 29 us -> none
    all_gather x1, waiting for transfers between devices: 0.02 us -> 21.2 us  [shards(): full_weight = lax.all_gather(weight[0], 'dp', axis=0, tiled=True)]
    all_to_all x0 -> x1, waiting for transfers between devices: none -> 14 us  [shards(): lax.all_to_all(unit_rows.astype(jnp.bfloat16), 'dp', split_axis=1, concat...]
    ppermute x2, waiting for transfers between devices: 0.01 us -> 6.17 us  [shifted(): return lax.ppermute(block, axis, route)]
    all_to_all x0 -> x1, starting transfers between devices: none -> 4.93 us  [shards(): lax.all_to_all(unit_rows.astype(jnp.bfloat16), 'dp', split_axis=1, concat...]
  transfers between devices with their start and end apart: 8 -> 7, of which waited for: 5 -> 6; matrix products, arithmetic and copies ran while one was open for 6% -> 5% of each run, Pallas kernels for 0% -> 0%
where the time goes in v1:
time: 186 us
  waiting for transfers between devices  115 us (62%)
  starting transfers between devices  23.5 us (13%)
  matrix products  19.6 us (11%)
  between operations  18 us (10%)
  local copies, waits for them, and re-layouts  7.52 us (4%)
  other arithmetic  2.24 us (1%)
    ppermute x2, waiting for transfers between devices, mirrored(): return lax.ppermute(block, axis, [(i, count - 1 - i) for i in range(count)])  40 us
    all_gather x1, waiting for transfers between devices, shards(): all_delta = lax.all_gather(delta, 'dp', axis=0, tiled=True)  33.3 us
    all_gather x1, waiting for transfers between devices, shards(): full_weight = lax.all_gather(weight[0], 'dp', axis=0, tiled=True)  21.2 us
    all_to_all x1, waiting for transfers between devices, shards(): lax.all_to_all(unit_rows.astype(jnp.bfloat16), 'dp', split_axis=1, concat...  14 us
    ppermute x2, starting transfers between devices, mirrored(): return lax.ppermute(block, axis, [(i, count - 1 - i) for i in range(count)])  13.4 us
    ppermute x2, waiting for transfers between devices, shifted(): return lax.ppermute(block, axis, route)  6.17 us
    dot_general x1, matrix products, shards(): lax.dot_general(own_units, all_delta, (((0,), (0,)), ((), ())), preferred...  6.14 us
    dot_general x1, matrix products, forward_rows(): pre_act = jnp.dot(normed, weight_mat, preferred_element_type=jnp.float32)  5.68 us
  transfers between devices with their start and end apart: 7, of which 6 were waited for; matrix products, arithmetic and copies ran while one was open for 5% of the time, Pallas kernels for 0%

profile of v1, /device:TPU:1, one launch (start us, length us, event | category | flops | bytes accessed | tf_op | source)
XLA Modules:
  0.0 185.7 jit_solution(747904167445929783)
XLA Ops:
  7.2 1.4 copy.20
  8.7 9.0 %collective-permute-start.3 = (bf16[128,2048]{1,0:T(8,128)(2,1)}, bf16[128,2048]{1,0:T(8,128)(2,1)S(1)}, u32[]{:S(2)}, u32[]{:S(2)}) collective-permute-start(bf16[128,2048]{1,0:T(8,128)(2,1)} %bitcast.55), channel_id=1, source_target_pairs={{0,240},{16,224},{32,208},{48,192},{64,176},{80,160},{96,144},{112... | collective-permute-start | bytes 1572872 | tf_op jit(solution)/shard_map/ppermute | solution.py:11
  17.6 1.2 dynamic_slice.16
  20.2 1.2 dynamic_slice.14
  24.0 28.4 %collective-permute-done.3 = bf16[128,2048]{1,0:T(8,128)(2,1)S(1)} collective-permute-done((bf16[128,2048]{1,0:T(8,128)(2,1)}, bf16[128,2048]{1,0:T(8,128)(2,1)S(1)}, u32[]{:S(2)}, u32[]{:S(2)}) %collective-permute-start.3) | collective-permute-done | bytes 524320 | tf_op jit(solution)/shard_map/ppermute | solution.py:11
  52.5 4.5 %collective-permute-start.1 = (bf16[128,2048]{1,0:T(8,128)(2,1)S(1)}, bf16[128,2048]{1,0:T(8,128)(2,1)S(1)}, u32[]{:S(2)}, u32[]{:S(2)}) collective-permute-start(bf16[128,2048]{1,0:T(8,128)(2,1)S(1)} %get-tuple-element.6), channel_id=1, source_target_pairs={{0,240},{16,224},{32,208},{48,192},{64,176},{80,160},{96,144},{112... | collective-permute-start | bytes 1572872 | tf_op jit(solution)/shard_map/ppermute | solution.py:11
  57.0 11.7 %collective-permute-done.1 = bf16[128,2048]{1,0:T(8,128)(2,1)S(1)} collective-permute-done((bf16[128,2048]{1,0:T(8,128)(2,1)S(1)}, bf16[128,2048]{1,0:T(8,128)(2,1)S(1)}, u32[]{:S(2)}, u32[]{:S(2)}) %collective-permute-start.1) | collective-permute-done | bytes 524320 | tf_op jit(solution)/shard_map/ppermute | solution.py:11
  68.9 21.2 %all-gather.6.cloned.1.call-done = bf16[1,2048,2048]{2,1,0:T(8,128)(2,1)} async-done(((bf16[1,128,2048]{2,1,0:T(8,128)(2,1)}), bf16[1,2048,2048]{2,1,0:T(8,128)(2,1)}) %all-gather.6.cloned.1.call-update) | async-done | bytes 8388624 | tf_op jit(solution)/shard_map/all_gather | solution.py:41
  90.1 4.8 %fusion.2 = f32[128,2048]{1,0:T(8,128)S(1)} fusion(bf16[1,2048,2048]{2,1,0:T(8,128)(2,1)} %all-gather.6.cloned.1.call-done, bf16[128,2048]{1,0:T(8,128)(2,1)S(1)} %collective-permute-done.1, f32[128]{0:T(128)S(1)} %add_rsqrt_fusion, f32[2048]{0:T(1024)} %bitcast.58), kind=kOutput, calls=%fused_computation.2 | convolution fusion | flops 1074790400 | bytes 9970176 | tf_op jit(solution)/shard_map/dot_general | solution.py:51
  95.0 1.0 slice-done.1
  96.0 2.9 %fusion.6 = f32[128,2048]{1,0:T(8,128)S(1)} fusion(bf16[1,2048,2048]{2,1,0:T(8,128)(2,1)S(1)} %bitcast.53, f32[128,2048]{1,0:T(8,128)S(1)} %fusion.2, bf16[1,128,2048]{2,1,0:T(8,128)(2,1)S(1)} %copy-done.2, f32[2048]{0:T(1024)S(1)} %bitcast.59), kind=kOutput, calls=%fused_computation.6 | convolution fusion | flops 1076625408 | bytes 11018240 | tf_op jit(solution)/shard_map/dot_general | solution.py:60
  98.9 0.3 fusion.31
  99.2 1.5 fusion.19
  100.8 0.2 fusion.21
  101.0 5.7 %fusion.24 = bf16[128,2048]{1,0:T(8,128)(2,1)} fusion(bf16[1,2048,2048]{2,1,0:T(8,128)(2,1)} %all-gather.6.cloned.1.call-done, f32[2048]{0:T(1024)S(1)} %bitcast.60, f32[128]{0:T(128)S(1)} %add_rsqrt_fusion.1, bf16[1,128,2048]{2,1,0:T(8,128)(2,1)S(1)} %copy-done.3), kind=kOutput, calls=%fused_computation.29 | convolution fusion | flops 1076625408 | bytes 9445888 | tf_op jit(solution)/shard_map/dot_general | solution.py:24
  106.7 5.1 %collective-permute-start.2 = (bf16[128,2048]{1,0:T(8,128)(2,1)S(1)}, bf16[128,2048]{1,0:T(8,128)(2,1)S(1)}, u32[]{:S(2)}, u32[]{:S(2)}) collective-permute-start(bf16[128,2048]{1,0:T(8,128)(2,1)S(1)} %get-tuple-element.12), channel_id=1, source_target_pairs={{16,0},{32,16},{48,32},{64,48},{80,64},{96,80},{112,96},{128,112},... | collective-permute-start | bytes 1572872 | tf_op jit(solution)/shard_map/ppermute | solution.py:17
  111.8 0.9 copy.15
  112.7 4.9 %all-to-all-start = ((bf16[128,16,128]{2,0,1:T(8,128)(2,1)}), bf16[128,16,128]{2,0,1:T(8,128)(2,1)S(1)}, u32[]{:S(2)}, u32[]{:S(2)}) async-start(bf16[128,16,128]{2,0,1:T(8,128)(2,1)} %bitcast.51), calls=%async_computation | async-start | bytes 1048576 | tf_op jit(solution)/shard_map/all_to_all | solution.py:48
  117.6 6.2 %collective-permute-done = bf16[128,2048]{1,0:T(8,128)(2,1)S(1)} collective-permute-done((bf16[128,2048]{1,0:T(8,128)(2,1)}, bf16[128,2048]{1,0:T(8,128)(2,1)S(1)}, u32[]{:S(2)}, u32[]{:S(2)}) %collective-permute-start) | collective-permute-done | bytes 524320 | tf_op jit(solution)/shard_map/ppermute | solution.py:17
  123.8 14.0 %all-to-all-done = bf16[128,16,128]{2,0,1:T(8,128)(2,1)S(1)} async-done(((bf16[128,16,128]{2,0,1:T(8,128)(2,1)}), bf16[128,16,128]{2,0,1:T(8,128)(2,1)S(1)}, u32[]{:S(2)}, u32[]{:S(2)}) %all-to-all-start) | async-done | bytes 524320 | tf_op jit(solution)/shard_map/all_to_all | solution.py:48
  137.8 33.3 %all-gather.4.cloned.1.call-done = bf16[2048,2048]{1,0:T(8,128)(2,1)} async-done(((bf16[128,2048]{1,0:T(8,128)(2,1)}), bf16[2048,2048]{1,0:T(8,128)(2,1)}) %all-gather.4.cloned.1.call-update) | async-done | bytes 8388624 | tf_op jit(solution)/shard_map/all_gather | solution.py:55
  171.1 6.1 %fusion.25 = (f32[128]{0:T(128)}, f32[1,128,2048]{2,1,0:T(8,128)}) fusion(bf16[1,128,2048]{2,1,0:T(8,128)(2,1)S(1)} %copy-done.1, f32[128]{0:T(128)S(1)} %fusion.38, bf16[2048,128]{1,0:T(8,128)(2,1)S(1)} %bitcast.54, bf16[2048,2048]{1,0:T(8,128)(2,1)} %all-gather.4.cloned.1.call-done), kind=kOutput, calls=%fused_computation.31 | convolution fusion | flops 1074790272 | bytes 10486784 | tf_op jit(solution)/shard_map/dot_general | solution.py:70
  177.2 0.8 copy.21
  178.0 0.8 copy.22
  (26 shorter events, 0.5 us)
Async XLA Ops:
  7.2 82.9 %all-gather.6.cloned.1.call-start = ((), (), s32[]{:S(2)}) async-start(), calls=%async_computation.2 | async-start | bytes 8912896 | tf_op jit(solution)/shard_map/all_gather | solution.py:41
  8.6 162.5 %all-gather.4.cloned.1.call-start = ((), (), s32[]{:S(2)}) async-start(), calls=%async_computation.1 | async-start | bytes 8912896 | tf_op jit(solution)/shard_map/all_gather | solution.py:55
  8.7 43.7 %collective-permute-start.3 = (bf16[128,2048]{1,0:T(8,128)(2,1)}, bf16[128,2048]{1,0:T(8,128)(2,1)S(1)}, u32[]{:S(2)}, u32[]{:S(2)}) collective-permute-start(bf16[128,2048]{1,0:T(8,128)(2,1)} %bitcast.55), channel_id=1, source_target_pairs={{0,240},{16,224},{32,208},{48,192},{64,176},{80,160},{96,144},{112... | collective-permute-start | bytes 1572872 | tf_op jit(solution)/shard_map/ppermute | solution.py:11
  52.5 42.5 %copy-start = (bf16[1,3,128,2048]{3,2,1,0:T(8,128)(2,1)}, bf16[1,3,128,2048]{3,2,1,0:T(8,128)(2,1)S(1)}, u32[]{:S(2)}) copy-start(bf16[1,3,128,2048]{3,2,1,0:T(8,128)(2,1)S(1)} %get-tuple-element.20) | copy-start | bytes 4718596
  52.5 16.2 %collective-permute-start.1 = (bf16[128,2048]{1,0:T(8,128)(2,1)S(1)}, bf16[128,2048]{1,0:T(8,128)(2,1)S(1)}, u32[]{:S(2)}, u32[]{:S(2)}) collective-permute-start(bf16[128,2048]{1,0:T(8,128)(2,1)S(1)} %get-tuple-element.6), channel_id=1, source_target_pairs={{0,240},{16,224},{32,208},{48,192},{64,176},{80,160},{96,144},{112... | collective-permute-start | bytes 1572872 | tf_op jit(solution)/shard_map/ppermute | solution.py:11
  68.9 26.1 %copy-start.2 = (bf16[1,128,2048]{2,1,0:T(8,128)(2,1)S(1)}, bf16[1,128,2048]{2,1,0:T(8,128)(2,1)}, u32[]{:S(2)}) copy-start(bf16[1,128,2048]{2,1,0:T(8,128)(2,1)} %param.10) | copy-start | bytes 1572868
  68.9 26.1 %copy-start.4 = (f32[1,2048]{1,0:T(1,128)S(1)}, f32[1,2048]{1,0:T(1,128)}, u32[]{:S(2)}) copy-start(f32[1,2048]{1,0:T(1,128)} %param.8) | copy-start | bytes 24580
  90.1 4.9 %slice-start = ((s8[8388608]{0:T(1024)(128)(4,1)}), s8[4194304]{0:T(1024)(128)(4,1)S(1)}, s32[]{:S(2)}) async-start(s8[8388608]{0:T(1024)(128)(4,1)} %bitcast.52), calls=%async_computation.3 | async-start | bytes 8388608
  90.1 5.9 %slice-start.1 = ((s8[8388608]{0:T(1024)(128)(4,1)}), s8[4194304]{0:T(1024)(128)(4,1)S(1)}, s32[]{:S(2)}) async-start(s8[8388608]{0:T(1024)(128)(4,1)} %bitcast.52), calls=%async_computation.4 | async-start | bytes 8388608
  96.0 4.8 %copy-start.3 = (bf16[1,128,2048]{2,1,0:T(8,128)(2,1)S(1)}, bf16[1,128,2048]{2,1,0:T(8,128)(2,1)}, u32[]{:S(2)}) copy-start(bf16[1,128,2048]{2,1,0:T(8,128)(2,1)} %param.9) | copy-start | bytes 1572868
  101.0 70.1 %copy-start.1 = (bf16[1,128,2048]{2,1,0:T(8,128)(2,1)S(1)}, bf16[1,128,2048]{2,1,0:T(8,128)(2,1)}, u32[]{:S(2)}) copy-start(bf16[1,128,2048]{2,1,0:T(8,128)(2,1)} %param.7) | copy-start | bytes 1572868
  106.7 17.1 %collective-permute-start = (bf16[128,2048]{1,0:T(8,128)(2,1)}, bf16[128,2048]{1,0:T(8,128)(2,1)S(1)}, u32[]{:S(2)}, u32[]{:S(2)}) collective-permute-start(bf16[128,2048]{1,0:T(8,128)(2,1)} %fusion.24), channel_id=1, source_target_pairs={{240,0},{0,16},{16,32},{32,48},{48,64},{64,80},{80,96},{96,112},{1... | collective-permute-start | bytes 1572872 | tf_op jit(solution)/shard_map/ppermute | solution.py:17
  106.7 17.1 %collective-permute-start.2 = (bf16[128,2048]{1,0:T(8,128)(2,1)S(1)}, bf16[128,2048]{1,0:T(8,128)(2,1)S(1)}, u32[]{:S(2)}, u32[]{:S(2)}) collective-permute-start(bf16[128,2048]{1,0:T(8,128)(2,1)S(1)} %get-tuple-element.12), channel_id=1, source_target_pairs={{16,0},{32,16},{48,32},{64,48},{80,64},{96,80},{112,96},{128,112},... | collective-permute-start | bytes 1572872 | tf_op jit(solution)/shard_map/ppermute | solution.py:17
  112.7 25.1 %all-to-all-start = ((bf16[128,16,128]{2,0,1:T(8,128)(2,1)}), bf16[128,16,128]{2,0,1:T(8,128)(2,1)S(1)}, u32[]{:S(2)}, u32[]{:S(2)}) async-start(bf16[128,16,128]{2,0,1:T(8,128)(2,1)} %bitcast.51), calls=%async_computation | async-start | bytes 1048576 | tf_op jit(solution)/shard_map/all_to_all | solution.py:48
Sparse Core Ops, SparseCore 0:
  9.9 80.2 all-gather.5
  100.9 70.1 all-gather.3

commit v2 on v1

v2 whole, which is shorter than its diff:
```python
import functools

import jax
import jax.numpy as jnp
from jax import lax
from jax.experimental import pallas as pl
from jax.experimental.pallas import tpu as pltpu
from jax.sharding import PartitionSpec as P

EPSILON = 1e-05
RING, PAIR, CORES = 4, 2, 2
CHIPS = RING * PAIR
MEMBERS = CHIPS * CORES
BLOCK = 128
TILE = 256

VMEM = pl.BlockSpec(memory_space=pltpu.VMEM)
SMEM = pl.BlockSpec(memory_space=pltpu.SMEM)
ANY = pl.BlockSpec(memory_space=pl.ANY)
F32, BF16 = jnp.float32, jnp.bfloat16


def struct(shape, dtype):
    return jax.ShapeDtypeStruct(shape, dtype)


def call(kernel, outs, args, specs, out_specs=None, scratch=(), flops=0, megabytes=32):
    nbytes = sum(a.size * a.dtype.itemsize for a in list(args) + list(outs))
    return pl.pallas_call(
        kernel,
        out_shape=list(outs),
        in_specs=list(specs),
        out_specs=list(out_specs) if out_specs else [VMEM] * len(outs),
        scratch_shapes=list(scratch),
        cost_estimate=pl.CostEstimate(flops=flops, bytes_accessed=nbytes, transcendentals=0),
        compiler_params=pltpu.CompilerParams(vmem_limit_bytes=megabytes * 1024 * 1024),
    )(*args)


def mirrored(block):
    count = lax.axis_size("section")
    return lax.ppermute(block, "section", [(i, count - 1 - i) for i in range(count)])


def shifted(block, distance):
    count = lax.axis_size("section")
    return lax.ppermute(block, "section", [((i - distance) % count, i) for i in range(count)])


def hop(block, ring=0, pair=0, core=0):
    route = []
    for i in range(MEMBERS):
        y, x, c = i // (PAIR * CORES), i // CORES % PAIR, i % CORES
        route.append((i, (((y + ring) % RING) * PAIR + (x ^ pair)) * CORES + (c ^ core)))
    return lax.ppermute(block, "dp", route)


def gathered(own):
    rows = own.shape[0] // 2
    pair = hop(own, pair=1)
    below = hop(own, ring=1)
    above = hop(own, ring=-1)
    far_low = hop(below[:rows], ring=1)
    far_high = hop(above[rows:], ring=-1)
    pair_below = hop(pair, ring=1)
    pair_above = hop(pair, ring=-1)
    pair_far_low = hop(far_low, pair=1)
    pair_far_high = hop(far_high, pair=1)
    early = [(0, 0, [own]), (0, 1, [pair]), (-1, 0, [below]), (1, 0, [above])]
    late = [
        (2, 0, [far_low, far_high]),
        (-1, 1, [pair_below]),
        (1, 1, [pair_above]),
        (2, 1, [pair_far_low, pair_far_high]),
    ]
    return early, late


def place():
    member = lax.axis_index("dp")
    core = lax.rem(member, CORES)
    return member, core


def chip_of(up, other):
    member = lax.axis_index("dp")
    ring_at = lax.div(member, PAIR * CORES)
    pair_at = lax.rem(lax.div(member, CORES), PAIR)
    pair_to = 1 - pair_at if other else pair_at
    return lax.rem(ring_at + up + RING, RING) * PAIR + pair_to


def columns_of(step):
    return pl.ds(pl.multiple_of(step * TILE, TILE), TILE)


def inverse_rms(values):
    return lax.rsqrt(jnp.mean(values * values, -1, keepdims=True) + EPSILON)


def fetch_kernel(slots, held, out, sem):
    partner = lax.axis_size("section") - 1 - lax.axis_index("section")
    copy = pltpu.make_async_copy(held.at[0, slots[partner]], out, sem)
    copy.start()
    copy.wait()


def normed_kernel(rows, gain, mine, send, *units):
    _, core = place()
    values = rows[...].astype(F32)
    unit = values * inverse_rms(values)
    normed = (unit * gain[...]).astype(BF16)
    for chip in range(CHIPS):
        at = chip * CORES * BLOCK
        first, second = normed[:, at : at + BLOCK], normed[:, at + BLOCK : at + 2 * BLOCK]
        mine[chip] = jnp.where(core == 0, first, second)
        send[chip] = jnp.where(core == 0, second, first)
        if units:
            first = jnp.transpose(unit[:, at : at + BLOCK]).astype(BF16)
            second = jnp.transpose(unit[:, at + BLOCK : at + 2 * BLOCK]).astype(BF16)
            units[0][chip, 0] = jnp.where(core == 0, first, second)
            units[0][chip, 1] = jnp.where(core == 0, second, first)


def product_kernel(layout, stacked, added, *refs):
    refs = list(refs)
    left = refs.pop()
    out_own, out_other = refs[-2:]
    del refs[-2:]
    if stacked:
        both = refs.pop(0)
        own, other = (lambda chip: both[chip, 0]), (lambda chip: both[chip, 1])
    else:
        own_ref, other_ref = refs.pop(0), refs.pop(0)
        own, other = (lambda chip: own_ref[chip]), (lambda chip: other_ref[chip])
    totals = [refs.pop(), refs.pop()][::-1] if added else None
    for k, (up, to_other, _) in enumerate(layout):
        chip = chip_of(up, to_other)
        left[:BLOCK, k * BLOCK : (k + 1) * BLOCK] = own(chip)
        left[BLOCK:, k * BLOCK : (k + 1) * BLOCK] = other(chip)

    @pl.loop(0, out_own.shape[1] // TILE)
    def _(step):
        columns = columns_of(step)
        right = jnp.concatenate([part[:, columns] for part in refs], 0)
        result = jnp.dot(left[...], right, preferred_element_type=F32)
        low, high = result[:BLOCK], result[BLOCK:]
        if added:
            low, high = low + totals[0][:, columns], high + totals[1][:, columns]
        out_own[:, columns] = low
        out_other[:, columns] = high


def product(blocks, chunks, totals=()):
    parts = [part for chunk in chunks for part in chunk[2]]
    layout = [(up, other, len(p)) for up, other, p in chunks]
    depth, width = len(chunks) * BLOCK, parts[0].shape[1]
    args = [*blocks, *parts, *totals]
    out = struct((BLOCK, width), F32)
    return call(
        functools.partial(product_kernel, layout, len(blocks) == 1, bool(totals)),
        [out, out],
        args,
        [VMEM] * len(args),
        scratch=[pltpu.VMEM((2 * BLOCK, depth), BF16)],
        flops=2 * 2 * BLOCK * depth * width,
    )


def delta_kernel(own, received, grads, delta):
    @pl.loop(0, delta.shape[1] // TILE)
    def _(step):
        columns = columns_of(step)
        pre_act = own[:, columns] + received[:, columns]
        sigma = jax.nn.sigmoid(pre_act)
        grad_f = grads[:, columns].astype(F32)
        delta[:, columns] = (grad_f * sigma * (1.0 + pre_act * (1.0 - sigma))).astype(BF16)


def out_kernel(own, received, acts, out):
    @pl.loop(0, out.shape[1] // TILE)
    def _(step):
        columns = columns_of(step)
        pre_act = own[:, columns] + received[:, columns]
        values = acts[:, columns].astype(F32)
        out[:, columns] = (values + pre_act * jax.nn.sigmoid(pre_act)).astype(BF16)


def back_kernel(layout, delta_own, delta_other, *refs):
    refs = list(refs)
    left = refs.pop()
    back_own, back_other = refs[-2:]
    left[:BLOCK] = delta_own[...]
    left[BLOCK:] = delta_other[...]
    at = 0
    for k in range(0, len(layout), 2):
        parts = []
        for _, _, count in layout[k : k + 2]:
            parts += [refs[at + i][...] for i in range(count)]
            at += count
        right = jnp.concatenate(parts, 0)
        result = lax.dot_general(
            left[...], right, (((1,), (1,)), ((), ())), preferred_element_type=F32
        )
        for i, (up, other, _) in enumerate(layout[k : k + 2]):
            chip = chip_of(up, other)
            back_own[chip] = result[:BLOCK, i * BLOCK : (i + 1) * BLOCK]
            back_other[chip] = result[BLOCK:, i * BLOCK : (i + 1) * BLOCK]


def grad_kernel(panel, gain, grads, back_own, back_received, grad_acts, through):
    _, core = place()
    values = panel[...].astype(F32)
    inverse = inverse_rms(values)
    for chip in range(CHIPS):
        at = chip * CORES * BLOCK
        own, received = back_own[chip], back_received[chip]
        through[:, at : at + BLOCK] = jnp.where(core == 0, own, received)
        through[:, at + BLOCK : at + 2 * BLOCK] = jnp.where(core == 0, received, own)
    unit = values * inverse
    scaled = through[...] * gain[...]
    mean = jnp.mean(scaled * unit, -1, keepdims=True)
    grad_acts[...] = (grads[...].astype(F32) + inverse * (scaled - unit * mean)).astype(BF16)


def park_kernel(slots, held, stashed, out, sems):
    partner = lax.axis_size("section") - 1 - lax.axis_index("section")
    slot = slots[partner]
    for k in range(held.shape[1]):

        @pl.when(slot == k)
        def _(k=k):
            pltpu.make_async_copy(stashed, out.at[0, k], sems.at[k]).start()

        @pl.when(slot != k)
        def _(k=k):
            pltpu.make_async_copy(held.at[0, k], out.at[0, k], sems.at[k]).start()

    for k in range(held.shape[1]):
        pltpu.make_async_copy(stashed, out.at[0, k], sems.at[k]).wait()


def finish_kernel(
    own, received, weight, gain, acts, grads, weight_grad, gain_grad, next_acts, next_grads, sems
):
    member, _ = place()
    copies = [
        pltpu.make_async_copy(acts, next_acts.at[0], sems.at[0]),
        pltpu.make_async_copy(grads, next_grads.at[0], sems.at[1]),
    ]
    for copy in copies:
        copy.start()
    own_gain = gain[:, pl.ds(pl.multiple_of(member * BLOCK, BLOCK), BLOCK)]
    scale = jnp.transpose(jnp.broadcast_to(own_gain, (BLOCK, BLOCK)))[:, :1]
    total = jnp.zeros((BLOCK, 1), F32)
    for at in range(0, own.shape[1], TILE):
        outer = own[:, at : at + TILE] + received[:, at : at + TILE]
        weight_grad[0, :, at : at + TILE] = outer * scale
        total += jnp.sum(outer * weight[0, :, at : at + TILE].astype(F32), -1, keepdims=True)
    gain_grad[...] = jnp.transpose(jnp.broadcast_to(total, (BLOCK, BLOCK)))[:1]
    for copy in copies:
        copy.wait()


def shards(weight, gain, acts_in, grads_in, parked, fetch_slot, park_slot):
    tokens, width = acts_in.shape[1:]
    acts, grads = acts_in[0], grads_in[0]
    rows, blocks = struct((tokens, width), BF16), struct((CHIPS, BLOCK, BLOCK), BF16)
    sent_rows = struct((tokens, width), BF16)
    back = struct((CHIPS, BLOCK, BLOCK), F32)

    (fetched,) = call(
        fetch_kernel, [sent_rows], [fetch_slot, parked], [SMEM, ANY], [ANY], [pltpu.SemaphoreType.DMA]
    )
    panel = mirrored(fetched)
    early, late = gathered(weight[0])
    stashed = mirrored(acts)

    mine, send = call(normed_kernel, [blocks, blocks], [acts, gain], [VMEM] * 2)
    forward = [mine, hop(send, core=1)]
    pre = product(forward, early)
    pre_own, pre_other = product(forward, late, pre)

    mine, send, units = call(
        normed_kernel,
        [blocks, blocks, struct((CHIPS, CORES, BLOCK, BLOCK), BF16)],
        [panel, gain],
        [VMEM] * 2,
    )
    backward = [mine, hop(send, core=1)]
    panel_pre = product(backward, early)
    panel_own, panel_other = product(backward, late, panel_pre)
    units = lax.all_to_all(
        units,
        "dp",
        split_axis=0,
        concat_axis=0,
        tiled=True,
        axis_index_groups=[[chip * CORES + c for chip in range(CHIPS)] for c in range(CORES)],
    )

    (delta,) = call(
        delta_kernel, [rows], [panel_own, hop(panel_other, core=1), grads], [VMEM] * 3
    )
    delta_early, delta_late = gathered(delta)

    (out_rows,) = call(
        out_kernel, [rows], [pre_own, hop(pre_other, core=1), acts], [VMEM] * 3
    )
    next_acts = shifted(out_rows, 1)

    chunks = early + late
    parts = [part for chunk in chunks for part in chunk[2]]
    back_own, back_other = call(
        functools.partial(back_kernel, [(up, other, len(p)) for up, other, p in chunks]),
        [back, back],
        [delta, hop(delta, core=1), *parts],
        [VMEM] * (2 + len(parts)),
        scratch=[pltpu.VMEM((2 * BLOCK, width), BF16)],
        flops=2 * 2 * BLOCK * CHIPS * BLOCK * width,
    )
    (grad_acts,) = call(
        grad_kernel,
        [rows],
        [panel, gain, grads, back_own, hop(back_other, core=1)],
        [VMEM] * 5,
        scratch=[pltpu.VMEM((tokens, width), F32)],
    )
    next_grads = shifted(grad_acts, -1)
    (parked_out,) = call(
        park_kernel,
        [struct(parked.shape, BF16)],
        [park_slot, parked, stashed],
        [SMEM, ANY, ANY],
        [ANY],
        [pltpu.SemaphoreType.DMA((parked.shape[1],))],
    )

    outer = product([units], delta_early)
    outer_own, outer_other = product([units], delta_late, outer)
    weight_grad, gain_grad, next_acts, next_grads = call(
        finish_kernel,
        [
            struct((1, BLOCK, width), F32),
            struct((1, BLOCK), F32),
            struct((1, tokens, width), BF16),
            struct((1, tokens, width), BF16),
        ],
        [outer_own, hop(outer_other, core=1), weight, gain, next_acts, next_grads],
        [VMEM] * 4 + [ANY] * 2,
        [VMEM, VMEM, ANY, ANY],
        [pltpu.SemaphoreType.DMA((2,))],
    )
    return next_acts, next_grads, parked_out, weight_grad, gain_grad


def solution(mesh):
    return jax.shard_map(
        shards,
        mesh=mesh,
        in_specs=(
            P("section", "dp", None),
            P("section", None),
            P("section", "dp", None),
            P("section", "dp", None),
            P("section", None, "dp", None),
            P(),
            P(),
        ),
        out_specs=(
            P("section", "dp", None),
            P("section", "dp", None),
            P("section", None, "dp", None),
            P("section", "dp", None),
            P("section", "dp"),
        ),
        check_vma=False,
    )
```

time: 186 us -> 152 us (0.82)
  waiting for transfers between devices: 115 us -> 58 us
  starting transfers between devices: 23.5 us -> 54.4 us
  Pallas kernels: 0 us -> 30.1 us
  matrix products: 19.6 us -> 0 us
  between operations: 18 us -> 1.14 us
  other arithmetic: 2.24 us -> 0 us
    all_gather x2 -> x0, waiting for transfers between devices: 54.5 us -> none  [the longest x1 33.3 us: shards(): all_delta = lax.all_gather(delta, 'dp', axis=0, tiled=True)]
    ppermute x4 -> x29, starting transfers between devices: 18.5 us -> 50.3 us  [the longest x25 32.1 us: hop(): return lax.ppermute(block, 'dp', route)]
    pallas_call x0 -> x15, Pallas kernels: none -> 30.1 us  [call(): pl.pallas_call(kernel, out_shape=list(outs), in_specs=list(specs), out_sp...]
    dot_general x4 -> x0, matrix products: 19.6 us -> none  [the longest x1 6.14 us: shards(): lax.dot_general(own_units, all_delta, (((0,), (0,)), ((), ())), preferred...]
    all_to_all x1, waiting for transfers between devices: 14 us -> 0.01 us  [shards(): lax.all_to_all(units, 'dp', split_axis=0, concat_axis=0, tiled=True, axis...]
    ppermute x4 -> x29, waiting for transfers between devices: 46.2 us -> 58 us  [the longest x2 30.4 us: mirrored(): lax.ppermute(block, 'section', [(i, count - 1 - i) for i in range(count)])]
    dynamic_slice x2 -> x0, local copies, waits for them, and re-layouts: 2.48 us -> none  [the longest x1 1.24 us: shards(): send_slot = lax.dynamic_index_in_dim(fetch_slot, partner, 0, keepdims=False)]
    slice x0 -> x4, local copies, waits for them, and re-layouts: none -> 1.97 us  [the longest x2 0.99 us: gathered(): far_high = hop(above[rows:], ring=-1)]
  transfers between devices with their start and end apart: 7 -> 30, of which waited for: 6 -> 10; matrix products, arithmetic and copies ran while one was open for 5% -> 1% of each run, Pallas kernels for 0% -> 16%
where the time goes in v2:
time: 152 us; the launch traced here: 151 us
  waiting for transfers between devices  58 us (38%)
  starting transfers between devices  54.4 us (36%)
  Pallas kernels  30.1 us (20%)
  local copies, waits for them, and re-layouts  7.52 us (5%)
    ppermute x25, starting transfers between devices, hop(): return lax.ppermute(block, 'dp', route)  32.1 us
    ppermute x2, waiting for transfers between devices, mirrored(): lax.ppermute(block, 'section', [(i, count - 1 - i) for i in range(count)])  30.4 us
    pallas_call x15, Pallas kernels, call(): pl.pallas_call(kernel, out_shape=list(outs), in_specs=list(specs), out_sp...  30.1 us
    ppermute x25, waiting for transfers between devices, hop(): return lax.ppermute(block, 'dp', route)  18.1 us
    ppermute x2, starting transfers between devices, mirrored(): lax.ppermute(block, 'section', [(i, count - 1 - i) for i in range(count)])  12.9 us
    ppermute x2, waiting for transfers between devices, shifted(): lax.ppermute(block, 'section', [((i - distance) % count, i) for i in rang...  9.5 us
    unnamed x52, local copies, waits for them, and re-layouts  5.55 us
    ppermute x2, starting transfers between devices, shifted(): lax.ppermute(block, 'section', [((i - distance) % count, i) for i in rang...  5.21 us
  transfers between devices with their start and end apart: 30, of which 10 were waited for; matrix products, arithmetic and copies ran while one was open for 1% of the time, Pallas kernels for 16%

profile of v2, /device:TPU:1, one launch (start us, length us, event | category | flops | bytes accessed | tf_op | source)
XLA Modules:
  0.0 151.2 jit_solution(12742875026870859335)
XLA Ops:
  0.6 3.6 %collective-permute-start.4 = (bf16[128,2048]{1,0:T(8,128)(2,1)}, bf16[128,2048]{1,0:T(8,128)(2,1)S(1)}, u32[]{:S(2)}, u32[]{:S(2)}) collective-permute-start(bf16[128,2048]{1,0:T(8,128)(2,1)} %bitcast.3), channel_id=1, source_target_pairs={{0,12},{1,13},{2,14},{3,15},{4,0},{5,1},{6,2},{7,3},{8,4},{9,5},{1... | collective-permute-start | bytes 1572872 | tf_op jit(solution)/shard_map/ppermute | solution.py:55
  8.2 7.8 %collective-permute-start = (bf16[128,2048]{1,0:T(8,128)(2,1)S(1)}, bf16[128,2048]{1,0:T(8,128)(2,1)S(1)}, u32[]{:S(2)}, u32[]{:S(2)}) collective-permute-start(bf16[128,2048]{1,0:T(8,128)(2,1)S(1)} %shard_map.110), channel_id=1, source_target_pairs={{0,240},{16,224},{32,208},{48,192},{64,176},{80,160},{96,144},{112... | collective-permute-start | bytes 1572872 | tf_op jit(solution)/shard_map/ppermute | solution.py:42
  16.0 2.8 %collective-permute-start.5 = (bf16[64,2048]{1,0:T(8,128)(2,1)S(1)}, bf16[64,2048]{1,0:T(8,128)(2,1)S(1)}, u32[]{:S(2)}, u32[]{:S(2)}) collective-permute-start(bf16[64,2048]{1,0:T(8,128)(2,1)S(1)} %slice.17), channel_id=1, source_target_pairs={{0,12},{1,13},{2,14},{3,15},{4,0},{5,1},{6,2},{7,3},{8,4},{9,5},{1... | collective-permute-start | bytes 786440 | tf_op jit(solution)/shard_map/ppermute | solution.py:55
  19.0 2.7 %collective-permute-start.8 = (bf16[128,2048]{1,0:T(8,128)(2,1)S(1)}, bf16[128,2048]{1,0:T(8,128)(2,1)S(1)}, u32[]{:S(2)}, u32[]{:S(2)}) collective-permute-start(bf16[128,2048]{1,0:T(8,128)(2,1)S(1)} %collective-permute-done.6.refs_3_.refs_1_), channel_id=1, source_target_pairs={{0,12},{1,13},{2,14},{3,15},{4,0},{5,1},{6,2},{7,3},{8,4},{9,5},{1... | collective-permute-start | bytes 1572872 | tf_op jit(solution)/shard_map/ppermute | solution.py:55
  21.7 17.5 %collective-permute-done.rows.panel = bf16[128,2048]{1,0:T(8,128)(2,1)S(1)} collective-permute-done((bf16[128,2048]{1,0:T(8,128)(2,1)S(1)}, bf16[128,2048]{1,0:T(8,128)(2,1)S(1)}, u32[]{:S(2)}, u32[]{:S(2)}) %collective-permute-start) | collective-permute-done | bytes 524320 | tf_op jit(solution)/shard_map/ppermute | solution.py:42
  44.8 4.5 %collective-permute-done.10.refs_7_.refs_9_ = bf16[64,2048]{1,0:T(8,128)(2,1)S(1)} collective-permute-done((bf16[64,2048]{1,0:T(8,128)(2,1)S(1)}, bf16[64,2048]{1,0:T(8,128)(2,1)S(1)}, u32[]{:S(2)}, u32[]{:S(2)}) %collective-permute-start.10) | collective-permute-done | bytes 262176 | tf_op jit(solution)/shard_map/ppermute | solution.py:55
  49.3 5.6 %collective-permute-done.9.refs_6_.refs_8_ = bf16[64,2048]{1,0:T(8,128)(2,1)S(1)} collective-permute-done((bf16[64,2048]{1,0:T(8,128)(2,1)S(1)}, bf16[64,2048]{1,0:T(8,128)(2,1)S(1)}, u32[]{:S(2)}, u32[]{:S(2)}) %collective-permute-start.9) | collective-permute-done | bytes 262176 | tf_op jit(solution)/shard_map/ppermute | solution.py:55
  57.8 2.3 %collective-permute-done.11.received = f32[128,2048]{1,0:T(8,128)S(1)} collective-permute-done((f32[128,2048]{1,0:T(8,128)S(1)}, f32[128,2048]{1,0:T(8,128)S(1)}, u32[]{:S(2)}, u32[]{:S(2)}) %collective-permute-start.11) | collective-permute-done | bytes 1048608 | tf_op jit(solution)/shard_map/ppermute | solution.py:55
  61.3 2.7 %collective-permute-start.14 = (bf16[128,2048]{1,0:T(8,128)(2,1)}, bf16[128,2048]{1,0:T(8,128)(2,1)}, u32[]{:S(2)}, u32[]{:S(2)}) collective-permute-start(bf16[128,2048]{1,0:T(8,128)(2,1)} %shard_map.114.refs_1_.delta_own), channel_id=1, source_target_pairs={{0,12},{1,13},{2,14},{3,15},{4,0},{5,1},{6,2},{7,3},{8,4},{9,5},{1... | collective-permute-start | bytes 1572872 | tf_op jit(solution)/shard_map/ppermute | solution.py:55
  66.9 4.1 %all-to-all-start = ((bf16[8,2,128,128]{3,2,1,0:T(8,128)(2,1)}), bf16[8,2,128,128]{3,2,1,0:T(8,128)(2,1)}, u32[]{:S(2)}, u32[]{:S(2)}) async-start(bf16[8,2,128,128]{3,2,1,0:T(8,128)(2,1)} %copy-done.22), calls=%async_computation | async-start | bytes 1048576 | tf_op jit(solution)/shard_map/all_to_all | solution.py:293
  72.1 3.0 %shard_map.118 = (f32[128,2048]{1,0:T(8,128)S(1)}, f32[128,2048]{1,0:T(8,128)S(1)}) custom-call(bf16[8,128,128]{2,1,0:T(8,128)(2,1)S(1)} %copy-done.21, bf16[8,128,128]{2,1,0:T(8,128)(2,1)} %collective-permute-done.22.refs_1_, bf16[128,2048]{1,0:T(8,128)(2,1)S(1)} %bitcast.7, bf16[128,2048]{1,0:T(8,128)(2,1)S(1)} %collective-permute-done.6.refs_3_.refs_1_, ...), custom_call_target="tpu_custom_call" | custom-call | flops 536870912 | bytes 4718592 | tf_op jit(solution)/shard_map/pallas_call | solution.py:29
  78.4 2.4 %collective-permute-start.15 = (bf16[64,2048]{1,0:T(8,128)(2,1)S(1)}, bf16[64,2048]{1,0:T(8,128)(2,1)}, u32[]{:S(2)}, u32[]{:S(2)}) collective-permute-start(bf16[64,2048]{1,0:T(8,128)(2,1)S(1)} %slice.19), channel_id=1, source_target_pairs={{0,12},{1,13},{2,14},{3,15},{4,0},{5,1},{6,2},{7,3},{8,4},{9,5},{1... | collective-permute-start | bytes 786440 | tf_op jit(solution)/shard_map/ppermute | solution.py:55
  80.8 2.7 %collective-permute-start.18 = (bf16[128,2048]{1,0:T(8,128)(2,1)}, bf16[128,2048]{1,0:T(8,128)(2,1)}, u32[]{:S(2)}, u32[]{:S(2)}) collective-permute-start(bf16[128,2048]{1,0:T(8,128)(2,1)} %collective-permute-done.16.refs_2_), channel_id=1, source_target_pairs={{0,12},{1,13},{2,14},{3,15},{4,0},{5,1},{6,2},{7,3},{8,4},{9,5},{1... | collective-permute-start | bytes 1572872 | tf_op jit(solution)/shard_map/ppermute | solution.py:55
  83.5 3.9 %shard_map.119 = (f32[128,2048]{1,0:T(8,128)S(1)}, f32[128,2048]{1,0:T(8,128)}) custom-call(bf16[8,128,128]{2,1,0:T(8,128)(2,1)S(1)} %copy-done.21, bf16[8,128,128]{2,1,0:T(8,128)(2,1)} %collective-permute-done.22.refs_1_, bf16[64,2048]{1,0:T(8,128)(2,1)S(1)} %copy-done.4, bf16[64,2048]{1,0:T(8,128)(2,1)S(1)} %collective-permute-done.5.refs_3_.refs_5_, ...), custom_call_target="tpu_custom_call" | custom-call | flops 536870912 | bytes 6815744 | tf_op jit(solution)/shard_map/pallas_call | solution.py:29
  88.3 5.2 %collective-permute-start.23 = (f32[128,2048]{1,0:T(8,128)}, f32[128,2048]{1,0:T(8,128)}, u32[]{:S(2)}, u32[]{:S(2)}) collective-permute-start(f32[128,2048]{1,0:T(8,128)} %get-tuple-element.44), channel_id=1, source_target_pairs={{0,1},{1,0},{2,3},{3,2},{4,5},{5,4},{6,7},{7,6},{8,9},{9,8},{10,11... | collective-permute-start | bytes 3145736 | tf_op jit(solution)/shard_map/ppermute | solution.py:55
  95.0 3.7 %shard_map.115 = (f32[128,2048]{1,0:T(8,128)S(1)}, f32[128,2048]{1,0:T(8,128)S(1)}) custom-call(bf16[8,2,128,128]{3,2,1,0:T(8,128)(2,1)} %all-to-all-done.refs_0_, bf16[128,2048]{1,0:T(8,128)(2,1)} %shard_map.114.refs_1_.delta_own, bf16[128,2048]{1,0:T(8,128)(2,1)} %collective-permute-done.16.refs_2_, bf16[128,2048]{1,0:T(8,128)(2,1)} %collective-permute-done.12.refs_3_, ...), custom_call_target="tpu_custom_call" | custom-call | flops 536870912 | bytes 4718592 | tf_op jit(solution)/shard_map/pallas_call | solution.py:29
  98.8 2.5 %shard_map.121 = (f32[8,128,128]{2,1,0:T(8,128)S(1)}, f32[8,128,128]{2,1,0:T(8,128)S(1)}) custom-call(bf16[128,2048]{1,0:T(8,128)(2,1)} %shard_map.114.refs_1_.delta_own, bf16[128,2048]{1,0:T(8,128)(2,1)} %collective-permute-done.25.delta_other, bf16[128,2048]{1,0:T(8,128)(2,1)S(1)} %bitcast.8, bf16[128,2048]{1,0:T(8,128)(2,1)S(1)} %collective-permute-done.6.refs_3_.refs_1_, ...), custom_call_target="tpu_custom_call" | custom-call | flops 1073741824 | bytes 6291456 | tf_op jit(solution)/shard_map/pallas_call | solution.py:29
  103.0 4.3 %collective-permute-done.20.refs_6_ = bf16[64,2048]{1,0:T(8,128)(2,1)} collective-permute-done((bf16[64,2048]{1,0:T(8,128)(2,1)}, bf16[64,2048]{1,0:T(8,128)(2,1)}, u32[]{:S(2)}, u32[]{:S(2)}) %collective-permute-start.20) | collective-permute-done | bytes 262176 | tf_op jit(solution)/shard_map/ppermute | solution.py:55
  107.3 3.7 %shard_map.116 = (f32[128,2048]{1,0:T(8,128)S(1)}, f32[128,2048]{1,0:T(8,128)S(1)}) custom-call(bf16[8,2,128,128]{3,2,1,0:T(8,128)(2,1)} %all-to-all-done.refs_0_, bf16[64,2048]{1,0:T(8,128)(2,1)} %collective-permute-done.13.refs_1_, bf16[64,2048]{1,0:T(8,128)(2,1)} %collective-permute-done.15.refs_2_, bf16[128,2048]{1,0:T(8,128)(2,1)} %collective-permute-done.17.refs_3_, ...), custom_call_target="tpu_custom_call" | custom-call | flops 536870912 | bytes 6815744 | tf_op jit(solution)/shard_map/pallas_call | solution.py:29
  112.0 5.1 %collective-permute-start.28 = (bf16[128,2048]{1,0:T(8,128)(2,1)S(1)}, bf16[128,2048]{1,0:T(8,128)(2,1)S(1)}, u32[]{:S(2)}, u32[]{:S(2)}) collective-permute-start(bf16[128,2048]{1,0:T(8,128)(2,1)S(1)} %bitcast.12), channel_id=1, source_target_pairs={{0,240},{16,224},{32,208},{48,192},{64,176},{80,160},{96,144},{112... | collective-permute-start | bytes 1572872 | tf_op jit(solution)/shard_map/ppermute | solution.py:42
  119.6 5.1 %collective-permute-start.27 = (bf16[128,2048]{1,0:T(8,128)(2,1)S(1)}, bf16[128,2048]{1,0:T(8,128)(2,1)S(1)}, u32[]{:S(2)}, u32[]{:S(2)}) collective-permute-start(bf16[128,2048]{1,0:T(8,128)(2,1)S(1)} %shard_map.122), channel_id=1, source_target_pairs={{16,0},{32,16},{48,32},{64,48},{80,64},{96,80},{112,96},{128,112},... | collective-permute-start | bytes 1572872 | tf_op jit(solution)/shard_map/ppermute | solution.py:47
  124.8 13.0 %collective-permute-done.28.stashed = bf16[128,2048]{1,0:T(8,128)(2,1)S(1)} collective-permute-done((bf16[128,2048]{1,0:T(8,128)(2,1)S(1)}, bf16[128,2048]{1,0:T(8,128)(2,1)S(1)}, u32[]{:S(2)}, u32[]{:S(2)}) %collective-permute-start.28) | collective-permute-done | bytes 524320 | tf_op jit(solution)/shard_map/ppermute | solution.py:42
  139.5 9.3 %collective-permute-done.24.acts = bf16[128,2048]{1,0:T(8,128)(2,1)S(1)} collective-permute-done((bf16[128,2048]{1,0:T(8,128)(2,1)S(1)}, bf16[128,2048]{1,0:T(8,128)(2,1)S(1)}, u32[]{:S(2)}, u32[]{:S(2)}) %collective-permute-start.24) | collective-permute-done | bytes 524320 | tf_op jit(solution)/shard_map/ppermute | solution.py:47
  149.0 2.0 %shard_map.123 = (f32[1,128,2048]{2,1,0:T(8,128)}, f32[1,128]{1,0:T(1,128)}, bf16[1,128,2048]{2,1,0:T(8,128)(2,1)}, bf16[1,128,2048]{2,1,0:T(8,128)(2,1)}) custom-call(f32[128,2048]{1,0:T(8,128)S(1)} %get-tuple-element.37.own, f32[128,2048]{1,0:T(8,128)S(1)} %collective-permute-done.21.received, bf16[1,128,2048]{2,1,0:T(8,128)(2,1)S(1)} %copy-done, ...), custom_call_target="tpu_custom_call" | custom-call | bytes 5775872 | tf_op jit(solution)/shard_map/pallas_call | solution.py:29
  (107 shorter events, 30.6 us)
Async XLA Ops:
  0.6 15.4 %collective-permute-start.4 = (bf16[128,2048]{1,0:T(8,128)(2,1)}, bf16[128,2048]{1,0:T(8,128)(2,1)S(1)}, u32[]{:S(2)}, u32[]{:S(2)}) collective-permute-start(bf16[128,2048]{1,0:T(8,128)(2,1)} %bitcast.3), channel_id=1, source_target_pairs={{0,12},{1,13},{2,14},{3,15},{4,0},{5,1},{6,2},{7,3},{8,4},{9,5},{1... | collective-permute-start | bytes 1572872 | tf_op jit(solution)/shard_map/ppermute | solution.py:55
  4.3 14.5 %collective-permute-start.2 = (bf16[128,2048]{1,0:T(8,128)(2,1)}, bf16[128,2048]{1,0:T(8,128)(2,1)S(1)}, u32[]{:S(2)}, u32[]{:S(2)}) collective-permute-start(bf16[128,2048]{1,0:T(8,128)(2,1)} %bitcast.4), channel_id=1, source_target_pairs={{0,4},{1,5},{2,6},{3,7},{4,8},{5,9},{6,10},{7,11},{8,12},{9,13},{1... | collective-permute-start | bytes 1572872 | tf_op jit(solution)/shard_map/ppermute | solution.py:55
  4.3 14.6 %collective-permute-start.6 = (bf16[128,2048]{1,0:T(8,128)(2,1)}, bf16[128,2048]{1,0:T(8,128)(2,1)S(1)}, u32[]{:S(2)}, u32[]{:S(2)}) collective-permute-start(bf16[128,2048]{1,0:T(8,128)(2,1)} %bitcast.5), channel_id=1, source_target_pairs={{0,2},{1,3},{2,0},{3,1},{4,6},{5,7},{6,4},{7,5},{8,10},{9,11},{10,... | collective-permute-start | bytes 1572872 | tf_op jit(solution)/shard_map/ppermute | solution.py:55
  8.2 30.9 %collective-permute-start = (bf16[128,2048]{1,0:T(8,128)(2,1)S(1)}, bf16[128,2048]{1,0:T(8,128)(2,1)S(1)}, u32[]{:S(2)}, u32[]{:S(2)}) collective-permute-start(bf16[128,2048]{1,0:T(8,128)(2,1)S(1)} %shard_map.110), channel_id=1, source_target_pairs={{0,240},{16,224},{32,208},{48,192},{64,176},{80,160},{96,144},{112... | collective-permute-start | bytes 1572872 | tf_op jit(solution)/shard_map/ppermute | solution.py:42
  16.0 25.3 %collective-permute-start.5 = (bf16[64,2048]{1,0:T(8,128)(2,1)S(1)}, bf16[64,2048]{1,0:T(8,128)(2,1)S(1)}, u32[]{:S(2)}, u32[]{:S(2)}) collective-permute-start(bf16[64,2048]{1,0:T(8,128)(2,1)S(1)} %slice.17), channel_id=1, source_target_pairs={{0,12},{1,13},{2,14},{3,15},{4,0},{5,1},{6,2},{7,3},{8,4},{9,5},{1... | collective-permute-start | bytes 786440 | tf_op jit(solution)/shard_map/ppermute | solution.py:55
  18.8 22.5 %collective-permute-start.3 = (bf16[64,2048]{1,0:T(8,128)(2,1)S(1)}, bf16[64,2048]{1,0:T(8,128)(2,1)S(1)}, u32[]{:S(2)}, u32[]{:S(2)}) collective-permute-start(bf16[64,2048]{1,0:T(8,128)(2,1)S(1)} %slice.16), channel_id=1, source_target_pairs={{0,4},{1,5},{2,6},{3,7},{4,8},{5,9},{6,10},{7,11},{8,12},{9,13},{1... | collective-permute-start | bytes 786440 | tf_op jit(solution)/shard_map/ppermute | solution.py:55
  18.9 36.0 %collective-permute-start.7 = (bf16[128,2048]{1,0:T(8,128)(2,1)S(1)}, bf16[128,2048]{1,0:T(8,128)(2,1)S(1)}, u32[]{:S(2)}, u32[]{:S(2)}) collective-permute-start(bf16[128,2048]{1,0:T(8,128)(2,1)S(1)} %collective-permute-done.6.refs_3_.refs_1_), channel_id=1, source_target_pairs={{0,4},{1,5},{2,6},{3,7},{4,8},{5,9},{6,10},{7,11},{8,12},{9,13},{1... | collective-permute-start | bytes 1572872 | tf_op jit(solution)/shard_map/ppermute | solution.py:55
  19.0 35.9 %collective-permute-start.8 = (bf16[128,2048]{1,0:T(8,128)(2,1)S(1)}, bf16[128,2048]{1,0:T(8,128)(2,1)S(1)}, u32[]{:S(2)}, u32[]{:S(2)}) collective-permute-start(bf16[128,2048]{1,0:T(8,128)(2,1)S(1)} %collective-permute-done.6.refs_3_.refs_1_), channel_id=1, source_target_pairs={{0,12},{1,13},{2,14},{3,15},{4,0},{5,1},{6,2},{7,3},{8,4},{9,5},{1... | collective-permute-start | bytes 1572872 | tf_op jit(solution)/shard_map/ppermute | solution.py:55
  41.3 13.5 %collective-permute-start.9 = (bf16[64,2048]{1,0:T(8,128)(2,1)S(1)}, bf16[64,2048]{1,0:T(8,128)(2,1)S(1)}, u32[]{:S(2)}, u32[]{:S(2)}) collective-permute-start(bf16[64,2048]{1,0:T(8,128)(2,1)S(1)} %collective-permute-done.3.refs_2_.refs_4_), channel_id=1, source_target_pairs={{0,2},{1,3},{2,0},{3,1},{4,6},{5,7},{6,4},{7,5},{8,10},{9,11},{10,... | collective-permute-start | bytes 786440 | tf_op jit(solution)/shard_map/ppermute | solution.py:55
  61.3 14.7 %collective-permute-start.12 = (bf16[128,2048]{1,0:T(8,128)(2,1)}, bf16[128,2048]{1,0:T(8,128)(2,1)}, u32[]{:S(2)}, u32[]{:S(2)}) collective-permute-start(bf16[128,2048]{1,0:T(8,128)(2,1)} %shard_map.114.refs_1_.delta_own), channel_id=1, source_target_pairs={{0,4},{1,5},{2,6},{3,7},{4,8},{5,9},{6,10},{7,11},{8,12},{9,13},{1... | collective-permute-start | bytes 1572872 | tf_op jit(solution)/shard_map/ppermute | solution.py:55
  61.3 16.1 %collective-permute-start.14 = (bf16[128,2048]{1,0:T(8,128)(2,1)}, bf16[128,2048]{1,0:T(8,128)(2,1)}, u32[]{:S(2)}, u32[]{:S(2)}) collective-permute-start(bf16[128,2048]{1,0:T(8,128)(2,1)} %shard_map.114.refs_1_.delta_own), channel_id=1, source_target_pairs={{0,12},{1,13},{2,14},{3,15},{4,0},{5,1},{6,2},{7,3},{8,4},{9,5},{1... | collective-permute-start | bytes 1572872 | tf_op jit(solution)/shard_map/ppermute | solution.py:55
  64.0 16.8 %collective-permute-start.16 = (bf16[128,2048]{1,0:T(8,128)(2,1)}, bf16[128,2048]{1,0:T(8,128)(2,1)}, u32[]{:S(2)}, u32[]{:S(2)}) collective-permute-start(bf16[128,2048]{1,0:T(8,128)(2,1)} %shard_map.114.refs_1_.delta_own), channel_id=1, source_target_pairs={{0,2},{1,3},{2,0},{3,1},{4,6},{5,7},{6,4},{7,5},{8,10},{9,11},{10,... | collective-permute-start | bytes 1572872 | tf_op jit(solution)/shard_map/ppermute | solution.py:55
  64.0 24.3 %collective-permute-start.25 = (bf16[128,2048]{1,0:T(8,128)(2,1)}, bf16[128,2048]{1,0:T(8,128)(2,1)}, u32[]{:S(2)}, u32[]{:S(2)}) collective-permute-start(bf16[128,2048]{1,0:T(8,128)(2,1)} %shard_map.114.refs_1_.delta_own), channel_id=1, source_target_pairs={{0,1},{1,0},{2,3},{3,2},{4,5},{5,4},{6,7},{7,6},{8,9},{9,8},{10,11... | collective-permute-start | bytes 1572872 | tf_op jit(solution)/shard_map/ppermute | solution.py:55
  66.9 28.1 %all-to-all-start = ((bf16[8,2,128,128]{3,2,1,0:T(8,128)(2,1)}), bf16[8,2,128,128]{3,2,1,0:T(8,128)(2,1)}, u32[]{:S(2)}, u32[]{:S(2)}) async-start(bf16[8,2,128,128]{3,2,1,0:T(8,128)(2,1)} %copy-done.22), calls=%async_computation | async-start | bytes 1048576 | tf_op jit(solution)/shard_map/all_to_all | solution.py:293
  77.0 16.6 %collective-permute-start.13 = (bf16[64,2048]{1,0:T(8,128)(2,1)S(1)}, bf16[64,2048]{1,0:T(8,128)(2,1)}, u32[]{:S(2)}, u32[]{:S(2)}) collective-permute-start(bf16[64,2048]{1,0:T(8,128)(2,1)S(1)} %slice.18), channel_id=1, source_target_pairs={{0,4},{1,5},{2,6},{3,7},{4,8},{5,9},{6,10},{7,11},{8,12},{9,13},{1... | collective-permute-start | bytes 786440 | tf_op jit(solution)/shard_map/ppermute | solution.py:55
  78.4 15.8 %collective-permute-start.15 = (bf16[64,2048]{1,0:T(8,128)(2,1)S(1)}, bf16[64,2048]{1,0:T(8,128)(2,1)}, u32[]{:S(2)}, u32[]{:S(2)}) collective-permute-start(bf16[64,2048]{1,0:T(8,128)(2,1)S(1)} %slice.19), channel_id=1, source_target_pairs={{0,12},{1,13},{2,14},{3,15},{4,0},{5,1},{6,2},{7,3},{8,4},{9,5},{1... | collective-permute-start | bytes 786440 | tf_op jit(solution)/shard_map/ppermute | solution.py:55
  80.8 26.6 %collective-permute-start.17 = (bf16[128,2048]{1,0:T(8,128)(2,1)}, bf16[128,2048]{1,0:T(8,128)(2,1)}, u32[]{:S(2)}, u32[]{:S(2)}) collective-permute-start(bf16[128,2048]{1,0:T(8,128)(2,1)} %collective-permute-done.16.refs_2_), channel_id=1, source_target_pairs={{0,4},{1,5},{2,6},{3,7},{4,8},{5,9},{6,10},{7,11},{8,12},{9,13},{1... | collective-permute-start | bytes 1572872 | tf_op jit(solution)/shard_map/ppermute | solution.py:55
  80.8 26.6 %collective-permute-start.18 = (bf16[128,2048]{1,0:T(8,128)(2,1)}, bf16[128,2048]{1,0:T(8,128)(2,1)}, u32[]{:S(2)}, u32[]{:S(2)}) collective-permute-start(bf16[128,2048]{1,0:T(8,128)(2,1)} %collective-permute-done.16.refs_2_), channel_id=1, source_target_pairs={{0,12},{1,13},{2,14},{3,15},{4,0},{5,1},{6,2},{7,3},{8,4},{9,5},{1... | collective-permute-start | bytes 1572872 | tf_op jit(solution)/shard_map/ppermute | solution.py:55
  88.3 28.8 %collective-permute-start.23 = (f32[128,2048]{1,0:T(8,128)}, f32[128,2048]{1,0:T(8,128)}, u32[]{:S(2)}, u32[]{:S(2)}) collective-permute-start(f32[128,2048]{1,0:T(8,128)} %get-tuple-element.44), channel_id=1, source_target_pairs={{0,1},{1,0},{2,3},{3,2},{4,5},{5,4},{6,7},{7,6},{8,9},{9,8},{10,11... | collective-permute-start | bytes 3145736 | tf_op jit(solution)/shard_map/ppermute | solution.py:55
  101.7 17.2 %collective-permute-start.26 = (f32[8,128,128]{2,1,0:T(8,128)S(1)}, f32[8,128,128]{2,1,0:T(8,128)S(1)}, u32[]{:S(2)}, u32[]{:S(2)}) collective-permute-start(f32[8,128,128]{2,1,0:T(8,128)S(1)} %get-tuple-element.46), channel_id=1, source_target_pairs={{0,1},{1,0},{2,3},{3,2},{4,5},{5,4},{6,7},{7,6},{8,9},{9,8},{10,11... | collective-permute-start | bytes 1572872 | tf_op jit(solution)/shard_map/ppermute | solution.py:55
  111.1 37.9 %collective-permute-start.21 = (f32[128,2048]{1,0:T(8,128)S(1)}, f32[128,2048]{1,0:T(8,128)S(1)}, u32[]{:S(2)}, u32[]{:S(2)}) collective-permute-start(f32[128,2048]{1,0:T(8,128)S(1)} %get-tuple-element.38), channel_id=1, source_target_pairs={{0,1},{1,0},{2,3},{3,2},{4,5},{5,4},{6,7},{7,6},{8,9},{9,8},{10,11... | collective-permute-start | bytes 3145736 | tf_op jit(solution)/shard_map/ppermute | solution.py:55
  112.0 25.7 %collective-permute-start.28 = (bf16[128,2048]{1,0:T(8,128)(2,1)S(1)}, bf16[128,2048]{1,0:T(8,128)(2,1)S(1)}, u32[]{:S(2)}, u32[]{:S(2)}) collective-permute-start(bf16[128,2048]{1,0:T(8,128)(2,1)S(1)} %bitcast.12), channel_id=1, source_target_pairs={{0,240},{16,224},{32,208},{48,192},{64,176},{80,160},{96,144},{112... | collective-permute-start | bytes 1572872 | tf_op jit(solution)/shard_map/ppermute | solution.py:42
  118.8 30.0 %collective-permute-start.24 = (bf16[128,2048]{1,0:T(8,128)(2,1)S(1)}, bf16[128,2048]{1,0:T(8,128)(2,1)S(1)}, u32[]{:S(2)}, u32[]{:S(2)}) collective-permute-start(bf16[128,2048]{1,0:T(8,128)(2,1)S(1)} %shard_map.120), channel_id=1, source_target_pairs={{240,0},{0,16},{16,32},{32,48},{48,64},{64,80},{80,96},{96,112},{1... | collective-permute-start | bytes 1572872 | tf_op jit(solution)/shard_map/ppermute | solution.py:47
  119.6 29.3 %collective-permute-start.27 = (bf16[128,2048]{1,0:T(8,128)(2,1)S(1)}, bf16[128,2048]{1,0:T(8,128)(2,1)S(1)}, u32[]{:S(2)}, u32[]{:S(2)}) collective-permute-start(bf16[128,2048]{1,0:T(8,128)(2,1)S(1)} %shard_map.122), channel_id=1, source_target_pairs={{16,0},{32,16},{48,32},{64,48},{80,64},{96,80},{112,96},{128,112},... | collective-permute-start | bytes 1572872 | tf_op jit(solution)/shard_map/ppermute | solution.py:47
  (32 other events, 260.8 us)

commit v3 on v2

v3 whole, which is shorter than its diff:
```python
import functools

import jax
import jax.numpy as jnp
from jax import lax
from jax.experimental import pallas as pl
from jax.experimental.pallas import tpu as pltpu
from jax.sharding import PartitionSpec as P

EPSILON = 1e-05
RING, PAIR, CORES = 4, 2, 2
CHIPS = RING * PAIR
MEMBERS = CHIPS * CORES
BLOCK = 128
TILE = 256
MEGABYTES = 12
WIDTH = 2048

VMEM = pl.BlockSpec(memory_space=pltpu.VMEM)
SMEM = pl.BlockSpec(memory_space=pltpu.SMEM)
ANY = pl.BlockSpec(memory_space=pl.ANY)
F32, BF16 = jnp.float32, jnp.bfloat16


def struct(shape, dtype):
    return jax.ShapeDtypeStruct(shape, dtype)


def call(
    name, kernel, outs, args, specs, out_specs=None, scratch=(), flops=0, after=(), aliases=None
):
    nbytes = sum(a.size * a.dtype.itemsize for a in list(args) + list(outs))
    given = len(args)

    def body(*refs):
        kernel(*refs[:given], *refs[given + len(after) :])

    return pl.pallas_call(
        body,
        out_shape=list(outs),
        in_specs=list(specs) + [ANY] * len(after),
        out_specs=list(out_specs) if out_specs else [VMEM] * len(outs),
        scratch_shapes=list(scratch),
        input_output_aliases=aliases or {},
        name=name,
        cost_estimate=pl.CostEstimate(flops=flops, bytes_accessed=nbytes, transcendentals=0),
        compiler_params=pltpu.CompilerParams(vmem_limit_bytes=MEGABYTES * 1024 * 1024),
    )(*args, *after)


def mirrored(block):
    count = lax.axis_size("section")
    return lax.ppermute(block, "section", [(i, count - 1 - i) for i in range(count)])


def shifted(block, distance):
    count = lax.axis_size("section")
    return lax.ppermute(block, "section", [((i - distance) % count, i) for i in range(count)])


def hop(block, ring=0, pair=0, core=0):
    route = []
    for i in range(MEMBERS):
        y, x, c = i // (PAIR * CORES), i // CORES % PAIR, i % CORES
        route.append((i, (((y + ring) % RING) * PAIR + (x ^ pair)) * CORES + (c ^ core)))
    return lax.ppermute(block, "dp", route)


def gathered(own, after=(), take_after=()):
    rows, width = own.shape
    half = rows // 2
    with jax.named_scope("below"):
        below = hop(own, ring=1)
    with jax.named_scope("above"):
        above = hop(own, ring=-1)
    with jax.named_scope("pair"):
        pair = hop(own, pair=1)
    packed = struct((half + rows, width), own.dtype)
    up, down = call(
        "pack",
        pack_kernel,
        [packed, packed],
        [below, above, pair],
        [VMEM] * 3,
        scratch=[pltpu.SemaphoreType.DMA((4,))],
        after=after,
    )
    with jax.named_scope("up"):
        up = hop(up, ring=1)
    with jax.named_scope("down"):
        down = hop(down, ring=-1)
    halves = struct((half, width), own.dtype)
    low, high, token = call(
        "take",
        take_kernel,
        [halves, halves, struct((8, BLOCK), F32)],
        [up, down],
        [VMEM] * 2,
        scratch=[pltpu.SemaphoreType.DMA((2,))],
        after=take_after,
    )
    with jax.named_scope("far_up"):
        far_up = hop(low, ring=1)
    with jax.named_scope("far_down"):
        far_down = hop(high, ring=-1)
    near = [
        (0, 0, [(own, 0, rows)]),
        (-1, 0, [(below, 0, rows)]),
        (1, 0, [(above, 0, rows)]),
        (0, 1, [(pair, 0, rows)]),
    ]
    middle = [
        (2, 0, [(up, 0, half), (down, rows, rows + half)]),
        (-1, 1, [(up, half, half + rows)]),
        (1, 1, [(down, 0, rows)]),
    ]
    far = [(2, 1, [(far_up, 0, half), (far_down, 0, half)])]
    return near, middle, far, token


def arrays_of(chunks):
    arrays, layout = [], []
    for up, other, pieces in chunks:
        placed = []
        for array, first, last in pieces:
            at = next((i for i, a in enumerate(arrays) if a is array), len(arrays))
            if at == len(arrays):
                arrays.append(array)
            placed.append((at, first, last))
        layout.append((up, other, placed))
    return arrays, layout


def place():
    member = lax.axis_index("dp")
    core = lax.rem(member, CORES)
    return member, core


def chip_of(up, other):
    member = lax.axis_index("dp")
    ring_at = lax.div(member, PAIR * CORES)
    pair_at = lax.rem(lax.div(member, CORES), PAIR)
    pair_to = 1 - pair_at if other else pair_at
    return lax.rem(ring_at + up + RING, RING) * PAIR + pair_to


def columns_of(step):
    return pl.ds(pl.multiple_of(step * TILE, TILE), TILE)


def inverse_rms(values):
    return lax.rsqrt(jnp.mean(values * values, -1, keepdims=True) + EPSILON)


def split_kernel(slots, held, mine, send, panel, sem):
    _, core = place()
    partner = lax.axis_size("section") - 1 - lax.axis_index("section")
    copy = pltpu.make_async_copy(held.at[0, slots[partner]], panel, sem)
    copy.start()
    copy.wait()
    for chip in range(CHIPS):
        at, to = chip * CORES * BLOCK, chip * BLOCK
        first, second = panel[:, at : at + BLOCK], panel[:, at + BLOCK : at + 2 * BLOCK]
        mine[:, to : to + BLOCK] = jnp.where(core == 0, first, second)
        send[:, to : to + BLOCK] = jnp.where(core == 0, second, first)


def join_kernel(mine, received, joined):
    rows = mine.shape[0]
    joined[:rows] = mine[...]
    joined[rows:] = received[...]


def copy_all(pairs, sems):
    copies = [pltpu.make_async_copy(a, b, sems.at[i]) for i, (a, b) in enumerate(pairs)]
    for copy in copies:
        copy.start()
    return copies


def pack_kernel(below, above, pair, up, down, sems):
    rows = pair.shape[0]
    half = rows // 2
    copies = copy_all(
        [
            (pair, up.at[pl.ds(half, rows)]),
            (pair, down.at[pl.ds(0, rows)]),
            (below.at[pl.ds(0, half)], up.at[pl.ds(0, half)]),
            (above.at[pl.ds(half, half)], down.at[pl.ds(rows, half)]),
        ],
        sems,
    )
    for copy in copies:
        copy.wait()


def take_kernel(up, down, low, high, token, sems):
    token[...] = jnp.zeros_like(token)
    rows = low.shape[0]
    copies = copy_all([(up.at[pl.ds(rows, rows)], low), (down.at[pl.ds(rows, rows)], high)], sems)
    for copy in copies:
        copy.wait()


def units_kernel(half, received, keep, send, panel):
    member, core = place()
    pair_at = lax.rem(lax.div(member, CORES), PAIR)
    rows = received.shape[0]
    for chip in range(CHIPS):
        at, of = chip * CORES * BLOCK, chip * BLOCK
        own, other = half[:rows, of : of + BLOCK], received[:, of : of + BLOCK]
        panel[:, at : at + BLOCK] = jnp.where(core == 0, own, other)
        panel[:, at + BLOCK : at + 2 * BLOCK] = jnp.where(core == 0, other, own)
    values = panel[...].astype(F32)
    unit = values * inverse_rms(values)
    for y in range(RING):
        blocks = []
        for block in range(PAIR * CORES):
            at = (y * PAIR * CORES + block) * BLOCK
            blocks.append(jnp.transpose(unit[:, at : at + BLOCK]).astype(BF16))
        for c in range(CORES):
            mine = [jnp.where(core == 0, blocks[x + c], blocks[x + 1 - c]) for x in (0, CORES)]
            keep[y, c] = jnp.where(pair_at == 0, mine[0], mine[1])
            send[y, c] = jnp.where(pair_at == 0, mine[1], mine[0])


def mix_kernel(keep, received, mixed, token):
    token[...] = jnp.zeros_like(token)
    for y in range(RING):
        mixed[y, 0] = keep[y]
        mixed[y, 1] = received[y]


def normed_kernel(rows, gain, mine, send):
    _, core = place()
    values = rows[...].astype(F32)
    unit = values * inverse_rms(values)
    normed = (unit * gain[...]).astype(BF16)
    for chip in range(CHIPS):
        at = chip * CORES * BLOCK
        first, second = normed[:, at : at + BLOCK], normed[:, at + BLOCK : at + 2 * BLOCK]
        mine[chip] = jnp.where(core == 0, first, second)
        send[chip] = jnp.where(core == 0, second, first)


def product_kernel(layout, kind, added, *refs):
    refs = list(refs)
    left, token = refs.pop(), refs.pop(-1)
    token[...] = jnp.zeros_like(token)
    out_own, out_other = refs[-2:]
    del refs[-2:]
    _, core = place()
    first_ref, second_ref = refs.pop(0), None if kind == "stacked" else refs.pop(0)
    totals = [refs.pop(), refs.pop()][::-1] if added else None
    for k, (up, to_other, _) in enumerate(layout):
        chip = chip_of(up, to_other)
        columns = slice(k * BLOCK, (k + 1) * BLOCK)
        if kind == "stacked":
            left[:BLOCK, columns] = first_ref[lax.div(chip, PAIR), to_other, 0]
            left[BLOCK:, columns] = first_ref[lax.div(chip, PAIR), to_other, 1]
        elif kind == "pair":
            left[:BLOCK, columns] = first_ref[chip]
            left[BLOCK:, columns] = second_ref[chip]
        else:
            at = pl.ds(pl.multiple_of(chip * BLOCK, BLOCK), BLOCK)
            of = pl.ds(pl.multiple_of((chip * CORES + core) * BLOCK, BLOCK), BLOCK)
            left[:, columns] = (first_ref[:, at].astype(F32) * second_ref[:, of]).astype(BF16)

    @pl.loop(0, WIDTH // TILE)
    def _(step):
        columns = columns_of(step)
        right = jnp.concatenate(
            [refs[i][first:last, columns] for _, _, placed in layout for i, first, last in placed], 0
        )
        result = jnp.dot(left[...], right, preferred_element_type=F32)
        low, high = result[:BLOCK], result[BLOCK:]
        if added:
            low, high = low + totals[0][:, columns], high + totals[1][:, columns]
        out_own[:, columns] = low
        out_other[:, columns] = high.astype(out_other.dtype)

    if kind == "panel":
        if added:
            squares = totals[1][:, WIDTH:]
            rounded = squares.astype(BF16)
            out_own[:, WIDTH:] = totals[0][:, WIDTH:]
            out_other[:, WIDTH : WIDTH + BLOCK] = rounded
            out_other[:, WIDTH + BLOCK :] = (squares - rounded.astype(F32)).astype(BF16)
        else:
            values = first_ref[...].astype(F32)
            squares = jnp.broadcast_to(
                jnp.sum(values * values, -1, keepdims=True), (2 * BLOCK, BLOCK)
            )
            out_own[:, WIDTH:] = squares[:BLOCK]
            out_other[:, WIDTH:] = squares[BLOCK:]


def product(name, kind, blocks, chunks, totals=(), after=()):
    parts, layout = arrays_of(chunks)
    depth, width = len(chunks) * BLOCK, WIDTH + (BLOCK if kind == "panel" else 0)
    last = struct((BLOCK, width + (BLOCK if kind == "panel" else 0)), BF16)
    args = [*blocks, *parts, *totals]
    out = struct((BLOCK, width), F32)
    return call(
        name,
        functools.partial(product_kernel, layout, kind, bool(totals)),
        [out, last if totals else out, struct((8, BLOCK), F32)],
        args,
        [VMEM] * len(args),
        scratch=[pltpu.VMEM((2 * BLOCK, depth), BF16)],
        flops=2 * 2 * BLOCK * depth * width,
        after=after,
    )


def delta_kernel(own, received, grads, delta):
    squares = own[:, WIDTH : WIDTH + 1] + (
        received[:, WIDTH : WIDTH + 1].astype(F32)
        + received[:, WIDTH + BLOCK : WIDTH + BLOCK + 1].astype(F32)
    )
    inverse = lax.rsqrt(squares * (1.0 / WIDTH) + EPSILON)

    @pl.loop(0, WIDTH // TILE)
    def _(step):
        columns = columns_of(step)
        pre_act = (own[:, columns] + received[:, columns].astype(F32)) * inverse
        sigma = jax.nn.sigmoid(pre_act)
        grad_f = grads[:, columns].astype(F32)
        delta[:, columns] = (grad_f * sigma * (1.0 + pre_act * (1.0 - sigma))).astype(BF16)


def out_kernel(own, received, acts, out, token):
    token[...] = jnp.zeros_like(token)

    @pl.loop(0, out.shape[1] // TILE)
    def _(step):
        columns = columns_of(step)
        pre_act = own[:, columns] + received[:, columns].astype(F32)
        values = acts[:, columns].astype(F32)
        out[:, columns] = (values + pre_act * jax.nn.sigmoid(pre_act)).astype(BF16)


def back_kernel(layout, delta_own, delta_other, *refs):
    refs = list(refs)
    left = refs.pop()
    back_own, back_other = refs[-2:]
    left[:BLOCK] = delta_own[...]
    left[BLOCK:] = delta_other[...]
    for k in range(0, len(layout), 2):
        right = jnp.concatenate(
            [refs[i][first:last] for _, _, placed in layout[k : k + 2] for i, first, last in placed], 0
        )
        result = lax.dot_general(
            left[...], right, (((1,), (1,)), ((), ())), preferred_element_type=F32
        )
        for i, (up, other, _) in enumerate(layout[k : k + 2]):
            chip = chip_of(up, other)
            back_own[chip] = result[:BLOCK, i * BLOCK : (i + 1) * BLOCK]
            back_other[chip] = result[BLOCK:, i * BLOCK : (i + 1) * BLOCK]


def grad_kernel(panel, gain, grads, back_own, back_received, grad_acts, token, through):
    token[...] = jnp.zeros_like(token)
    _, core = place()
    values = panel[...].astype(F32)
    inverse = inverse_rms(values)
    for chip in range(CHIPS):
        at = chip * CORES * BLOCK
        own, received = back_own[chip], back_received[chip]
        through[:, at : at + BLOCK] = jnp.where(core == 0, own, received)
        through[:, at + BLOCK : at + 2 * BLOCK] = jnp.where(core == 0, received, own)
    unit = values * inverse
    scaled = through[...] * gain[...]
    mean = jnp.mean(scaled * unit, -1, keepdims=True)
    grad_acts[...] = (grads[...].astype(F32) + inverse * (scaled - unit * mean)).astype(BF16)


def keep_kernel(held, out, token, sem):
    copy = pltpu.make_async_copy(held, out, sem)
    copy.start()
    token[...] = jnp.zeros_like(token)
    copy.wait()


def park_kernel(slots, kept, stashed, out, token, sem):
    del kept
    partner = lax.axis_size("section") - 1 - lax.axis_index("section")
    copy = pltpu.make_async_copy(stashed, out.at[0, slots[partner]], sem)
    copy.start()
    token[...] = jnp.zeros_like(token)
    copy.wait()


def emit_kernel(acts, grads, next_acts, next_grads, token):
    next_acts[0] = acts[...]
    next_grads[0] = grads[...]
    token[...] = jnp.zeros_like(token)


def finish_kernel(own, received, weight, gain, weight_grad, gain_grad):
    member, _ = place()
    own_gain = gain[:, pl.ds(pl.multiple_of(member * BLOCK, BLOCK), BLOCK)]
    scale = jnp.transpose(jnp.broadcast_to(own_gain, (BLOCK, BLOCK)))[:, :1]
    total = jnp.zeros((BLOCK, 1), F32)
    for at in range(0, own.shape[1], TILE):
        outer = own[:, at : at + TILE] + received[:, at : at + TILE].astype(F32)
        weight_grad[0, :, at : at + TILE] = outer * scale
        total += jnp.sum(outer * weight[0, :, at : at + TILE].astype(F32), -1, keepdims=True)
    gain_grad[...] = jnp.transpose(jnp.broadcast_to(total, (BLOCK, BLOCK)))[:1]


def shards(weight, gain, acts_in, grads_in, parked, fetch_slot, park_slot):
    tokens, width = acts_in.shape[1:]
    acts, grads = acts_in[0], grads_in[0]
    rows, blocks = struct((tokens, width), BF16), struct((CHIPS, BLOCK, BLOCK), BF16)
    token = struct((8, BLOCK), F32)
    back = struct((CHIPS, BLOCK, BLOCK), F32)

    half = struct((tokens, width // CORES), BF16)
    mine, send = call(
        "split",
        split_kernel,
        [half, half],
        [fetch_slot, parked],
        [SMEM, ANY],
        scratch=[pltpu.VMEM((tokens, width), BF16), pltpu.SemaphoreType.DMA],
    )
    (joined,) = call(
        "join",
        join_kernel,
        [struct((2 * tokens, width // CORES), BF16)],
        [mine, hop(send, core=1)],
        [VMEM] * 2,
    )
    with jax.named_scope("panel"):
        panel_half = mirrored(joined)
    mine, send = call("norm_acts", normed_kernel, [blocks, blocks], [acts, gain], [VMEM] * 2)
    kept, kept_token = call(
        "keep",
        keep_kernel,
        [struct(parked.shape, BF16), token],
        [parked],
        [VMEM],
        [ANY, VMEM],
        [pltpu.SemaphoreType.DMA],
        after=[joined],
    )
    with jax.named_scope("weight"):
        near, middle, far, _ = gathered(weight[0], after=[joined, mine, kept_token])

    with jax.named_scope("acts"):
        forward = [mine, hop(send, core=1)]
    *pre, _ = product("forward_near", "pair", forward, near)
    pre_own, pre_other, forward_token = product(
        "forward_far", "pair", forward, middle + far, pre
    )

    backward = [panel_half, gain]
    *panel_pre, _ = product(
        "backward_near", "panel", backward, near + middle, after=[forward_token]
    )
    panel_own, panel_other, _ = product("backward_far", "panel", backward, far, panel_pre)
    with jax.named_scope("pre_acts"):
        received = hop(pre_other, core=1)
    out_rows, out_token = call(
        "out",
        out_kernel, [rows, token], [pre_own, received, acts], [VMEM] * 3
    )
    with jax.named_scope("next_acts"):
        next_acts = shifted(out_rows, 1)

    with jax.named_scope("pre"):
        received = hop(panel_other, core=1)
    with jax.named_scope("restore"):
        restored = hop(panel_half[tokens:], core=1)
    ring_blocks = (RING, CORES, BLOCK, BLOCK)
    keep, send, panel = call(
        "units",
        units_kernel,
        [struct(ring_blocks, BF16), struct(ring_blocks, BF16), rows],
        [panel_half, restored],
        [VMEM] * 2,
    )
    (delta,) = call(
        "delta", delta_kernel, [rows], [panel_own, received, grads], [VMEM] * 3, after=[keep]
    )
    with jax.named_scope("delta"):
        delta_near, delta_middle, delta_far, take_token = gathered(delta, [out_token])
    with jax.named_scope("stash"):
        stashed = mirrored(acts)

    with jax.named_scope("pair_units"):
        received = hop(send, pair=1)
    mixed, mix_token = call(
        "mix",
        mix_kernel,
        [struct((RING, PAIR, CORES, BLOCK, BLOCK), BF16), token],
        [keep, received],
        [VMEM] * 2,
    )
    units = lax.all_to_all(
        mixed,
        "dp",
        split_axis=0,
        concat_axis=0,
        tiled=True,
        axis_index_groups=[
            [(y * PAIR + x) * CORES + c for y in range(RING)] for x in range(PAIR) for c in range(CORES)
        ],
    )

    with jax.named_scope("delta_other"):
        delta_other = hop(delta, core=1)
    chunks = near + middle + far
    parts, layout = arrays_of(chunks)
    back_own, back_other = call(
        "back",
        functools.partial(back_kernel, layout),
        [back, back],
        [delta, delta_other, *parts],
        [VMEM] * (2 + len(parts)),
        scratch=[pltpu.VMEM((2 * BLOCK, width), BF16)],
        flops=2 * 2 * BLOCK * CHIPS * BLOCK * width,
    )
    with jax.named_scope("back"):
        back_received = hop(back_other, core=1)
    grad_acts, grad_token = call(
        "grads",
        grad_kernel,
        [rows, token],
        [panel, gain, grads, back_own, back_received],
        [VMEM] * 5,
        scratch=[pltpu.VMEM((tokens, width), F32)],
    )
    with jax.named_scope("next_grads"):
        next_grads = shifted(grad_acts, -1)
    *outer, near_token = product(
        "outer_near",
        "stacked",
        [units],
        delta_near + delta_middle,
        after=[grad_token],
    )
    parked_out, parked_token = call(
        "park",
        park_kernel,
        [struct(parked.shape, BF16), token],
        [park_slot, kept, stashed],
        [SMEM, ANY, VMEM],
        [ANY, VMEM],
        [pltpu.SemaphoreType.DMA],
        aliases={1: 0},
        after=[near_token],
    )

    outer_own, outer_other, outer_token = product(
        "outer_far", "stacked", [units], delta_far, outer, after=[parked_token, next_acts, next_grads]
    )
    with jax.named_scope("outer"):
        outer_received = hop(outer_other, core=1)
    next_acts, next_grads, emitted = call(
        "emit",
        emit_kernel,
        [struct((1, tokens, width), BF16), struct((1, tokens, width), BF16), token],
        [next_acts, next_grads],
        [VMEM] * 2,
        after=[outer_token],
    )
    weight_grad, gain_grad = call(
        "finish",
        finish_kernel,
        [struct((1, BLOCK, width), F32), struct((1, BLOCK), F32)],
        [outer_own, outer_received, weight, gain],
        [VMEM] * 4,
        after=[emitted],
    )
    return next_acts, next_grads, parked_out, weight_grad, gain_grad


def solution(mesh):
    return jax.shard_map(
        shards,
        mesh=mesh,
        in_specs=(
            P("section", "dp", None),
            P("section", None),
            P("section", "dp", None),
            P("section", "dp", None),
            P("section", None, "dp", None),
            P(),
            P(),
        ),
        out_specs=(
            P("section", "dp", None),
            P("section", "dp", None),
            P("section", None, "dp", None),
            P("section", "dp", None),
            P("section", "dp"),
        ),
        check_vma=False,
    )
```

time: 152 us -> 129 us (0.85)
  waiting for transfers between devices: 58 us -> 35.6 us
  Pallas kernels: 30.1 us -> 32.9 us
  starting transfers between devices: 54.4 us -> 52.3 us
    ppermute x2, waiting for transfers between devices: 30.4 us -> 7.73 us  [mirrored(): lax.ppermute(block, 'section', [(i, count - 1 - i) for i in range(count)])]
    ppermute x25 -> x23, starting transfers between devices: 32.1 us -> 28.4 us  [hop(): return lax.ppermute(block, 'dp', route)]
    all_to_all x1, waiting for transfers between devices: 0.01 us -> 3.67 us  [shards(): lax.all_to_all(mixed, 'dp', split_axis=0, concat_axis=0, tiled=True, axis...]
    pallas_call x15 -> x23, Pallas kernels: 30.1 us -> 32.9 us  [call(): pl.pallas_call(body, out_shape=list(outs), in_specs=list(specs) + [ANY] *...]
    ppermute x2, starting transfers between devices: 12.9 us -> 15.2 us  [mirrored(): lax.ppermute(block, 'section', [(i, count - 1 - i) for i in range(count)])]
    slice x4 -> x1, local copies, waits for them, and re-layouts: 1.97 us -> 0.02 us  [shards(): restored = hop(panel_half[tokens:], core=1)]
    ppermute x2, waiting for transfers between devices: 9.5 us -> 7.75 us  [shifted(): lax.ppermute(block, 'section', [((i - distance) % count, i) for i in rang...]
    ppermute x25 -> x23, waiting for transfers between devices: 18.1 us -> 16.5 us  [hop(): return lax.ppermute(block, 'dp', route)]
  transfers between devices with their start and end apart: 30 -> 28, of which waited for: 10 -> 12; matrix products, arithmetic and copies ran while one was open for 1% -> 0% of each run, Pallas kernels for 16% -> 19%
where the time goes in v3:
time: 129 us; the launch traced here: 128 us
  starting transfers between devices  52.3 us (41%)
  waiting for transfers between devices  35.6 us (28%)
  Pallas kernels  32.9 us (26%)
  local copies, waits for them, and re-layouts  6.73 us (5%)
    pallas_call x23, Pallas kernels, call(): pl.pallas_call(body, out_shape=list(outs), in_specs=list(specs) + [ANY] *...  32.9 us
    ppermute x23, starting transfers between devices, hop(): return lax.ppermute(block, 'dp', route)  28.4 us
    ppermute x23, waiting for transfers between devices, hop(): return lax.ppermute(block, 'dp', route)  16.5 us
    ppermute x2, starting transfers between devices, mirrored(): lax.ppermute(block, 'section', [(i, count - 1 - i) for i in range(count)])  15.2 us
    ppermute x2, waiting for transfers between devices, shifted(): lax.ppermute(block, 'section', [((i - distance) % count, i) for i in rang...  7.75 us
    ppermute x2, waiting for transfers between devices, mirrored(): lax.ppermute(block, 'section', [(i, count - 1 - i) for i in range(count)])  7.73 us
    unnamed x30, local copies, waits for them, and re-layouts  6.71 us
    ppermute x2, starting transfers between devices, shifted(): lax.ppermute(block, 'section', [((i - distance) % count, i) for i in rang...  5.16 us
  transfers between devices with their start and end apart: 28, of which 12 were waited for; matrix products, arithmetic and copies ran while one was open for 0% of the time, Pallas kernels for 19%

profile of v3, /device:TPU:1, one launch (start us, length us, event | category | flops | bytes accessed | tf_op | source)
XLA Modules:
  0.0 128.4 jit_solution(16313783723543151677)
XLA Ops:
  0.6 2.2 %collective-permute-start.1 = (bf16[128,2048]{1,0:T(8,128)(2,1)}, bf16[128,2048]{1,0:T(8,128)(2,1)S(1)}, u32[]{:S(2)}, u32[]{:S(2)}) collective-permute-start(bf16[128,2048]{1,0:T(8,128)(2,1)} %bitcast.3), channel_id=1, source_target_pairs={{0,4},{1,5},{2,6},{3,7},{4,8},{5,9},{6,10},{7,11},{8,12},{9,13},{1... | collective-permute-start | bytes 1572872 | tf_op jit(solution)/shard_map/weight/below/ppermute | solution.py:66
  18.7 9.2 %collective-permute-start.11 = (bf16[256,1024]{1,0:T(8,128)(2,1)S(1)}, bf16[256,1024]{1,0:T(8,128)(2,1)S(1)}, u32[]{:S(2)}, u32[]{:S(2)}) collective-permute-start(bf16[256,1024]{1,0:T(8,128)(2,1)S(1)} %join.1.refs_1_.refs_3_), channel_id=1, source_target_pairs={{0,240},{16,224},{32,208},{48,192},{64,176},{80,160},{96,144},{112... | collective-permute-start | bytes 1572872 | tf_op jit(solution)/shard_map/panel/ppermute | solution.py:53
  27.9 2.8 %collective-permute-start = (bf16[8,128,128]{2,1,0:T(8,128)(2,1)S(1)}, bf16[8,128,128]{2,1,0:T(8,128)(2,1)S(1)}, u32[]{:S(2)}, u32[]{:S(2)}) collective-permute-start(bf16[8,128,128]{2,1,0:T(8,128)(2,1)S(1)} %get-tuple-element.52), channel_id=1, source_target_pairs={{0,1},{1,0},{2,3},{3,2},{4,5},{5,4},{6,7},{7,6},{8,9},{9,8},{10,11... | collective-permute-start | bytes 786440 | tf_op jit(solution)/shard_map/acts/ppermute | solution.py:66
  30.7 2.4 %collective-permute-done.5.refs_0_.refs_2_.refs_6_ = bf16[192,2048]{1,0:T(8,128)(2,1)S(1)} collective-permute-done((bf16[192,2048]{1,0:T(8,128)(2,1)S(1)}, bf16[192,2048]{1,0:T(8,128)(2,1)S(1)}, u32[]{:S(2)}, u32[]{:S(2)}) %collective-permute-start.5) | collective-permute-done | bytes 786464 | tf_op jit(solution)/shard_map/weight/up/ppermute | solution.py:66
  37.2 2.3 %forward_near.1 = (f32[128,2048]{1,0:T(8,128)S(1)}, f32[128,2048]{1,0:T(8,128)S(1)}, f32[8,128]{1,0:T(8,128)}) custom-call(bf16[8,128,128]{2,1,0:T(8,128)(2,1)S(1)} %get-tuple-element.51.refs_4_.refs_0_, bf16[8,128,128]{2,1,0:T(8,128)(2,1)S(1)} %collective-permute-done.refs_1_, bf16[128,2048]{1,0:T(8,128)(2,1)S(1)} %bitcast.6, ...), custom_call_target="tpu_custom_call" | custom-call | flops 536870912 | bytes 4722688 | tf_op jit(solution)/shard_map/forward_near/pallas_call | solution.py:38
  41.2 2.0 %forward_far.1 = (f32[128,2048]{1,0:T(8,128)S(1)}, bf16[128,2048]{1,0:T(8,128)(2,1)S(1)}, f32[8,128]{1,0:T(8,128)S(1)}) custom-call(bf16[8,128,128]{2,1,0:T(8,128)(2,1)S(1)} %get-tuple-element.51.refs_4_.refs_0_, bf16[8,128,128]{2,1,0:T(8,128)(2,1)S(1)} %collective-permute-done.refs_1_, bf16[192,2048]{1,0:T(8,128)(2,1)S(1)} %collective-permute-done.5.refs_0_.refs_2_.refs_6_, ...), custom_call_target="tpu_custom_call" | custom-call | flops 536870912 | bytes 6295552 | tf_op jit(solution)/shard_map/forward_far/pallas_call | solution.py:38
  43.2 7.7 %collective-permute-done.11.refs_0_ = bf16[256,1024]{1,0:T(8,128)(2,1)S(1)} collective-permute-done((bf16[256,1024]{1,0:T(8,128)(2,1)S(1)}, bf16[256,1024]{1,0:T(8,128)(2,1)S(1)}, u32[]{:S(2)}, u32[]{:S(2)}) %collective-permute-start.11) | collective-permute-done | bytes 524320 | tf_op jit(solution)/shard_map/panel/ppermute | solution.py:53
  51.0 3.0 %backward_near.1 = (f32[128,2176]{1,0:T(8,128)S(1)}, f32[128,2176]{1,0:T(8,128)S(1)}, f32[8,128]{1,0:T(8,128)}) custom-call(bf16[256,1024]{1,0:T(8,128)(2,1)S(1)} %collective-permute-done.11.refs_0_, f32[1,2048]{1,0:T(1,128)S(1)} %copy-done.12, bf16[128,2048]{1,0:T(8,128)(2,1)S(1)} %bitcast.7, bf16[128,2048]{1,0:T(8,128)(2,1)S(1)} %collective-permute-done.1.refs_0_.refs_3_, ...), custom_call_target="tpu_custom_call" | custom-call | flops 998244352 | bytes 6434816 | tf_op jit(solution)/shard_map/backward_near/pallas_call | solution.py:38
  53.9 2.0 %backward_far.1 = (f32[128,2176]{1,0:T(8,128)S(1)}, bf16[128,2304]{1,0:T(8,128)(2,1)S(1)}, f32[8,128]{1,0:T(8,128)}) custom-call(bf16[256,1024]{1,0:T(8,128)(2,1)S(1)} %collective-permute-done.11.refs_0_, f32[1,2048]{1,0:T(1,128)S(1)} %copy-done.12, bf16[64,2048]{1,0:T(8,128)(2,1)S(1)} %collective-permute-done.7.refs_4_.refs_2_.refs_8_, ...), custom_call_target="tpu_custom_call" | custom-call | flops 142606336 | bytes 4993024 | tf_op jit(solution)/shard_map/backward_far/pallas_call | solution.py:38
  57.1 1.9 %collective-permute-done.12.refs_1_ = bf16[128,1024]{1,0:T(8,128)(2,1)S(1)} collective-permute-done((bf16[128,1024]{1,0:T(8,128)(2,1)S(1)}, bf16[128,1024]{1,0:T(8,128)(2,1)S(1)}, u32[]{:S(2)}, u32[]{:S(2)}) %collective-permute-start.12) | collective-permute-done | bytes 262176 | tf_op jit(solution)/shard_map/restore/ppermute | solution.py:66
  61.2 2.7 %collective-permute-start.19 = (bf16[128,2048]{1,0:T(8,128)(2,1)S(1)}, bf16[128,2048]{1,0:T(8,128)(2,1)S(1)}, u32[]{:S(2)}, u32[]{:S(2)}) collective-permute-start(bf16[128,2048]{1,0:T(8,128)(2,1)S(1)} %delta.1.refs_0_.refs_1_), channel_id=1, source_target_pairs={{0,12},{1,13},{2,14},{3,15},{4,0},{5,1},{6,2},{7,3},{8,4},{9,5},{1... | collective-permute-start | bytes 1572872 | tf_op jit(solution)/shard_map/delta/above/ppermute | solution.py:66
  64.2 2.2 %out.1 = (bf16[128,2048]{1,0:T(8,128)(2,1)}, f32[8,128]{1,0:T(8,128)S(1)}) custom-call(f32[128,2048]{1,0:T(8,128)S(1)} %get-tuple-element.62.refs_0_, bf16[128,2048]{1,0:T(8,128)(2,1)S(1)} %collective-permute-done.9.refs_1_, bf16[128,2048]{1,0:T(8,128)(2,1)} %bitcast.refs_0_.refs_2_), custom_call_target="tpu_custom_call" | custom-call | bytes 2625536 | tf_op jit(solution)/shard_map/out/pallas_call | solution.py:38
  68.9 6.6 %collective-permute-done.18.refs_0_.refs_2_ = bf16[128,2048]{1,0:T(8,128)(2,1)S(1)} collective-permute-done((bf16[128,2048]{1,0:T(8,128)(2,1)S(1)}, bf16[128,2048]{1,0:T(8,128)(2,1)S(1)}, u32[]{:S(2)}, u32[]{:S(2)}) %collective-permute-start.18) | collective-permute-done | bytes 524320 | tf_op jit(solution)/shard_map/delta/below/ppermute | solution.py:66
  77.8 2.7 %collective-permute-start.22 = (bf16[192,2048]{1,0:T(8,128)(2,1)}, bf16[192,2048]{1,0:T(8,128)(2,1)S(1)}, u32[]{:S(2)}, u32[]{:S(2)}) collective-permute-start(bf16[192,2048]{1,0:T(8,128)(2,1)} %get-tuple-element.79), channel_id=1, source_target_pairs={{0,12},{1,13},{2,14},{3,15},{4,0},{5,1},{6,2},{7,3},{8,4},{9,5},{1... | collective-permute-start | bytes 2359304 | tf_op jit(solution)/shard_map/delta/down/ppermute | solution.py:66
  80.8 6.0 %collective-permute-start.25 = (bf16[128,2048]{1,0:T(8,128)(2,1)}, bf16[128,2048]{1,0:T(8,128)(2,1)}, u32[]{:S(2)}, u32[]{:S(2)}) collective-permute-start(bf16[128,2048]{1,0:T(8,128)(2,1)} %bitcast.refs_0_.refs_2_), channel_id=1, source_target_pairs={{0,240},{16,224},{32,208},{48,192},{64,176},{80,160},{96,144},{112... | collective-permute-start | bytes 1572872 | tf_op jit(solution)/shard_map/stash/ppermute | solution.py:53
  86.8 2.0 %collective-permute-start.10 = (bf16[128,2048]{1,0:T(8,128)(2,1)}, bf16[128,2048]{1,0:T(8,128)(2,1)}, u32[]{:S(2)}, u32[]{:S(2)}) collective-permute-start(bf16[128,2048]{1,0:T(8,128)(2,1)} %get-tuple-element.64), channel_id=1, source_target_pairs={{240,0},{0,16},{16,32},{32,48},{48,64},{64,80},{80,96},{96,112},{1... | collective-permute-start | bytes 1572872 | tf_op jit(solution)/shard_map/next_acts/ppermute | solution.py:58
  90.3 3.1 %collective-permute-start.16 = (bf16[128,2048]{1,0:T(8,128)(2,1)}, bf16[128,2048]{1,0:T(8,128)(2,1)}, u32[]{:S(2)}, u32[]{:S(2)}) collective-permute-start(bf16[128,2048]{1,0:T(8,128)(2,1)} %get-tuple-element.74), channel_id=1, source_target_pairs={{16,0},{32,16},{48,32},{64,48},{80,64},{96,80},{112,96},{128,112},... | collective-permute-start | bytes 1572872 | tf_op jit(solution)/shard_map/next_grads/ppermute | solution.py:58
  94.9 3.5 %all-to-all-start = ((bf16[4,2,2,128,128]{4,3,2,1,0:T(8,128)(2,1)}), bf16[4,2,2,128,128]{4,3,2,1,0:T(8,128)(2,1)S(1)}, u32[]{:S(2)}, u32[]{:S(2)}) async-start(bf16[4,2,2,128,128]{4,3,2,1,0:T(8,128)(2,1)} %copy-done.10), calls=%async_computation | async-start | bytes 1048576 | tf_op jit(solution)/shard_map/all_to_all | solution.py:502
  102.0 3.7 %all-to-all-done.refs_0_ = bf16[4,2,2,128,128]{4,3,2,1,0:T(8,128)(2,1)S(1)} async-done(((bf16[4,2,2,128,128]{4,3,2,1,0:T(8,128)(2,1)}), bf16[4,2,2,128,128]{4,3,2,1,0:T(8,128)(2,1)S(1)}, u32[]{:S(2)}, u32[]{:S(2)}) %all-to-all-start) | async-done | bytes 524320 | tf_op jit(solution)/shard_map/all_to_all | solution.py:502
  108.8 2.6 %outer_near.1 = (f32[128,2048]{1,0:T(8,128)S(1)}, f32[128,2048]{1,0:T(8,128)S(1)}, f32[8,128]{1,0:T(8,128)S(1)}) custom-call(bf16[4,2,2,128,128]{4,3,2,1,0:T(8,128)(2,1)S(1)} %all-to-all-done.refs_0_, bf16[128,2048]{1,0:T(8,128)(2,1)S(1)} %delta.1.refs_0_.refs_1_, bf16[128,2048]{1,0:T(8,128)(2,1)S(1)} %copy-done.4, bf16[128,2048]{1,0:T(8,128)(2,1)S(1)} %copy-done.6, ...), custom_call_target="tpu_custom_call" | custom-call | flops 939524096 | bytes 6295552 | tf_op jit(solution)/shard_map/outer_near/pallas_call | solution.py:38
  111.4 1.9 %park.1 = (bf16[1,3,128,2048]{3,2,1,0:T(8,128)(2,1)}, f32[8,128]{1,0:T(8,128)S(1)}) custom-call(s32[16]{0:T(128)S(1)} %copy-done.14, bf16[1,3,128,2048]{3,2,1,0:T(8,128)(2,1)} %get-tuple-element.85.refs_1_, bf16[128,2048]{1,0:T(8,128)(2,1)} %collective-permute-done.25.refs_2_, f32[8,128]{1,0:T(8,128)S(1)} %get-tuple-element.86.refs_3_), custom_call_target="tpu_custom_call", output_to_operand_aliasing={{0}: (1, {})} | custom-call | bytes 3674176 | tf_op jit(solution)/shard_map/park/pallas_call | solution.py:38
  113.3 7.8 %collective-permute-done.10.refs_6_.refs_0_ = bf16[128,2048]{1,0:T(8,128)(2,1)} collective-permute-done((bf16[128,2048]{1,0:T(8,128)(2,1)}, bf16[128,2048]{1,0:T(8,128)(2,1)}, u32[]{:S(2)}, u32[]{:S(2)}) %collective-permute-start.10) | collective-permute-done | bytes 524320 | tf_op jit(solution)/shard_map/next_acts/ppermute | solution.py:58
  121.1 2.4 %outer_far.1 = (f32[128,2048]{1,0:T(8,128)S(1)}, bf16[128,2048]{1,0:T(8,128)(2,1)S(1)}, f32[8,128]{1,0:T(8,128)S(1)}) custom-call(bf16[4,2,2,128,128]{4,3,2,1,0:T(8,128)(2,1)S(1)} %all-to-all-done.refs_0_, bf16[64,2048]{1,0:T(8,128)(2,1)S(1)} %collective-permute-done.23.refs_1_, bf16[64,2048]{1,0:T(8,128)(2,1)} %collective-permute-done.24.refs_2_, ...), custom_call_target="tpu_custom_call" | custom-call | flops 134217728 | bytes 4722688 | tf_op jit(solution)/shard_map/outer_far/pallas_call | solution.py:38
  125.0 2.2 %emit.1 = (bf16[1,128,2048]{2,1,0:T(8,128)(2,1)}, bf16[1,128,2048]{2,1,0:T(8,128)(2,1)}, f32[8,128]{1,0:T(8,128)S(1)}) custom-call(bf16[128,2048]{1,0:T(8,128)(2,1)} %collective-permute-done.10.refs_6_.refs_0_, bf16[128,2048]{1,0:T(8,128)(2,1)} %collective-permute-done.16.refs_7_.refs_1_, f32[8,128]{1,0:T(8,128)S(1)} %get-tuple-element.88.refs_2_), custom_call_target="tpu_custom_call" | custom-call | bytes 2101248 | tf_op jit(solution)/shard_map/emit/pallas_call | solution.py:38
  (86 shorter events, 42.9 us)
Async XLA Ops:
  0.6 13.5 %collective-permute-start.1 = (bf16[128,2048]{1,0:T(8,128)(2,1)}, bf16[128,2048]{1,0:T(8,128)(2,1)S(1)}, u32[]{:S(2)}, u32[]{:S(2)}) collective-permute-start(bf16[128,2048]{1,0:T(8,128)(2,1)} %bitcast.3), channel_id=1, source_target_pairs={{0,4},{1,5},{2,6},{3,7},{4,8},{5,9},{6,10},{7,11},{8,12},{9,13},{1... | collective-permute-start | bytes 1572872 | tf_op jit(solution)/shard_map/weight/below/ppermute | solution.py:66
  2.8 12.4 %collective-permute-start.2 = (bf16[128,2048]{1,0:T(8,128)(2,1)}, bf16[128,2048]{1,0:T(8,128)(2,1)S(1)}, u32[]{:S(2)}, u32[]{:S(2)}) collective-permute-start(bf16[128,2048]{1,0:T(8,128)(2,1)} %bitcast.4), channel_id=1, source_target_pairs={{0,12},{1,13},{2,14},{3,15},{4,0},{5,1},{6,2},{7,3},{8,4},{9,5},{1... | collective-permute-start | bytes 1572872 | tf_op jit(solution)/shard_map/weight/above/ppermute | solution.py:66
  4.4 11.4 %collective-permute-start.3 = (bf16[128,2048]{1,0:T(8,128)(2,1)}, bf16[128,2048]{1,0:T(8,128)(2,1)S(1)}, u32[]{:S(2)}, u32[]{:S(2)}) collective-permute-start(bf16[128,2048]{1,0:T(8,128)(2,1)} %bitcast.5), channel_id=1, source_target_pairs={{0,2},{1,3},{2,0},{3,1},{4,6},{5,7},{6,4},{7,5},{8,10},{9,11},{10,... | collective-permute-start | bytes 1572872 | tf_op jit(solution)/shard_map/weight/pair/ppermute | solution.py:66
  15.9 17.2 %collective-permute-start.5 = (bf16[192,2048]{1,0:T(8,128)(2,1)S(1)}, bf16[192,2048]{1,0:T(8,128)(2,1)S(1)}, u32[]{:S(2)}, u32[]{:S(2)}) collective-permute-start(bf16[192,2048]{1,0:T(8,128)(2,1)S(1)} %get-tuple-element.56), channel_id=1, source_target_pairs={{0,4},{1,5},{2,6},{3,7},{4,8},{5,9},{6,10},{7,11},{8,12},{9,13},{1... | collective-permute-start | bytes 2359304 | tf_op jit(solution)/shard_map/weight/up/ppermute | solution.py:66
  17.1 16.7 %collective-permute-start.6 = (bf16[192,2048]{1,0:T(8,128)(2,1)S(1)}, bf16[192,2048]{1,0:T(8,128)(2,1)S(1)}, u32[]{:S(2)}, u32[]{:S(2)}) collective-permute-start(bf16[192,2048]{1,0:T(8,128)(2,1)S(1)} %get-tuple-element.57), channel_id=1, source_target_pairs={{0,12},{1,13},{2,14},{3,15},{4,0},{5,1},{6,2},{7,3},{8,4},{9,5},{1... | collective-permute-start | bytes 2359304 | tf_op jit(solution)/shard_map/weight/down/ppermute | solution.py:66
  18.7 32.3 %collective-permute-start.11 = (bf16[256,1024]{1,0:T(8,128)(2,1)S(1)}, bf16[256,1024]{1,0:T(8,128)(2,1)S(1)}, u32[]{:S(2)}, u32[]{:S(2)}) collective-permute-start(bf16[256,1024]{1,0:T(8,128)(2,1)S(1)} %join.1.refs_1_.refs_3_), channel_id=1, source_target_pairs={{0,240},{16,224},{32,208},{48,192},{64,176},{80,160},{96,144},{112... | collective-permute-start | bytes 1572872 | tf_op jit(solution)/shard_map/panel/ppermute | solution.py:53
  27.9 9.3 %collective-permute-start = (bf16[8,128,128]{2,1,0:T(8,128)(2,1)S(1)}, bf16[8,128,128]{2,1,0:T(8,128)(2,1)S(1)}, u32[]{:S(2)}, u32[]{:S(2)}) collective-permute-start(bf16[8,128,128]{2,1,0:T(8,128)(2,1)S(1)} %get-tuple-element.52), channel_id=1, source_target_pairs={{0,1},{1,0},{2,3},{3,2},{4,5},{5,4},{6,7},{7,6},{8,9},{9,8},{10,11... | collective-permute-start | bytes 786440 | tf_op jit(solution)/shard_map/acts/ppermute | solution.py:66
  34.4 6.8 %collective-permute-start.7 = (bf16[64,2048]{1,0:T(8,128)(2,1)S(1)}, bf16[64,2048]{1,0:T(8,128)(2,1)S(1)}, u32[]{:S(2)}, u32[]{:S(2)}) collective-permute-start(bf16[64,2048]{1,0:T(8,128)(2,1)S(1)} %get-tuple-element.58), channel_id=1, source_target_pairs={{0,4},{1,5},{2,6},{3,7},{4,8},{5,9},{6,10},{7,11},{8,12},{9,13},{1... | collective-permute-start | bytes 786440 | tf_op jit(solution)/shard_map/weight/far_up/ppermute | solution.py:66
  35.6 5.7 %collective-permute-start.8 = (bf16[64,2048]{1,0:T(8,128)(2,1)S(1)}, bf16[64,2048]{1,0:T(8,128)(2,1)S(1)}, u32[]{:S(2)}, u32[]{:S(2)}) collective-permute-start(bf16[64,2048]{1,0:T(8,128)(2,1)S(1)} %get-tuple-element.59), channel_id=1, source_target_pairs={{0,12},{1,13},{2,14},{3,15},{4,0},{5,1},{6,2},{7,3},{8,4},{9,5},{1... | collective-permute-start | bytes 786440 | tf_op jit(solution)/shard_map/weight/far_down/ppermute | solution.py:66
  59.5 4.7 %collective-permute-start.9 = (bf16[128,2048]{1,0:T(8,128)(2,1)S(1)}, bf16[128,2048]{1,0:T(8,128)(2,1)S(1)}, u32[]{:S(2)}, u32[]{:S(2)}) collective-permute-start(bf16[128,2048]{1,0:T(8,128)(2,1)S(1)} %get-tuple-element.63), channel_id=1, source_target_pairs={{0,1},{1,0},{2,3},{3,2},{4,5},{5,4},{6,7},{7,6},{8,9},{9,8},{10,11... | collective-permute-start | bytes 1572872 | tf_op jit(solution)/shard_map/pre_acts/ppermute | solution.py:66
  60.9 5.4 %collective-permute-start.14 = (bf16[128,2048]{1,0:T(8,128)(2,1)S(1)}, bf16[128,2048]{1,0:T(8,128)(2,1)S(1)}, u32[]{:S(2)}, u32[]{:S(2)}) collective-permute-start(bf16[128,2048]{1,0:T(8,128)(2,1)S(1)} %delta.1.refs_0_.refs_1_), channel_id=1, source_target_pairs={{0,1},{1,0},{2,3},{3,2},{4,5},{5,4},{6,7},{7,6},{8,9},{9,8},{10,11... | collective-permute-start | bytes 1572872 | tf_op jit(solution)/shard_map/delta_other/ppermute | solution.py:66
  61.2 14.3 %collective-permute-start.18 = (bf16[128,2048]{1,0:T(8,128)(2,1)S(1)}, bf16[128,2048]{1,0:T(8,128)(2,1)S(1)}, u32[]{:S(2)}, u32[]{:S(2)}) collective-permute-start(bf16[128,2048]{1,0:T(8,128)(2,1)S(1)} %delta.1.refs_0_.refs_1_), channel_id=1, source_target_pairs={{0,4},{1,5},{2,6},{3,7},{4,8},{5,9},{6,10},{7,11},{8,12},{9,13},{1... | collective-permute-start | bytes 1572872 | tf_op jit(solution)/shard_map/delta/below/ppermute | solution.py:66
  61.2 14.3 %collective-permute-start.19 = (bf16[128,2048]{1,0:T(8,128)(2,1)S(1)}, bf16[128,2048]{1,0:T(8,128)(2,1)S(1)}, u32[]{:S(2)}, u32[]{:S(2)}) collective-permute-start(bf16[128,2048]{1,0:T(8,128)(2,1)S(1)} %delta.1.refs_0_.refs_1_), channel_id=1, source_target_pairs={{0,12},{1,13},{2,14},{3,15},{4,0},{5,1},{6,2},{7,3},{8,4},{9,5},{1... | collective-permute-start | bytes 1572872 | tf_op jit(solution)/shard_map/delta/above/ppermute | solution.py:66
  63.8 12.5 %collective-permute-start.20 = (bf16[128,2048]{1,0:T(8,128)(2,1)S(1)}, bf16[128,2048]{1,0:T(8,128)(2,1)S(1)}, u32[]{:S(2)}, u32[]{:S(2)}) collective-permute-start(bf16[128,2048]{1,0:T(8,128)(2,1)S(1)} %delta.1.refs_0_.refs_1_), channel_id=1, source_target_pairs={{0,2},{1,3},{2,0},{3,1},{4,6},{5,7},{6,4},{7,5},{8,10},{9,11},{10,... | collective-permute-start | bytes 1572872 | tf_op jit(solution)/shard_map/delta/pair/ppermute | solution.py:66
  67.6 19.2 %collective-permute-start.15 = (f32[8,128,128]{2,1,0:T(8,128)S(1)}, f32[8,128,128]{2,1,0:T(8,128)S(1)}, u32[]{:S(2)}, u32[]{:S(2)}) collective-permute-start(f32[8,128,128]{2,1,0:T(8,128)S(1)} %get-tuple-element.73), channel_id=1, source_target_pairs={{0,1},{1,0},{2,3},{3,2},{4,5},{5,4},{6,7},{7,6},{8,9},{9,8},{10,11... | collective-permute-start | bytes 1572872 | tf_op jit(solution)/shard_map/back/ppermute | solution.py:66
  77.7 20.6 %collective-permute-start.21 = (bf16[192,2048]{1,0:T(8,128)(2,1)}, bf16[192,2048]{1,0:T(8,128)(2,1)S(1)}, u32[]{:S(2)}, u32[]{:S(2)}) collective-permute-start(bf16[192,2048]{1,0:T(8,128)(2,1)} %get-tuple-element.78), channel_id=1, source_target_pairs={{0,4},{1,5},{2,6},{3,7},{4,8},{5,9},{6,10},{7,11},{8,12},{9,13},{1... | collective-permute-start | bytes 2359304 | tf_op jit(solution)/shard_map/delta/up/ppermute | solution.py:66
  77.8 20.6 %collective-permute-start.22 = (bf16[192,2048]{1,0:T(8,128)(2,1)}, bf16[192,2048]{1,0:T(8,128)(2,1)S(1)}, u32[]{:S(2)}, u32[]{:S(2)}) collective-permute-start(bf16[192,2048]{1,0:T(8,128)(2,1)} %get-tuple-element.79), channel_id=1, source_target_pairs={{0,12},{1,13},{2,14},{3,15},{4,0},{5,1},{6,2},{7,3},{8,4},{9,5},{1... | collective-permute-start | bytes 2359304 | tf_op jit(solution)/shard_map/delta/down/ppermute | solution.py:66
  80.5 9.8 %collective-permute-start.17 = (bf16[4,2,128,128]{3,2,1,0:T(8,128)(2,1)S(1)}, bf16[4,2,128,128]{3,2,1,0:T(8,128)(2,1)S(1)}, u32[]{:S(2)}, u32[]{:S(2)}) collective-permute-start(bf16[4,2,128,128]{3,2,1,0:T(8,128)(2,1)S(1)} %get-tuple-element.75), channel_id=1, source_target_pairs={{0,2},{1,3},{2,0},{3,1},{4,6},{5,7},{6,4},{7,5},{8,10},{9,11},{10,... | collective-permute-start | bytes 786440 | tf_op jit(solution)/shard_map/pair_units/ppermute | solution.py:66
  80.8 30.6 %collective-permute-start.25 = (bf16[128,2048]{1,0:T(8,128)(2,1)}, bf16[128,2048]{1,0:T(8,128)(2,1)}, u32[]{:S(2)}, u32[]{:S(2)}) collective-permute-start(bf16[128,2048]{1,0:T(8,128)(2,1)} %bitcast.refs_0_.refs_2_), channel_id=1, source_target_pairs={{0,240},{16,224},{32,208},{48,192},{64,176},{80,160},{96,144},{112... | collective-permute-start | bytes 1572872 | tf_op jit(solution)/shard_map/stash/ppermute | solution.py:53
  86.8 34.3 %collective-permute-start.10 = (bf16[128,2048]{1,0:T(8,128)(2,1)}, bf16[128,2048]{1,0:T(8,128)(2,1)}, u32[]{:S(2)}, u32[]{:S(2)}) collective-permute-start(bf16[128,2048]{1,0:T(8,128)(2,1)} %get-tuple-element.64), channel_id=1, source_target_pairs={{240,0},{0,16},{16,32},{32,48},{48,64},{64,80},{80,96},{96,112},{1... | collective-permute-start | bytes 1572872 | tf_op jit(solution)/shard_map/next_acts/ppermute | solution.py:58
  90.3 30.7 %collective-permute-start.16 = (bf16[128,2048]{1,0:T(8,128)(2,1)}, bf16[128,2048]{1,0:T(8,128)(2,1)}, u32[]{:S(2)}, u32[]{:S(2)}) collective-permute-start(bf16[128,2048]{1,0:T(8,128)(2,1)} %get-tuple-element.74), channel_id=1, source_target_pairs={{16,0},{32,16},{48,32},{64,48},{80,64},{96,80},{112,96},{128,112},... | collective-permute-start | bytes 1572872 | tf_op jit(solution)/shard_map/next_grads/ppermute | solution.py:58
  94.9 10.8 %all-to-all-start = ((bf16[4,2,2,128,128]{4,3,2,1,0:T(8,128)(2,1)}), bf16[4,2,2,128,128]{4,3,2,1,0:T(8,128)(2,1)S(1)}, u32[]{:S(2)}, u32[]{:S(2)}) async-start(bf16[4,2,2,128,128]{4,3,2,1,0:T(8,128)(2,1)} %copy-done.10), calls=%async_computation | async-start | bytes 1048576 | tf_op jit(solution)/shard_map/all_to_all | solution.py:502
  99.2 21.8 %collective-permute-start.23 = (bf16[64,2048]{1,0:T(8,128)(2,1)}, bf16[64,2048]{1,0:T(8,128)(2,1)S(1)}, u32[]{:S(2)}, u32[]{:S(2)}) collective-permute-start(bf16[64,2048]{1,0:T(8,128)(2,1)} %get-tuple-element.80), channel_id=1, source_target_pairs={{0,4},{1,5},{2,6},{3,7},{4,8},{5,9},{6,10},{7,11},{8,12},{9,13},{1... | collective-permute-start | bytes 786440 | tf_op jit(solution)/shard_map/delta/far_up/ppermute | solution.py:66
  100.7 20.3 %collective-permute-start.24 = (bf16[64,2048]{1,0:T(8,128)(2,1)}, bf16[64,2048]{1,0:T(8,128)(2,1)}, u32[]{:S(2)}, u32[]{:S(2)}) collective-permute-start(bf16[64,2048]{1,0:T(8,128)(2,1)} %get-tuple-element.81), channel_id=1, source_target_pairs={{0,12},{1,13},{2,14},{3,15},{4,0},{5,1},{6,2},{7,3},{8,4},{9,5},{1... | collective-permute-start | bytes 786440 | tf_op jit(solution)/shard_map/delta/far_down/ppermute | solution.py:66
  (19 other events, 107.9 us)

commit v4 on v3

--- a/solution.py
+++ b/solution.py
@@ -281,19 +281,12 @@
         out_other[:, columns] = high.astype(out_other.dtype)
 
     if kind == "panel":
-        if added:
-            squares = totals[1][:, WIDTH:]
-            rounded = squares.astype(BF16)
-            out_own[:, WIDTH:] = totals[0][:, WIDTH:]
-            out_other[:, WIDTH : WIDTH + BLOCK] = rounded
-            out_other[:, WIDTH + BLOCK :] = (squares - rounded.astype(F32)).astype(BF16)
-        else:
-            values = first_ref[...].astype(F32)
-            squares = jnp.broadcast_to(
-                jnp.sum(values * values, -1, keepdims=True), (2 * BLOCK, BLOCK)
-            )
-            out_own[:, WIDTH:] = squares[:BLOCK]
-            out_other[:, WIDTH:] = squares[BLOCK:]
+        values = first_ref[...].astype(F32)
+        squares = jnp.broadcast_to(jnp.sum(values * values, -1, keepdims=True), (2 * BLOCK, BLOCK))
+        out_own[:, WIDTH:] = squares[:BLOCK]
+        rounded = squares[BLOCK:].astype(BF16)
+        out_other[:, WIDTH : WIDTH + BLOCK] = rounded
+        out_other[:, WIDTH + BLOCK :] = (squares[BLOCK:] - rounded.astype(F32)).astype(BF16)
 
 
 def product(name, kind, blocks, chunks, totals=(), after=()):
@@ -305,7 +298,7 @@
     return call(
         name,
         functools.partial(product_kernel, layout, kind, bool(totals)),
-        [out, last if totals else out, struct((8, BLOCK), F32)],
+        [out, last if totals or kind == "panel" else out, struct((8, BLOCK), F32)],
         args,
         [VMEM] * len(args),
         scratch=[pltpu.VMEM((2 * BLOCK, depth), BF16)],
@@ -457,10 +450,9 @@
     )
 
     backward = [panel_half, gain]
-    *panel_pre, _ = product(
-        "backward_near", "panel", backward, near + middle, after=[forward_token]
-    )
-    panel_own, panel_other, _ = product("backward_far", "panel", backward, far, panel_pre)
+    panel_own, panel_other, _ = product(
+        "backward", "panel", backward, near + middle + far, after=[forward_token]
+    )
     with jax.named_scope("pre_acts"):
         received = hop(pre_other, core=1)
     out_rows, out_token = call(

time: 129 us -> 127 us (0.984)
  Pallas kernels: 32.9 us -> 31.3 us
    pallas_call x23 -> x22, Pallas kernels: 32.9 us -> 31.3 us  [call(): pl.pallas_call(body, out_shape=list(outs), in_specs=list(specs) + [ANY] *...]
where the time goes in v4:
time: 127 us
  starting transfers between devices  52.2 us (41%)
  waiting for transfers between devices  35.6 us (28%)
  Pallas kernels  31.3 us (25%)
  local copies, waits for them, and re-layouts  6.73 us (5%)
    pallas_call x22, Pallas kernels, call(): pl.pallas_call(body, out_shape=list(outs), in_specs=list(specs) + [ANY] *...  31.3 us
    ppermute x23, starting transfers between devices, hop(): return lax.ppermute(block, 'dp', route)  28.4 us
    ppermute x23, waiting for transfers between devices, hop(): return lax.ppermute(block, 'dp', route)  16.5 us
    ppermute x2, starting transfers between devices, mirrored(): lax.ppermute(block, 'section', [(i, count - 1 - i) for i in range(count)])  15.2 us
    ppermute x2, waiting for transfers between devices, shifted(): lax.ppermute(block, 'section', [((i - distance) % count, i) for i in rang...  7.75 us
    ppermute x2, waiting for transfers between devices, mirrored(): lax.ppermute(block, 'section', [(i, count - 1 - i) for i in range(count)])  7.73 us
    unnamed x30, local copies, waits for them, and re-layouts  6.71 us
    ppermute x2, starting transfers between devices, shifted(): lax.ppermute(block, 'section', [((i - distance) % count, i) for i in rang...  5.16 us
  transfers between devices with their start and end apart: 28, of which 12 were waited for; matrix products, arithmetic and copies ran while one was open for 0% of the time, Pallas kernels for 19%

profile of v4, /device:TPU:1, one launch (start us, length us, event | category | flops | bytes accessed | tf_op | source)
XLA Modules:
  0.0 126.8 jit_solution(2689115944201923610)
XLA Ops:
  0.6 2.2 %collective-permute-start.1 = (bf16[128,2048]{1,0:T(8,128)(2,1)}, bf16[128,2048]{1,0:T(8,128)(2,1)S(1)}, u32[]{:S(2)}, u32[]{:S(2)}) collective-permute-start(bf16[128,2048]{1,0:T(8,128)(2,1)} %bitcast.3), channel_id=1, source_target_pairs={{0,4},{1,5},{2,6},{3,7},{4,8},{5,9},{6,10},{7,11},{8,12},{9,13},{1... | collective-permute-start | bytes 1572872 | tf_op jit(solution)/shard_map/weight/below/ppermute | solution.py:66
  18.7 9.2 %collective-permute-start.11 = (bf16[256,1024]{1,0:T(8,128)(2,1)S(1)}, bf16[256,1024]{1,0:T(8,128)(2,1)S(1)}, u32[]{:S(2)}, u32[]{:S(2)}) collective-permute-start(bf16[256,1024]{1,0:T(8,128)(2,1)S(1)} %join.1.refs_1_.refs_3_), channel_id=1, source_target_pairs={{0,240},{16,224},{32,208},{48,192},{64,176},{80,160},{96,144},{112... | collective-permute-start | bytes 1572872 | tf_op jit(solution)/shard_map/panel/ppermute | solution.py:53
  27.9 2.8 %collective-permute-start = (bf16[8,128,128]{2,1,0:T(8,128)(2,1)S(1)}, bf16[8,128,128]{2,1,0:T(8,128)(2,1)S(1)}, u32[]{:S(2)}, u32[]{:S(2)}) collective-permute-start(bf16[8,128,128]{2,1,0:T(8,128)(2,1)S(1)} %get-tuple-element.50), channel_id=1, source_target_pairs={{0,1},{1,0},{2,3},{3,2},{4,5},{5,4},{6,7},{7,6},{8,9},{9,8},{10,11... | collective-permute-start | bytes 786440 | tf_op jit(solution)/shard_map/acts/ppermute | solution.py:66
  30.7 2.4 %collective-permute-done.5.refs_0_.refs_2_.refs_6_ = bf16[192,2048]{1,0:T(8,128)(2,1)S(1)} collective-permute-done((bf16[192,2048]{1,0:T(8,128)(2,1)S(1)}, bf16[192,2048]{1,0:T(8,128)(2,1)S(1)}, u32[]{:S(2)}, u32[]{:S(2)}) %collective-permute-start.5) | collective-permute-done | bytes 786464 | tf_op jit(solution)/shard_map/weight/up/ppermute | solution.py:66
  37.2 2.3 %forward_near.1 = (f32[128,2048]{1,0:T(8,128)S(1)}, f32[128,2048]{1,0:T(8,128)S(1)}, f32[8,128]{1,0:T(8,128)}) custom-call(bf16[8,128,128]{2,1,0:T(8,128)(2,1)S(1)} %get-tuple-element.49.refs_4_.refs_0_, bf16[8,128,128]{2,1,0:T(8,128)(2,1)S(1)} %collective-permute-done.refs_1_, bf16[128,2048]{1,0:T(8,128)(2,1)S(1)} %bitcast.6, ...), custom_call_target="tpu_custom_call" | custom-call | flops 536870912 | bytes 4722688 | tf_op jit(solution)/shard_map/forward_near/pallas_call | solution.py:38
  39.5 1.7 %collective-permute-done.7.refs_4_.refs_8_ = bf16[64,2048]{1,0:T(8,128)(2,1)S(1)} collective-permute-done((bf16[64,2048]{1,0:T(8,128)(2,1)S(1)}, bf16[64,2048]{1,0:T(8,128)(2,1)S(1)}, u32[]{:S(2)}, u32[]{:S(2)}) %collective-permute-start.7) | collective-permute-done | bytes 262176 | tf_op jit(solution)/shard_map/weight/far_up/ppermute | solution.py:66
  41.2 2.0 %forward_far.1 = (f32[128,2048]{1,0:T(8,128)S(1)}, bf16[128,2048]{1,0:T(8,128)(2,1)S(1)}, f32[8,128]{1,0:T(8,128)S(1)}) custom-call(bf16[8,128,128]{2,1,0:T(8,128)(2,1)S(1)} %get-tuple-element.49.refs_4_.refs_0_, bf16[8,128,128]{2,1,0:T(8,128)(2,1)S(1)} %collective-permute-done.refs_1_, bf16[192,2048]{1,0:T(8,128)(2,1)S(1)} %collective-permute-done.5.refs_0_.refs_2_.refs_6_, ...), custom_call_target="tpu_custom_call" | custom-call | flops 536870912 | bytes 6295552 | tf_op jit(solution)/shard_map/forward_far/pallas_call | solution.py:38
  43.2 7.7 %collective-permute-done.11.refs_0_ = bf16[256,1024]{1,0:T(8,128)(2,1)S(1)} collective-permute-done((bf16[256,1024]{1,0:T(8,128)(2,1)S(1)}, bf16[256,1024]{1,0:T(8,128)(2,1)S(1)}, u32[]{:S(2)}, u32[]{:S(2)}) %collective-permute-start.11) | collective-permute-done | bytes 524320 | tf_op jit(solution)/shard_map/panel/ppermute | solution.py:53
  51.0 3.4 %backward.1 = (f32[128,2176]{1,0:T(8,128)S(1)}, bf16[128,2304]{1,0:T(8,128)(2,1)S(1)}, f32[8,128]{1,0:T(8,128)}) custom-call(bf16[256,1024]{1,0:T(8,128)(2,1)S(1)} %collective-permute-done.11.refs_0_, f32[1,2048]{1,0:T(1,128)S(1)} %copy-done.12, bf16[128,2048]{1,0:T(8,128)(2,1)S(1)} %bitcast.7, bf16[128,2048]{1,0:T(8,128)(2,1)S(1)} %collective-permute-done.1.refs_0_.refs_3_, ...), custom_call_target="tpu_custom_call" | custom-call | flops 1140850688 | bytes 6434816 | tf_op jit(solution)/shard_map/backward/pallas_call | solution.py:38
  55.5 1.9 %collective-permute-done.12.refs_1_ = bf16[128,1024]{1,0:T(8,128)(2,1)S(1)} collective-permute-done((bf16[128,1024]{1,0:T(8,128)(2,1)S(1)}, bf16[128,1024]{1,0:T(8,128)(2,1)S(1)}, u32[]{:S(2)}, u32[]{:S(2)}) %collective-permute-start.12) | collective-permute-done | bytes 262176 | tf_op jit(solution)/shard_map/restore/ppermute | solution.py:66
  59.5 2.7 %collective-permute-start.19 = (bf16[128,2048]{1,0:T(8,128)(2,1)S(1)}, bf16[128,2048]{1,0:T(8,128)(2,1)S(1)}, u32[]{:S(2)}, u32[]{:S(2)}) collective-permute-start(bf16[128,2048]{1,0:T(8,128)(2,1)S(1)} %delta.1.refs_0_.refs_1_), channel_id=1, source_target_pairs={{0,12},{1,13},{2,14},{3,15},{4,0},{5,1},{6,2},{7,3},{8,4},{9,5},{1... | collective-permute-start | bytes 1572872 | tf_op jit(solution)/shard_map/delta/above/ppermute | solution.py:66
  62.5 2.2 %out.1 = (bf16[128,2048]{1,0:T(8,128)(2,1)}, f32[8,128]{1,0:T(8,128)S(1)}) custom-call(f32[128,2048]{1,0:T(8,128)S(1)} %get-tuple-element.60.refs_0_, bf16[128,2048]{1,0:T(8,128)(2,1)S(1)} %collective-permute-done.9.refs_1_, bf16[128,2048]{1,0:T(8,128)(2,1)} %bitcast.refs_0_.refs_2_), custom_call_target="tpu_custom_call" | custom-call | bytes 2625536 | tf_op jit(solution)/shard_map/out/pallas_call | solution.py:38
  67.3 6.6 %collective-permute-done.18.refs_0_.refs_2_ = bf16[128,2048]{1,0:T(8,128)(2,1)S(1)} collective-permute-done((bf16[128,2048]{1,0:T(8,128)(2,1)S(1)}, bf16[128,2048]{1,0:T(8,128)(2,1)S(1)}, u32[]{:S(2)}, u32[]{:S(2)}) %collective-permute-start.18) | collective-permute-done | bytes 524320 | tf_op jit(solution)/shard_map/delta/below/ppermute | solution.py:66
  76.2 2.7 %collective-permute-start.22 = (bf16[192,2048]{1,0:T(8,128)(2,1)}, bf16[192,2048]{1,0:T(8,128)(2,1)S(1)}, u32[]{:S(2)}, u32[]{:S(2)}) collective-permute-start(bf16[192,2048]{1,0:T(8,128)(2,1)} %get-tuple-element.75), channel_id=1, source_target_pairs={{0,12},{1,13},{2,14},{3,15},{4,0},{5,1},{6,2},{7,3},{8,4},{9,5},{1... | collective-permute-start | bytes 2359304 | tf_op jit(solution)/shard_map/delta/down/ppermute | solution.py:66
  79.2 6.0 %collective-permute-start.25 = (bf16[128,2048]{1,0:T(8,128)(2,1)}, bf16[128,2048]{1,0:T(8,128)(2,1)}, u32[]{:S(2)}, u32[]{:S(2)}) collective-permute-start(bf16[128,2048]{1,0:T(8,128)(2,1)} %bitcast.refs_0_.refs_2_), channel_id=1, source_target_pairs={{0,240},{16,224},{32,208},{48,192},{64,176},{80,160},{96,144},{112... | collective-permute-start | bytes 1572872 | tf_op jit(solution)/shard_map/stash/ppermute | solution.py:53
  85.2 2.0 %collective-permute-start.10 = (bf16[128,2048]{1,0:T(8,128)(2,1)}, bf16[128,2048]{1,0:T(8,128)(2,1)}, u32[]{:S(2)}, u32[]{:S(2)}) collective-permute-start(bf16[128,2048]{1,0:T(8,128)(2,1)} %get-tuple-element.62), channel_id=1, source_target_pairs={{240,0},{0,16},{16,32},{32,48},{48,64},{64,80},{80,96},{96,112},{1... | collective-permute-start | bytes 1572872 | tf_op jit(solution)/shard_map/next_acts/ppermute | solution.py:58
  88.7 3.1 %collective-permute-start.16 = (bf16[128,2048]{1,0:T(8,128)(2,1)}, bf16[128,2048]{1,0:T(8,128)(2,1)}, u32[]{:S(2)}, u32[]{:S(2)}) collective-permute-start(bf16[128,2048]{1,0:T(8,128)(2,1)} %get-tuple-element.70), channel_id=1, source_target_pairs={{16,0},{32,16},{48,32},{64,48},{80,64},{96,80},{112,96},{128,112},... | collective-permute-start | bytes 1572872 | tf_op jit(solution)/shard_map/next_grads/ppermute | solution.py:58
  93.3 3.5 %all-to-all-start = ((bf16[4,2,2,128,128]{4,3,2,1,0:T(8,128)(2,1)}), bf16[4,2,2,128,128]{4,3,2,1,0:T(8,128)(2,1)S(1)}, u32[]{:S(2)}, u32[]{:S(2)}) async-start(bf16[4,2,2,128,128]{4,3,2,1,0:T(8,128)(2,1)} %copy-done.10), calls=%async_computation | async-start | bytes 1048576 | tf_op jit(solution)/shard_map/all_to_all | solution.py:494
  100.4 3.7 %all-to-all-done.refs_0_ = bf16[4,2,2,128,128]{4,3,2,1,0:T(8,128)(2,1)S(1)} async-done(((bf16[4,2,2,128,128]{4,3,2,1,0:T(8,128)(2,1)}), bf16[4,2,2,128,128]{4,3,2,1,0:T(8,128)(2,1)S(1)}, u32[]{:S(2)}, u32[]{:S(2)}) %all-to-all-start) | async-done | bytes 524320 | tf_op jit(solution)/shard_map/all_to_all | solution.py:494
  107.2 2.6 %outer_near.1 = (f32[128,2048]{1,0:T(8,128)S(1)}, f32[128,2048]{1,0:T(8,128)S(1)}, f32[8,128]{1,0:T(8,128)S(1)}) custom-call(bf16[4,2,2,128,128]{4,3,2,1,0:T(8,128)(2,1)S(1)} %all-to-all-done.refs_0_, bf16[128,2048]{1,0:T(8,128)(2,1)S(1)} %delta.1.refs_0_.refs_1_, bf16[128,2048]{1,0:T(8,128)(2,1)S(1)} %copy-done.4, bf16[128,2048]{1,0:T(8,128)(2,1)S(1)} %copy-done.6, ...), custom_call_target="tpu_custom_call" | custom-call | flops 939524096 | bytes 6295552 | tf_op jit(solution)/shard_map/outer_near/pallas_call | solution.py:38
  109.8 1.9 %park.1 = (bf16[1,3,128,2048]{3,2,1,0:T(8,128)(2,1)}, f32[8,128]{1,0:T(8,128)S(1)}) custom-call(s32[16]{0:T(128)S(1)} %copy-done.14, bf16[1,3,128,2048]{3,2,1,0:T(8,128)(2,1)} %get-tuple-element.81.refs_1_, bf16[128,2048]{1,0:T(8,128)(2,1)} %collective-permute-done.25.refs_2_, f32[8,128]{1,0:T(8,128)S(1)} %get-tuple-element.82.refs_3_), custom_call_target="tpu_custom_call", output_to_operand_aliasing={{0}: (1, {})} | custom-call | bytes 3674176 | tf_op jit(solution)/shard_map/park/pallas_call | solution.py:38
  111.7 7.7 %collective-permute-done.10.refs_6_.refs_0_ = bf16[128,2048]{1,0:T(8,128)(2,1)} collective-permute-done((bf16[128,2048]{1,0:T(8,128)(2,1)}, bf16[128,2048]{1,0:T(8,128)(2,1)}, u32[]{:S(2)}, u32[]{:S(2)}) %collective-permute-start.10) | collective-permute-done | bytes 524320 | tf_op jit(solution)/shard_map/next_acts/ppermute | solution.py:58
  119.5 2.4 %outer_far.1 = (f32[128,2048]{1,0:T(8,128)S(1)}, bf16[128,2048]{1,0:T(8,128)(2,1)S(1)}, f32[8,128]{1,0:T(8,128)S(1)}) custom-call(bf16[4,2,2,128,128]{4,3,2,1,0:T(8,128)(2,1)S(1)} %all-to-all-done.refs_0_, bf16[64,2048]{1,0:T(8,128)(2,1)S(1)} %collective-permute-done.23.refs_1_, bf16[64,2048]{1,0:T(8,128)(2,1)} %collective-permute-done.24.refs_2_, ...), custom_call_target="tpu_custom_call" | custom-call | flops 134217728 | bytes 4722688 | tf_op jit(solution)/shard_map/outer_far/pallas_call | solution.py:38
  123.3 2.2 %emit.1 = (bf16[1,128,2048]{2,1,0:T(8,128)(2,1)}, bf16[1,128,2048]{2,1,0:T(8,128)(2,1)}, f32[8,128]{1,0:T(8,128)S(1)}) custom-call(bf16[128,2048]{1,0:T(8,128)(2,1)} %collective-permute-done.10.refs_6_.refs_0_, bf16[128,2048]{1,0:T(8,128)(2,1)} %collective-permute-done.16.refs_7_.refs_1_, f32[8,128]{1,0:T(8,128)S(1)} %get-tuple-element.84.refs_2_), custom_call_target="tpu_custom_call" | custom-call | bytes 2101248 | tf_op jit(solution)/shard_map/emit/pallas_call | solution.py:38
  (85 shorter events, 41.2 us)
Async XLA Ops:
  0.6 13.5 %collective-permute-start.1 = (bf16[128,2048]{1,0:T(8,128)(2,1)}, bf16[128,2048]{1,0:T(8,128)(2,1)S(1)}, u32[]{:S(2)}, u32[]{:S(2)}) collective-permute-start(bf16[128,2048]{1,0:T(8,128)(2,1)} %bitcast.3), channel_id=1, source_target_pairs={{0,4},{1,5},{2,6},{3,7},{4,8},{5,9},{6,10},{7,11},{8,12},{9,13},{1... | collective-permute-start | bytes 1572872 | tf_op jit(solution)/shard_map/weight/below/ppermute | solution.py:66
  2.8 12.4 %collective-permute-start.2 = (bf16[128,2048]{1,0:T(8,128)(2,1)}, bf16[128,2048]{1,0:T(8,128)(2,1)S(1)}, u32[]{:S(2)}, u32[]{:S(2)}) collective-permute-start(bf16[128,2048]{1,0:T(8,128)(2,1)} %bitcast.4), channel_id=1, source_target_pairs={{0,12},{1,13},{2,14},{3,15},{4,0},{5,1},{6,2},{7,3},{8,4},{9,5},{1... | collective-permute-start | bytes 1572872 | tf_op jit(solution)/shard_map/weight/above/ppermute | solution.py:66
  4.4 11.4 %collective-permute-start.3 = (bf16[128,2048]{1,0:T(8,128)(2,1)}, bf16[128,2048]{1,0:T(8,128)(2,1)S(1)}, u32[]{:S(2)}, u32[]{:S(2)}) collective-permute-start(bf16[128,2048]{1,0:T(8,128)(2,1)} %bitcast.5), channel_id=1, source_target_pairs={{0,2},{1,3},{2,0},{3,1},{4,6},{5,7},{6,4},{7,5},{8,10},{9,11},{10,... | collective-permute-start | bytes 1572872 | tf_op jit(solution)/shard_map/weight/pair/ppermute | solution.py:66
  15.9 17.2 %collective-permute-start.5 = (bf16[192,2048]{1,0:T(8,128)(2,1)S(1)}, bf16[192,2048]{1,0:T(8,128)(2,1)S(1)}, u32[]{:S(2)}, u32[]{:S(2)}) collective-permute-start(bf16[192,2048]{1,0:T(8,128)(2,1)S(1)} %get-tuple-element.54), channel_id=1, source_target_pairs={{0,4},{1,5},{2,6},{3,7},{4,8},{5,9},{6,10},{7,11},{8,12},{9,13},{1... | collective-permute-start | bytes 2359304 | tf_op jit(solution)/shard_map/weight/up/ppermute | solution.py:66
  17.1 16.7 %collective-permute-start.6 = (bf16[192,2048]{1,0:T(8,128)(2,1)S(1)}, bf16[192,2048]{1,0:T(8,128)(2,1)S(1)}, u32[]{:S(2)}, u32[]{:S(2)}) collective-permute-start(bf16[192,2048]{1,0:T(8,128)(2,1)S(1)} %get-tuple-element.55), channel_id=1, source_target_pairs={{0,12},{1,13},{2,14},{3,15},{4,0},{5,1},{6,2},{7,3},{8,4},{9,5},{1... | collective-permute-start | bytes 2359304 | tf_op jit(solution)/shard_map/weight/down/ppermute | solution.py:66
  18.7 32.3 %collective-permute-start.11 = (bf16[256,1024]{1,0:T(8,128)(2,1)S(1)}, bf16[256,1024]{1,0:T(8,128)(2,1)S(1)}, u32[]{:S(2)}, u32[]{:S(2)}) collective-permute-start(bf16[256,1024]{1,0:T(8,128)(2,1)S(1)} %join.1.refs_1_.refs_3_), channel_id=1, source_target_pairs={{0,240},{16,224},{32,208},{48,192},{64,176},{80,160},{96,144},{112... | collective-permute-start | bytes 1572872 | tf_op jit(solution)/shard_map/panel/ppermute | solution.py:53
  27.9 9.3 %collective-permute-start = (bf16[8,128,128]{2,1,0:T(8,128)(2,1)S(1)}, bf16[8,128,128]{2,1,0:T(8,128)(2,1)S(1)}, u32[]{:S(2)}, u32[]{:S(2)}) collective-permute-start(bf16[8,128,128]{2,1,0:T(8,128)(2,1)S(1)} %get-tuple-element.50), channel_id=1, source_target_pairs={{0,1},{1,0},{2,3},{3,2},{4,5},{5,4},{6,7},{7,6},{8,9},{9,8},{10,11... | collective-permute-start | bytes 786440 | tf_op jit(solution)/shard_map/acts/ppermute | solution.py:66
  34.4 6.8 %collective-permute-start.7 = (bf16[64,2048]{1,0:T(8,128)(2,1)S(1)}, bf16[64,2048]{1,0:T(8,128)(2,1)S(1)}, u32[]{:S(2)}, u32[]{:S(2)}) collective-permute-start(bf16[64,2048]{1,0:T(8,128)(2,1)S(1)} %get-tuple-element.56), channel_id=1, source_target_pairs={{0,4},{1,5},{2,6},{3,7},{4,8},{5,9},{6,10},{7,11},{8,12},{9,13},{1... | collective-permute-start | bytes 786440 | tf_op jit(solution)/shard_map/weight/far_up/ppermute | solution.py:66
  35.6 5.7 %collective-permute-start.8 = (bf16[64,2048]{1,0:T(8,128)(2,1)S(1)}, bf16[64,2048]{1,0:T(8,128)(2,1)S(1)}, u32[]{:S(2)}, u32[]{:S(2)}) collective-permute-start(bf16[64,2048]{1,0:T(8,128)(2,1)S(1)} %get-tuple-element.57), channel_id=1, source_target_pairs={{0,12},{1,13},{2,14},{3,15},{4,0},{5,1},{6,2},{7,3},{8,4},{9,5},{1... | collective-permute-start | bytes 786440 | tf_op jit(solution)/shard_map/weight/far_down/ppermute | solution.py:66
  57.8 4.7 %collective-permute-start.9 = (bf16[128,2048]{1,0:T(8,128)(2,1)S(1)}, bf16[128,2048]{1,0:T(8,128)(2,1)S(1)}, u32[]{:S(2)}, u32[]{:S(2)}) collective-permute-start(bf16[128,2048]{1,0:T(8,128)(2,1)S(1)} %get-tuple-element.61), channel_id=1, source_target_pairs={{0,1},{1,0},{2,3},{3,2},{4,5},{5,4},{6,7},{7,6},{8,9},{9,8},{10,11... | collective-permute-start | bytes 1572872 | tf_op jit(solution)/shard_map/pre_acts/ppermute | solution.py:66
  59.3 5.4 %collective-permute-start.14 = (bf16[128,2048]{1,0:T(8,128)(2,1)S(1)}, bf16[128,2048]{1,0:T(8,128)(2,1)S(1)}, u32[]{:S(2)}, u32[]{:S(2)}) collective-permute-start(bf16[128,2048]{1,0:T(8,128)(2,1)S(1)} %delta.1.refs_0_.refs_1_), channel_id=1, source_target_pairs={{0,1},{1,0},{2,3},{3,2},{4,5},{5,4},{6,7},{7,6},{8,9},{9,8},{10,11... | collective-permute-start | bytes 1572872 | tf_op jit(solution)/shard_map/delta_other/ppermute | solution.py:66
  59.5 14.3 %collective-permute-start.18 = (bf16[128,2048]{1,0:T(8,128)(2,1)S(1)}, bf16[128,2048]{1,0:T(8,128)(2,1)S(1)}, u32[]{:S(2)}, u32[]{:S(2)}) collective-permute-start(bf16[128,2048]{1,0:T(8,128)(2,1)S(1)} %delta.1.refs_0_.refs_1_), channel_id=1, source_target_pairs={{0,4},{1,5},{2,6},{3,7},{4,8},{5,9},{6,10},{7,11},{8,12},{9,13},{1... | collective-permute-start | bytes 1572872 | tf_op jit(solution)/shard_map/delta/below/ppermute | solution.py:66
  59.5 14.3 %collective-permute-start.19 = (bf16[128,2048]{1,0:T(8,128)(2,1)S(1)}, bf16[128,2048]{1,0:T(8,128)(2,1)S(1)}, u32[]{:S(2)}, u32[]{:S(2)}) collective-permute-start(bf16[128,2048]{1,0:T(8,128)(2,1)S(1)} %delta.1.refs_0_.refs_1_), channel_id=1, source_target_pairs={{0,12},{1,13},{2,14},{3,15},{4,0},{5,1},{6,2},{7,3},{8,4},{9,5},{1... | collective-permute-start | bytes 1572872 | tf_op jit(solution)/shard_map/delta/above/ppermute | solution.py:66
  62.2 12.5 %collective-permute-start.20 = (bf16[128,2048]{1,0:T(8,128)(2,1)S(1)}, bf16[128,2048]{1,0:T(8,128)(2,1)S(1)}, u32[]{:S(2)}, u32[]{:S(2)}) collective-permute-start(bf16[128,2048]{1,0:T(8,128)(2,1)S(1)} %delta.1.refs_0_.refs_1_), channel_id=1, source_target_pairs={{0,2},{1,3},{2,0},{3,1},{4,6},{5,7},{6,4},{7,5},{8,10},{9,11},{10,... | collective-permute-start | bytes 1572872 | tf_op jit(solution)/shard_map/delta/pair/ppermute | solution.py:66
  66.0 19.2 %collective-permute-start.15 = (f32[8,128,128]{2,1,0:T(8,128)S(1)}, f32[8,128,128]{2,1,0:T(8,128)S(1)}, u32[]{:S(2)}, u32[]{:S(2)}) collective-permute-start(f32[8,128,128]{2,1,0:T(8,128)S(1)} %get-tuple-element.69), channel_id=1, source_target_pairs={{0,1},{1,0},{2,3},{3,2},{4,5},{5,4},{6,7},{7,6},{8,9},{9,8},{10,11... | collective-permute-start | bytes 1572872 | tf_op jit(solution)/shard_map/back/ppermute | solution.py:66
  76.1 20.7 %collective-permute-start.21 = (bf16[192,2048]{1,0:T(8,128)(2,1)}, bf16[192,2048]{1,0:T(8,128)(2,1)S(1)}, u32[]{:S(2)}, u32[]{:S(2)}) collective-permute-start(bf16[192,2048]{1,0:T(8,128)(2,1)} %get-tuple-element.74), channel_id=1, source_target_pairs={{0,4},{1,5},{2,6},{3,7},{4,8},{5,9},{6,10},{7,11},{8,12},{9,13},{1... | collective-permute-start | bytes 2359304 | tf_op jit(solution)/shard_map/delta/up/ppermute | solution.py:66
  76.2 20.6 %collective-permute-start.22 = (bf16[192,2048]{1,0:T(8,128)(2,1)}, bf16[192,2048]{1,0:T(8,128)(2,1)S(1)}, u32[]{:S(2)}, u32[]{:S(2)}) collective-permute-start(bf16[192,2048]{1,0:T(8,128)(2,1)} %get-tuple-element.75), channel_id=1, source_target_pairs={{0,12},{1,13},{2,14},{3,15},{4,0},{5,1},{6,2},{7,3},{8,4},{9,5},{1... | collective-permute-start | bytes 2359304 | tf_op jit(solution)/shard_map/delta/down/ppermute | solution.py:66
  78.8 9.9 %collective-permute-start.17 = (bf16[4,2,128,128]{3,2,1,0:T(8,128)(2,1)S(1)}, bf16[4,2,128,128]{3,2,1,0:T(8,128)(2,1)S(1)}, u32[]{:S(2)}, u32[]{:S(2)}) collective-permute-start(bf16[4,2,128,128]{3,2,1,0:T(8,128)(2,1)S(1)} %get-tuple-element.71), channel_id=1, source_target_pairs={{0,2},{1,3},{2,0},{3,1},{4,6},{5,7},{6,4},{7,5},{8,10},{9,11},{10,... | collective-permute-start | bytes 786440 | tf_op jit(solution)/shard_map/pair_units/ppermute | solution.py:66
  79.2 30.6 %collective-permute-start.25 = (bf16[128,2048]{1,0:T(8,128)(2,1)}, bf16[128,2048]{1,0:T(8,128)(2,1)}, u32[]{:S(2)}, u32[]{:S(2)}) collective-permute-start(bf16[128,2048]{1,0:T(8,128)(2,1)} %bitcast.refs_0_.refs_2_), channel_id=1, source_target_pairs={{0,240},{16,224},{32,208},{48,192},{64,176},{80,160},{96,144},{112... | collective-permute-start | bytes 1572872 | tf_op jit(solution)/shard_map/stash/ppermute | solution.py:53
  85.2 34.3 %collective-permute-start.10 = (bf16[128,2048]{1,0:T(8,128)(2,1)}, bf16[128,2048]{1,0:T(8,128)(2,1)}, u32[]{:S(2)}, u32[]{:S(2)}) collective-permute-start(bf16[128,2048]{1,0:T(8,128)(2,1)} %get-tuple-element.62), channel_id=1, source_target_pairs={{240,0},{0,16},{16,32},{32,48},{48,64},{64,80},{80,96},{96,112},{1... | collective-permute-start | bytes 1572872 | tf_op jit(solution)/shard_map/next_acts/ppermute | solution.py:58
  88.7 30.7 %collective-permute-start.16 = (bf16[128,2048]{1,0:T(8,128)(2,1)}, bf16[128,2048]{1,0:T(8,128)(2,1)}, u32[]{:S(2)}, u32[]{:S(2)}) collective-permute-start(bf16[128,2048]{1,0:T(8,128)(2,1)} %get-tuple-element.70), channel_id=1, source_target_pairs={{16,0},{32,16},{48,32},{64,48},{80,64},{96,80},{112,96},{128,112},... | collective-permute-start | bytes 1572872 | tf_op jit(solution)/shard_map/next_grads/ppermute | solution.py:58
  93.3 10.8 %all-to-all-start = ((bf16[4,2,2,128,128]{4,3,2,1,0:T(8,128)(2,1)}), bf16[4,2,2,128,128]{4,3,2,1,0:T(8,128)(2,1)S(1)}, u32[]{:S(2)}, u32[]{:S(2)}) async-start(bf16[4,2,2,128,128]{4,3,2,1,0:T(8,128)(2,1)} %copy-done.10), calls=%async_computation | async-start | bytes 1048576 | tf_op jit(solution)/shard_map/all_to_all | solution.py:494
  97.6 21.8 %collective-permute-start.23 = (bf16[64,2048]{1,0:T(8,128)(2,1)}, bf16[64,2048]{1,0:T(8,128)(2,1)S(1)}, u32[]{:S(2)}, u32[]{:S(2)}) collective-permute-start(bf16[64,2048]{1,0:T(8,128)(2,1)} %get-tuple-element.76), channel_id=1, source_target_pairs={{0,4},{1,5},{2,6},{3,7},{4,8},{5,9},{6,10},{7,11},{8,12},{9,13},{1... | collective-permute-start | bytes 786440 | tf_op jit(solution)/shard_map/delta/far_up/ppermute | solution.py:66
  99.1 20.3 %collective-permute-start.24 = (bf16[64,2048]{1,0:T(8,128)(2,1)}, bf16[64,2048]{1,0:T(8,128)(2,1)}, u32[]{:S(2)}, u32[]{:S(2)}) collective-permute-start(bf16[64,2048]{1,0:T(8,128)(2,1)} %get-tuple-element.77), channel_id=1, source_target_pairs={{0,12},{1,13},{2,14},{3,15},{4,0},{5,1},{6,2},{7,3},{8,4},{9,5},{1... | collective-permute-start | bytes 786440 | tf_op jit(solution)/shard_map/delta/far_down/ppermute | solution.py:66
  (19 other events, 106.0 us)

commit v5 on v4

--- a/solution.py
+++ b/solution.py
@@ -12,7 +12,7 @@
 CHIPS = RING * PAIR
 MEMBERS = CHIPS * CORES
 BLOCK = 128
-TILE = 256
+TILE = 1024
 MEGABYTES = 12
 WIDTH = 2048
 
@@ -203,9 +203,10 @@
         copy.wait()
 
 
-def units_kernel(half, received, keep, send, panel):
+def units_kernel(half, received, grads, keep, send, panel, grads_here):
     member, core = place()
     pair_at = lax.rem(lax.div(member, CORES), PAIR)
+    grads_here[...] = grads[...]
     rows = received.shape[0]
     for chip in range(CHIPS):
         at, of = chip * CORES * BLOCK, chip * BLOCK
@@ -467,15 +468,15 @@
     with jax.named_scope("restore"):
         restored = hop(panel_half[tokens:], core=1)
     ring_blocks = (RING, CORES, BLOCK, BLOCK)
-    keep, send, panel = call(
+    keep, send, panel, grads_here = call(
         "units",
         units_kernel,
-        [struct(ring_blocks, BF16), struct(ring_blocks, BF16), rows],
-        [panel_half, restored],
-        [VMEM] * 2,
+        [struct(ring_blocks, BF16), struct(ring_blocks, BF16), rows, rows],
+        [panel_half, restored, grads],
+        [VMEM] * 3,
     )
     (delta,) = call(
-        "delta", delta_kernel, [rows], [panel_own, received, grads], [VMEM] * 3, after=[keep]
+        "delta", delta_kernel, [rows], [panel_own, received, grads_here], [VMEM] * 3, after=[keep]
     )
     with jax.named_scope("delta"):
         delta_near, delta_middle, delta_far, take_token = gathered(delta, [out_token])
@@ -521,7 +522,7 @@
         "grads",
         grad_kernel,
         [rows, token],
-        [panel, gain, grads, back_own, back_received],
+        [panel, gain, grads_here, back_own, back_received],
         [VMEM] * 5,
         scratch=[pltpu.VMEM((tokens, width), F32)],
     )
@@ -547,7 +548,7 @@
     )
 
     outer_own, outer_other, outer_token = product(
-        "outer_far", "stacked", [units], delta_far, outer, after=[parked_token, next_acts, next_grads]
+        "outer_far", "stacked", [units], delta_far, outer, after=[parked_token, next_grads]
     )
     with jax.named_scope("outer"):
         outer_received = hop(outer_other, core=1)

time: 127 us -> 124 us (0.976)
  waiting for transfers between devices: 35.6 us -> 43.9 us
  Pallas kernels: 31.3 us -> 25.5 us
  starting transfers between devices: 52.2 us -> 46.7 us
    pallas_call x22, Pallas kernels: 31.3 us -> 25.5 us  [call(): pl.pallas_call(body, out_shape=list(outs), in_specs=list(specs) + [ANY] *...]
    ppermute x23, waiting for transfers between devices: 16.5 us -> 21.7 us  [hop(): return lax.ppermute(block, 'dp', route)]
    ppermute x2, starting transfers between devices: 5.16 us -> 0.08 us  [shifted(): lax.ppermute(block, 'section', [((i - distance) % count, i) for i in rang...]
    ppermute x2, waiting for transfers between devices: 7.73 us -> 11.6 us  [mirrored(): lax.ppermute(block, 'section', [(i, count - 1 - i) for i in range(count)])]
  transfers between devices with their start and end apart: 28 -> 28, of which waited for: 12 -> 14; matrix products, arithmetic and copies ran while one was open for 0% -> 0% of each run, Pallas kernels for 19% -> 18%
where the time goes in v5:
time: 124 us
  starting transfers between devices  46.7 us (38%)
  waiting for transfers between devices  43.9 us (35%)
  Pallas kernels  25.5 us (21%)
  local copies, waits for them, and re-layouts  6.72 us (5%)
    ppermute x23, starting transfers between devices, hop(): return lax.ppermute(block, 'dp', route)  28.3 us
    pallas_call x22, Pallas kernels, call(): pl.pallas_call(body, out_shape=list(outs), in_specs=list(specs) + [ANY] *...  25.5 us
    ppermute x23, waiting for transfers between devices, hop(): return lax.ppermute(block, 'dp', route)  21.7 us
    ppermute x2, starting transfers between devices, mirrored(): lax.ppermute(block, 'section', [(i, count - 1 - i) for i in range(count)])  14.9 us
    ppermute x2, waiting for transfers between devices, mirrored(): lax.ppermute(block, 'section', [(i, count - 1 - i) for i in range(count)])  11.6 us
    ppermute x2, waiting for transfers between devices, shifted(): lax.ppermute(block, 'section', [((i - distance) % count, i) for i in rang...  8 us
    unnamed x30, local copies, waits for them, and re-layouts  6.71 us
    all_to_all x1, starting transfers between devices, shards(): lax.all_to_all(mixed, 'dp', split_axis=0, concat_axis=0, tiled=True, axis...  3.47 us
  transfers between devices with their start and end apart: 28, of which 14 were waited for; matrix products, arithmetic and copies ran while one was open for 0% of the time, Pallas kernels for 18%

profile of v5, /device:TPU:1, one launch (start us, length us, event | category | flops | bytes accessed | tf_op | source)
XLA Modules:
  0.0 123.6 jit_solution(9492552474735264325)
XLA Ops:
  0.6 2.2 %collective-permute-start.1 = (bf16[128,2048]{1,0:T(8,128)(2,1)}, bf16[128,2048]{1,0:T(8,128)(2,1)S(1)}, u32[]{:S(2)}, u32[]{:S(2)}) collective-permute-start(bf16[128,2048]{1,0:T(8,128)(2,1)} %bitcast.3), channel_id=1, source_target_pairs={{0,4},{1,5},{2,6},{3,7},{4,8},{5,9},{6,10},{7,11},{8,12},{9,13},{1... | collective-permute-start | bytes 1572872 | tf_op jit(solution)/shard_map/weight/below/ppermute | solution.py:66
  8.4 1.7 %collective-permute-start.4 = (bf16[128,1024]{1,0:T(8,128)(2,1)S(1)}, bf16[128,1024]{1,0:T(8,128)(2,1)S(1)}, u32[]{:S(2)}, u32[]{:S(2)}) collective-permute-start(bf16[128,1024]{1,0:T(8,128)(2,1)S(1)} %get-tuple-element.53), channel_id=1, source_target_pairs={{0,1},{1,0},{2,3},{3,2},{4,5},{5,4},{6,7},{7,6},{8,9},{9,8},{10,11... | collective-permute-start | bytes 786440 | tf_op jit(solution)/shard_map/ppermute | solution.py:66
  18.7 9.2 %collective-permute-start.11 = (bf16[256,1024]{1,0:T(8,128)(2,1)S(1)}, bf16[256,1024]{1,0:T(8,128)(2,1)S(1)}, u32[]{:S(2)}, u32[]{:S(2)}) collective-permute-start(bf16[256,1024]{1,0:T(8,128)(2,1)S(1)} %join.1.refs_1_.refs_3_), channel_id=1, source_target_pairs={{0,240},{16,224},{32,208},{48,192},{64,176},{80,160},{96,144},{112... | collective-permute-start | bytes 1572872 | tf_op jit(solution)/shard_map/panel/ppermute | solution.py:53
  27.9 2.8 %collective-permute-start = (bf16[8,128,128]{2,1,0:T(8,128)(2,1)S(1)}, bf16[8,128,128]{2,1,0:T(8,128)(2,1)S(1)}, u32[]{:S(2)}, u32[]{:S(2)}) collective-permute-start(bf16[8,128,128]{2,1,0:T(8,128)(2,1)S(1)} %get-tuple-element.51), channel_id=1, source_target_pairs={{0,1},{1,0},{2,3},{3,2},{4,5},{5,4},{6,7},{7,6},{8,9},{9,8},{10,11... | collective-permute-start | bytes 786440 | tf_op jit(solution)/shard_map/acts/ppermute | solution.py:66
  30.7 2.4 %collective-permute-done.5.refs_0_.refs_2_.refs_6_ = bf16[192,2048]{1,0:T(8,128)(2,1)S(1)} collective-permute-done((bf16[192,2048]{1,0:T(8,128)(2,1)S(1)}, bf16[192,2048]{1,0:T(8,128)(2,1)S(1)}, u32[]{:S(2)}, u32[]{:S(2)}) %collective-permute-start.5) | collective-permute-done | bytes 786464 | tf_op jit(solution)/shard_map/weight/up/ppermute | solution.py:66
  35.6 1.6 %collective-permute-start.8 = (bf16[64,2048]{1,0:T(8,128)(2,1)S(1)}, bf16[64,2048]{1,0:T(8,128)(2,1)S(1)}, u32[]{:S(2)}, u32[]{:S(2)}) collective-permute-start(bf16[64,2048]{1,0:T(8,128)(2,1)S(1)} %get-tuple-element.58), channel_id=1, source_target_pairs={{0,12},{1,13},{2,14},{3,15},{4,0},{5,1},{6,2},{7,3},{8,4},{9,5},{1... | collective-permute-start | bytes 786440 | tf_op jit(solution)/shard_map/weight/far_down/ppermute | solution.py:66
  38.3 3.0 %collective-permute-done.7.refs_4_.refs_8_ = bf16[64,2048]{1,0:T(8,128)(2,1)S(1)} collective-permute-done((bf16[64,2048]{1,0:T(8,128)(2,1)S(1)}, bf16[64,2048]{1,0:T(8,128)(2,1)S(1)}, u32[]{:S(2)}, u32[]{:S(2)}) %collective-permute-start.7) | collective-permute-done | bytes 262176 | tf_op jit(solution)/shard_map/weight/far_up/ppermute | solution.py:66
  42.2 8.8 %collective-permute-done.11.refs_0_ = bf16[256,1024]{1,0:T(8,128)(2,1)S(1)} collective-permute-done((bf16[256,1024]{1,0:T(8,128)(2,1)S(1)}, bf16[256,1024]{1,0:T(8,128)(2,1)S(1)}, u32[]{:S(2)}, u32[]{:S(2)}) %collective-permute-start.11) | collective-permute-done | bytes 524320 | tf_op jit(solution)/shard_map/panel/ppermute | solution.py:53
  51.0 2.2 %backward.1 = (f32[128,2176]{1,0:T(8,128)S(1)}, bf16[128,2304]{1,0:T(8,128)(2,1)S(1)}, f32[8,128]{1,0:T(8,128)}) custom-call(bf16[256,1024]{1,0:T(8,128)(2,1)S(1)} %collective-permute-done.11.refs_0_, f32[1,2048]{1,0:T(1,128)S(1)} %copy-done.12, bf16[128,2048]{1,0:T(8,128)(2,1)S(1)} %bitcast.7, bf16[128,2048]{1,0:T(8,128)(2,1)S(1)} %collective-permute-done.1.refs_0_.refs_3_, ...), custom_call_target="tpu_custom_call" | custom-call | flops 1140850688 | bytes 6434816 | tf_op jit(solution)/shard_map/backward/pallas_call | solution.py:38
  54.3 1.9 %collective-permute-done.12.refs_1_ = bf16[128,1024]{1,0:T(8,128)(2,1)S(1)} collective-permute-done((bf16[128,1024]{1,0:T(8,128)(2,1)S(1)}, bf16[128,1024]{1,0:T(8,128)(2,1)S(1)}, u32[]{:S(2)}, u32[]{:S(2)}) %collective-permute-start.12) | collective-permute-done | bytes 262176 | tf_op jit(solution)/shard_map/restore/ppermute | solution.py:66
  58.1 2.7 %collective-permute-start.19 = (bf16[128,2048]{1,0:T(8,128)(2,1)S(1)}, bf16[128,2048]{1,0:T(8,128)(2,1)S(1)}, u32[]{:S(2)}, u32[]{:S(2)}) collective-permute-start(bf16[128,2048]{1,0:T(8,128)(2,1)S(1)} %delta.1.refs_0_.refs_1_), channel_id=1, source_target_pairs={{0,12},{1,13},{2,14},{3,15},{4,0},{5,1},{6,2},{7,3},{8,4},{9,5},{1... | collective-permute-start | bytes 1572872 | tf_op jit(solution)/shard_map/delta/above/ppermute | solution.py:66
  61.1 2.1 %out.1 = (bf16[128,2048]{1,0:T(8,128)(2,1)}, f32[8,128]{1,0:T(8,128)S(1)}) custom-call(f32[128,2048]{1,0:T(8,128)S(1)} %get-tuple-element.61.refs_0_, bf16[128,2048]{1,0:T(8,128)(2,1)S(1)} %collective-permute-done.9.refs_1_, bf16[128,2048]{1,0:T(8,128)(2,1)} %bitcast.refs_0_.refs_2_), custom_call_target="tpu_custom_call" | custom-call | bytes 2625536 | tf_op jit(solution)/shard_map/out/pallas_call | solution.py:38
  65.6 6.9 %collective-permute-done.18.refs_0_.refs_2_ = bf16[128,2048]{1,0:T(8,128)(2,1)S(1)} collective-permute-done((bf16[128,2048]{1,0:T(8,128)(2,1)S(1)}, bf16[128,2048]{1,0:T(8,128)(2,1)S(1)}, u32[]{:S(2)}, u32[]{:S(2)}) %collective-permute-start.18) | collective-permute-done | bytes 524320 | tf_op jit(solution)/shard_map/delta/below/ppermute | solution.py:66
  74.9 2.7 %collective-permute-start.22 = (bf16[192,2048]{1,0:T(8,128)(2,1)}, bf16[192,2048]{1,0:T(8,128)(2,1)S(1)}, u32[]{:S(2)}, u32[]{:S(2)}) collective-permute-start(bf16[192,2048]{1,0:T(8,128)(2,1)} %get-tuple-element.77), channel_id=1, source_target_pairs={{0,12},{1,13},{2,14},{3,15},{4,0},{5,1},{6,2},{7,3},{8,4},{9,5},{1... | collective-permute-start | bytes 2359304 | tf_op jit(solution)/shard_map/delta/down/ppermute | solution.py:66
  77.9 5.7 %collective-permute-start.25 = (bf16[128,2048]{1,0:T(8,128)(2,1)}, bf16[128,2048]{1,0:T(8,128)(2,1)}, u32[]{:S(2)}, u32[]{:S(2)}) collective-permute-start(bf16[128,2048]{1,0:T(8,128)(2,1)} %bitcast.refs_0_.refs_2_), channel_id=1, source_target_pairs={{0,240},{16,224},{32,208},{48,192},{64,176},{80,160},{96,144},{112... | collective-permute-start | bytes 1572872 | tf_op jit(solution)/shard_map/stash/ppermute | solution.py:53
  86.5 3.5 %all-to-all-start = ((bf16[4,2,2,128,128]{4,3,2,1,0:T(8,128)(2,1)}), bf16[4,2,2,128,128]{4,3,2,1,0:T(8,128)(2,1)S(1)}, u32[]{:S(2)}, u32[]{:S(2)}) async-start(bf16[4,2,2,128,128]{4,3,2,1,0:T(8,128)(2,1)} %copy-done.10), calls=%async_computation | async-start | bytes 1048576 | tf_op jit(solution)/shard_map/all_to_all | solution.py:495
  90.0 3.6 %collective-permute-done.21.refs_0_.refs_5_ = bf16[192,2048]{1,0:T(8,128)(2,1)S(1)} collective-permute-done((bf16[192,2048]{1,0:T(8,128)(2,1)}, bf16[192,2048]{1,0:T(8,128)(2,1)S(1)}, u32[]{:S(2)}, u32[]{:S(2)}) %collective-permute-start.21) | collective-permute-done | bytes 786464 | tf_op jit(solution)/shard_map/delta/up/ppermute | solution.py:66
  94.6 2.6 %collective-permute-start.24 = (bf16[64,2048]{1,0:T(8,128)(2,1)}, bf16[64,2048]{1,0:T(8,128)(2,1)}, u32[]{:S(2)}, u32[]{:S(2)}) collective-permute-start(bf16[64,2048]{1,0:T(8,128)(2,1)} %get-tuple-element.79), channel_id=1, source_target_pairs={{0,12},{1,13},{2,14},{3,15},{4,0},{5,1},{6,2},{7,3},{8,4},{9,5},{1... | collective-permute-start | bytes 786440 | tf_op jit(solution)/shard_map/delta/far_down/ppermute | solution.py:66
  97.3 2.6 %all-to-all-done.refs_0_ = bf16[4,2,2,128,128]{4,3,2,1,0:T(8,128)(2,1)S(1)} async-done(((bf16[4,2,2,128,128]{4,3,2,1,0:T(8,128)(2,1)}), bf16[4,2,2,128,128]{4,3,2,1,0:T(8,128)(2,1)S(1)}, u32[]{:S(2)}, u32[]{:S(2)}) %all-to-all-start) | async-done | bytes 524320 | tf_op jit(solution)/shard_map/all_to_all | solution.py:495
  104.5 2.8 %collective-permute-done.25.refs_2_ = bf16[128,2048]{1,0:T(8,128)(2,1)} collective-permute-done((bf16[128,2048]{1,0:T(8,128)(2,1)}, bf16[128,2048]{1,0:T(8,128)(2,1)}, u32[]{:S(2)}, u32[]{:S(2)}) %collective-permute-start.25) | collective-permute-done | bytes 524320 | tf_op jit(solution)/shard_map/stash/ppermute | solution.py:53
  107.3 1.9 %park.1 = (bf16[1,3,128,2048]{3,2,1,0:T(8,128)(2,1)}, f32[8,128]{1,0:T(8,128)S(1)}) custom-call(s32[16]{0:T(128)S(1)} %copy-done.14, bf16[1,3,128,2048]{3,2,1,0:T(8,128)(2,1)} %get-tuple-element.83.refs_1_, bf16[128,2048]{1,0:T(8,128)(2,1)} %collective-permute-done.25.refs_2_, f32[8,128]{1,0:T(8,128)S(1)} %get-tuple-element.84.refs_3_), custom_call_target="tpu_custom_call", output_to_operand_aliasing={{0}: (1, {})} | custom-call | bytes 3674176 | tf_op jit(solution)/shard_map/park/pallas_call | solution.py:38
  109.2 8.0 %collective-permute-done.16.refs_6_.refs_1_ = bf16[128,2048]{1,0:T(8,128)(2,1)} collective-permute-done((bf16[128,2048]{1,0:T(8,128)(2,1)}, bf16[128,2048]{1,0:T(8,128)(2,1)}, u32[]{:S(2)}, u32[]{:S(2)}) %collective-permute-start.16) | collective-permute-done | bytes 524320 | tf_op jit(solution)/shard_map/next_grads/ppermute | solution.py:58
  117.2 1.6 %outer_far.1 = (f32[128,2048]{1,0:T(8,128)S(1)}, bf16[128,2048]{1,0:T(8,128)(2,1)S(1)}, f32[8,128]{1,0:T(8,128)S(1)}) custom-call(bf16[4,2,2,128,128]{4,3,2,1,0:T(8,128)(2,1)S(1)} %all-to-all-done.refs_0_, bf16[64,2048]{1,0:T(8,128)(2,1)} %collective-permute-done.23.refs_1_, bf16[64,2048]{1,0:T(8,128)(2,1)} %collective-permute-done.24.refs_2_, ...), custom_call_target="tpu_custom_call" | custom-call | flops 134217728 | bytes 4722688 | tf_op jit(solution)/shard_map/outer_far/pallas_call | solution.py:38
  120.2 2.2 %emit.1 = (bf16[1,128,2048]{2,1,0:T(8,128)(2,1)}, bf16[1,128,2048]{2,1,0:T(8,128)(2,1)}, f32[8,128]{1,0:T(8,128)S(1)}) custom-call(bf16[128,2048]{1,0:T(8,128)(2,1)} %collective-permute-done.10.refs_0_, bf16[128,2048]{1,0:T(8,128)(2,1)} %collective-permute-done.16.refs_6_.refs_1_, f32[8,128]{1,0:T(8,128)S(1)} %get-tuple-element.86.refs_2_), custom_call_target="tpu_custom_call" | custom-call | bytes 2101248 | tf_op jit(solution)/shard_map/emit/pallas_call | solution.py:38
  (85 shorter events, 38.2 us)
Async XLA Ops:
  0.6 13.5 %collective-permute-start.1 = (bf16[128,2048]{1,0:T(8,128)(2,1)}, bf16[128,2048]{1,0:T(8,128)(2,1)S(1)}, u32[]{:S(2)}, u32[]{:S(2)}) collective-permute-start(bf16[128,2048]{1,0:T(8,128)(2,1)} %bitcast.3), channel_id=1, source_target_pairs={{0,4},{1,5},{2,6},{3,7},{4,8},{5,9},{6,10},{7,11},{8,12},{9,13},{1... | collective-permute-start | bytes 1572872 | tf_op jit(solution)/shard_map/weight/below/ppermute | solution.py:66
  2.8 12.4 %collective-permute-start.2 = (bf16[128,2048]{1,0:T(8,128)(2,1)}, bf16[128,2048]{1,0:T(8,128)(2,1)S(1)}, u32[]{:S(2)}, u32[]{:S(2)}) collective-permute-start(bf16[128,2048]{1,0:T(8,128)(2,1)} %bitcast.4), channel_id=1, source_target_pairs={{0,12},{1,13},{2,14},{3,15},{4,0},{5,1},{6,2},{7,3},{8,4},{9,5},{1... | collective-permute-start | bytes 1572872 | tf_op jit(solution)/shard_map/weight/above/ppermute | solution.py:66
  4.4 11.4 %collective-permute-start.3 = (bf16[128,2048]{1,0:T(8,128)(2,1)}, bf16[128,2048]{1,0:T(8,128)(2,1)S(1)}, u32[]{:S(2)}, u32[]{:S(2)}) collective-permute-start(bf16[128,2048]{1,0:T(8,128)(2,1)} %bitcast.5), channel_id=1, source_target_pairs={{0,2},{1,3},{2,0},{3,1},{4,6},{5,7},{6,4},{7,5},{8,10},{9,11},{10,... | collective-permute-start | bytes 1572872 | tf_op jit(solution)/shard_map/weight/pair/ppermute | solution.py:66
  15.9 17.2 %collective-permute-start.5 = (bf16[192,2048]{1,0:T(8,128)(2,1)S(1)}, bf16[192,2048]{1,0:T(8,128)(2,1)S(1)}, u32[]{:S(2)}, u32[]{:S(2)}) collective-permute-start(bf16[192,2048]{1,0:T(8,128)(2,1)S(1)} %get-tuple-element.55), channel_id=1, source_target_pairs={{0,4},{1,5},{2,6},{3,7},{4,8},{5,9},{6,10},{7,11},{8,12},{9,13},{1... | collective-permute-start | bytes 2359304 | tf_op jit(solution)/shard_map/weight/up/ppermute | solution.py:66
  17.1 16.7 %collective-permute-start.6 = (bf16[192,2048]{1,0:T(8,128)(2,1)S(1)}, bf16[192,2048]{1,0:T(8,128)(2,1)S(1)}, u32[]{:S(2)}, u32[]{:S(2)}) collective-permute-start(bf16[192,2048]{1,0:T(8,128)(2,1)S(1)} %get-tuple-element.56), channel_id=1, source_target_pairs={{0,12},{1,13},{2,14},{3,15},{4,0},{5,1},{6,2},{7,3},{8,4},{9,5},{1... | collective-permute-start | bytes 2359304 | tf_op jit(solution)/shard_map/weight/down/ppermute | solution.py:66
  18.7 32.3 %collective-permute-start.11 = (bf16[256,1024]{1,0:T(8,128)(2,1)S(1)}, bf16[256,1024]{1,0:T(8,128)(2,1)S(1)}, u32[]{:S(2)}, u32[]{:S(2)}) collective-permute-start(bf16[256,1024]{1,0:T(8,128)(2,1)S(1)} %join.1.refs_1_.refs_3_), channel_id=1, source_target_pairs={{0,240},{16,224},{32,208},{48,192},{64,176},{80,160},{96,144},{112... | collective-permute-start | bytes 1572872 | tf_op jit(solution)/shard_map/panel/ppermute | solution.py:53
  27.9 9.3 %collective-permute-start = (bf16[8,128,128]{2,1,0:T(8,128)(2,1)S(1)}, bf16[8,128,128]{2,1,0:T(8,128)(2,1)S(1)}, u32[]{:S(2)}, u32[]{:S(2)}) collective-permute-start(bf16[8,128,128]{2,1,0:T(8,128)(2,1)S(1)} %get-tuple-element.51), channel_id=1, source_target_pairs={{0,1},{1,0},{2,3},{3,2},{4,5},{5,4},{6,7},{7,6},{8,9},{9,8},{10,11... | collective-permute-start | bytes 786440 | tf_op jit(solution)/shard_map/acts/ppermute | solution.py:66
  34.4 6.8 %collective-permute-start.7 = (bf16[64,2048]{1,0:T(8,128)(2,1)S(1)}, bf16[64,2048]{1,0:T(8,128)(2,1)S(1)}, u32[]{:S(2)}, u32[]{:S(2)}) collective-permute-start(bf16[64,2048]{1,0:T(8,128)(2,1)S(1)} %get-tuple-element.57), channel_id=1, source_target_pairs={{0,4},{1,5},{2,6},{3,7},{4,8},{5,9},{6,10},{7,11},{8,12},{9,13},{1... | collective-permute-start | bytes 786440 | tf_op jit(solution)/shard_map/weight/far_up/ppermute | solution.py:66
  35.6 5.7 %collective-permute-start.8 = (bf16[64,2048]{1,0:T(8,128)(2,1)S(1)}, bf16[64,2048]{1,0:T(8,128)(2,1)S(1)}, u32[]{:S(2)}, u32[]{:S(2)}) collective-permute-start(bf16[64,2048]{1,0:T(8,128)(2,1)S(1)} %get-tuple-element.58), channel_id=1, source_target_pairs={{0,12},{1,13},{2,14},{3,15},{4,0},{5,1},{6,2},{7,3},{8,4},{9,5},{1... | collective-permute-start | bytes 786440 | tf_op jit(solution)/shard_map/weight/far_down/ppermute | solution.py:66
  56.7 4.3 %collective-permute-start.9 = (bf16[128,2048]{1,0:T(8,128)(2,1)S(1)}, bf16[128,2048]{1,0:T(8,128)(2,1)S(1)}, u32[]{:S(2)}, u32[]{:S(2)}) collective-permute-start(bf16[128,2048]{1,0:T(8,128)(2,1)S(1)} %get-tuple-element.62), channel_id=1, source_target_pairs={{0,1},{1,0},{2,3},{3,2},{4,5},{5,4},{6,7},{7,6},{8,9},{9,8},{10,11... | collective-permute-start | bytes 1572872 | tf_op jit(solution)/shard_map/pre_acts/ppermute | solution.py:66
  57.7 5.5 %collective-permute-start.14 = (bf16[128,2048]{1,0:T(8,128)(2,1)S(1)}, bf16[128,2048]{1,0:T(8,128)(2,1)S(1)}, u32[]{:S(2)}, u32[]{:S(2)}) collective-permute-start(bf16[128,2048]{1,0:T(8,128)(2,1)S(1)} %delta.1.refs_0_.refs_1_), channel_id=1, source_target_pairs={{0,1},{1,0},{2,3},{3,2},{4,5},{5,4},{6,7},{7,6},{8,9},{9,8},{10,11... | collective-permute-start | bytes 1572872 | tf_op jit(solution)/shard_map/delta_other/ppermute | solution.py:66
  57.9 14.6 %collective-permute-start.18 = (bf16[128,2048]{1,0:T(8,128)(2,1)S(1)}, bf16[128,2048]{1,0:T(8,128)(2,1)S(1)}, u32[]{:S(2)}, u32[]{:S(2)}) collective-permute-start(bf16[128,2048]{1,0:T(8,128)(2,1)S(1)} %delta.1.refs_0_.refs_1_), channel_id=1, source_target_pairs={{0,4},{1,5},{2,6},{3,7},{4,8},{5,9},{6,10},{7,11},{8,12},{9,13},{1... | collective-permute-start | bytes 1572872 | tf_op jit(solution)/shard_map/delta/below/ppermute | solution.py:66
  58.1 14.5 %collective-permute-start.19 = (bf16[128,2048]{1,0:T(8,128)(2,1)S(1)}, bf16[128,2048]{1,0:T(8,128)(2,1)S(1)}, u32[]{:S(2)}, u32[]{:S(2)}) collective-permute-start(bf16[128,2048]{1,0:T(8,128)(2,1)S(1)} %delta.1.refs_0_.refs_1_), channel_id=1, source_target_pairs={{0,12},{1,13},{2,14},{3,15},{4,0},{5,1},{6,2},{7,3},{8,4},{9,5},{1... | collective-permute-start | bytes 1572872 | tf_op jit(solution)/shard_map/delta/above/ppermute | solution.py:66
  60.7 12.6 %collective-permute-start.20 = (bf16[128,2048]{1,0:T(8,128)(2,1)S(1)}, bf16[128,2048]{1,0:T(8,128)(2,1)S(1)}, u32[]{:S(2)}, u32[]{:S(2)}) collective-permute-start(bf16[128,2048]{1,0:T(8,128)(2,1)S(1)} %delta.1.refs_0_.refs_1_), channel_id=1, source_target_pairs={{0,2},{1,3},{2,0},{3,1},{4,6},{5,7},{6,4},{7,5},{8,10},{9,11},{10,... | collective-permute-start | bytes 1572872 | tf_op jit(solution)/shard_map/delta/pair/ppermute | solution.py:66
  64.5 19.1 %collective-permute-start.15 = (f32[8,128,128]{2,1,0:T(8,128)S(1)}, f32[8,128,128]{2,1,0:T(8,128)S(1)}, u32[]{:S(2)}, u32[]{:S(2)}) collective-permute-start(f32[8,128,128]{2,1,0:T(8,128)S(1)} %get-tuple-element.71), channel_id=1, source_target_pairs={{0,1},{1,0},{2,3},{3,2},{4,5},{5,4},{6,7},{7,6},{8,9},{9,8},{10,11... | collective-permute-start | bytes 1572872 | tf_op jit(solution)/shard_map/back/ppermute | solution.py:66
  74.8 18.8 %collective-permute-start.21 = (bf16[192,2048]{1,0:T(8,128)(2,1)}, bf16[192,2048]{1,0:T(8,128)(2,1)S(1)}, u32[]{:S(2)}, u32[]{:S(2)}) collective-permute-start(bf16[192,2048]{1,0:T(8,128)(2,1)} %get-tuple-element.76), channel_id=1, source_target_pairs={{0,4},{1,5},{2,6},{3,7},{4,8},{5,9},{6,10},{7,11},{8,12},{9,13},{1... | collective-permute-start | bytes 2359304 | tf_op jit(solution)/shard_map/delta/up/ppermute | solution.py:66
  74.9 18.8 %collective-permute-start.22 = (bf16[192,2048]{1,0:T(8,128)(2,1)}, bf16[192,2048]{1,0:T(8,128)(2,1)S(1)}, u32[]{:S(2)}, u32[]{:S(2)}) collective-permute-start(bf16[192,2048]{1,0:T(8,128)(2,1)} %get-tuple-element.77), channel_id=1, source_target_pairs={{0,12},{1,13},{2,14},{3,15},{4,0},{5,1},{6,2},{7,3},{8,4},{9,5},{1... | collective-permute-start | bytes 2359304 | tf_op jit(solution)/shard_map/delta/down/ppermute | solution.py:66
  77.5 7.6 %collective-permute-start.17 = (bf16[4,2,128,128]{3,2,1,0:T(8,128)(2,1)S(1)}, bf16[4,2,128,128]{3,2,1,0:T(8,128)(2,1)S(1)}, u32[]{:S(2)}, u32[]{:S(2)}) collective-permute-start(bf16[4,2,128,128]{3,2,1,0:T(8,128)(2,1)S(1)} %get-tuple-element.73), channel_id=1, source_target_pairs={{0,2},{1,3},{2,0},{3,1},{4,6},{5,7},{6,4},{7,5},{8,10},{9,11},{10,... | collective-permute-start | bytes 786440 | tf_op jit(solution)/shard_map/pair_units/ppermute | solution.py:66
  77.9 29.4 %collective-permute-start.25 = (bf16[128,2048]{1,0:T(8,128)(2,1)}, bf16[128,2048]{1,0:T(8,128)(2,1)}, u32[]{:S(2)}, u32[]{:S(2)}) collective-permute-start(bf16[128,2048]{1,0:T(8,128)(2,1)} %bitcast.refs_0_.refs_2_), channel_id=1, source_target_pairs={{0,240},{16,224},{32,208},{48,192},{64,176},{80,160},{96,144},{112... | collective-permute-start | bytes 1572872 | tf_op jit(solution)/shard_map/stash/ppermute | solution.py:53
  85.0 32.2 %collective-permute-start.16 = (bf16[128,2048]{1,0:T(8,128)(2,1)}, bf16[128,2048]{1,0:T(8,128)(2,1)}, u32[]{:S(2)}, u32[]{:S(2)}) collective-permute-start(bf16[128,2048]{1,0:T(8,128)(2,1)} %get-tuple-element.72), channel_id=1, source_target_pairs={{16,0},{32,16},{48,32},{64,48},{80,64},{96,80},{112,96},{128,112},... | collective-permute-start | bytes 1572872 | tf_op jit(solution)/shard_map/next_grads/ppermute | solution.py:58
  86.5 13.3 %all-to-all-start = ((bf16[4,2,2,128,128]{4,3,2,1,0:T(8,128)(2,1)}), bf16[4,2,2,128,128]{4,3,2,1,0:T(8,128)(2,1)S(1)}, u32[]{:S(2)}, u32[]{:S(2)}) async-start(bf16[4,2,2,128,128]{4,3,2,1,0:T(8,128)(2,1)} %copy-done.10), calls=%async_computation | async-start | bytes 1048576 | tf_op jit(solution)/shard_map/all_to_all | solution.py:495
  94.5 22.7 %collective-permute-start.23 = (bf16[64,2048]{1,0:T(8,128)(2,1)}, bf16[64,2048]{1,0:T(8,128)(2,1)}, u32[]{:S(2)}, u32[]{:S(2)}) collective-permute-start(bf16[64,2048]{1,0:T(8,128)(2,1)} %get-tuple-element.78), channel_id=1, source_target_pairs={{0,4},{1,5},{2,6},{3,7},{4,8},{5,9},{6,10},{7,11},{8,12},{9,13},{1... | collective-permute-start | bytes 786440 | tf_op jit(solution)/shard_map/delta/far_up/ppermute | solution.py:66
  94.6 22.6 %collective-permute-start.24 = (bf16[64,2048]{1,0:T(8,128)(2,1)}, bf16[64,2048]{1,0:T(8,128)(2,1)}, u32[]{:S(2)}, u32[]{:S(2)}) collective-permute-start(bf16[64,2048]{1,0:T(8,128)(2,1)} %get-tuple-element.79), channel_id=1, source_target_pairs={{0,12},{1,13},{2,14},{3,15},{4,0},{5,1},{6,2},{7,3},{8,4},{9,5},{1... | collective-permute-start | bytes 786440 | tf_op jit(solution)/shard_map/delta/far_down/ppermute | solution.py:66
  97.3 22.9 %collective-permute-start.10 = (bf16[128,2048]{1,0:T(8,128)(2,1)}, bf16[128,2048]{1,0:T(8,128)(2,1)}, u32[]{:S(2)}, u32[]{:S(2)}) collective-permute-start(bf16[128,2048]{1,0:T(8,128)(2,1)} %get-tuple-element.63), channel_id=1, source_target_pairs={{240,0},{0,16},{16,32},{32,48},{48,64},{64,80},{80,96},{96,112},{1... | collective-permute-start | bytes 1572872 | tf_op jit(solution)/shard_map/next_acts/ppermute | solution.py:58
  (19 other events, 101.8 us)

commit v6 on v5

--- a/solution.py
+++ b/solution.py
@@ -82,7 +82,6 @@
         [packed, packed],
         [below, above, pair],
         [VMEM] * 3,
-        scratch=[pltpu.SemaphoreType.DMA((4,))],
         after=after,
     )
     with jax.named_scope("up"):
@@ -96,7 +95,6 @@
         [halves, halves, struct((8, BLOCK), F32)],
         [up, down],
         [VMEM] * 2,
-        scratch=[pltpu.SemaphoreType.DMA((2,))],
         after=take_after,
     )
     with jax.named_scope("far_up"):
@@ -172,35 +170,20 @@
     joined[rows:] = received[...]
 
 
-def copy_all(pairs, sems):
-    copies = [pltpu.make_async_copy(a, b, sems.at[i]) for i, (a, b) in enumerate(pairs)]
-    for copy in copies:
-        copy.start()
-    return copies
-
-
-def pack_kernel(below, above, pair, up, down, sems):
+def pack_kernel(below, above, pair, up, down):
     rows = pair.shape[0]
     half = rows // 2
-    copies = copy_all(
-        [
-            (pair, up.at[pl.ds(half, rows)]),
-            (pair, down.at[pl.ds(0, rows)]),
-            (below.at[pl.ds(0, half)], up.at[pl.ds(0, half)]),
-            (above.at[pl.ds(half, half)], down.at[pl.ds(rows, half)]),
-        ],
-        sems,
-    )
-    for copy in copies:
-        copy.wait()
-
-
-def take_kernel(up, down, low, high, token, sems):
-    token[...] = jnp.zeros_like(token)
+    up[:half] = below[:half]
+    up[half:] = pair[...]
+    down[:rows] = pair[...]
+    down[rows:] = above[half:]
+
+
+def take_kernel(up, down, low, high, token):
     rows = low.shape[0]
-    copies = copy_all([(up.at[pl.ds(rows, rows)], low), (down.at[pl.ds(rows, rows)], high)], sems)
-    for copy in copies:
-        copy.wait()
+    token[...] = jnp.zeros_like(token)
+    low[...] = up[rows : 2 * rows]
+    high[...] = down[rows : 2 * rows]
 
 
 def units_kernel(half, received, grads, keep, send, panel, grads_here):

time: 124 us -> 124 us (level)
  no operation moved by 1% of the time
where the time goes in v6:
time: 124 us; the launch traced here: 123 us
  starting transfers between devices  46.3 us (37%)
  waiting for transfers between devices  44.2 us (36%)
  Pallas kernels  25.4 us (20%)
  local copies, waits for them, and re-layouts  6.72 us (5%)
    ppermute x23, starting transfers between devices, hop(): return lax.ppermute(block, 'dp', route)  27.9 us
    pallas_call x22, Pallas kernels, call(): pl.pallas_call(body, out_shape=list(outs), in_specs=list(specs) + [ANY] *...  25.4 us
    ppermute x23, waiting for transfers between devices, hop(): return lax.ppermute(block, 'dp', route)  21.7 us
    ppermute x2, starting transfers between devices, mirrored(): lax.ppermute(block, 'section', [(i, count - 1 - i) for i in range(count)])  14.9 us
    ppermute x2, waiting for transfers between devices, mirrored(): lax.ppermute(block, 'section', [(i, count - 1 - i) for i in range(count)])  11.6 us
    ppermute x2, waiting for transfers between devices, shifted(): lax.ppermute(block, 'section', [((i - distance) % count, i) for i in rang...  8.22 us
    unnamed x30, local copies, waits for them, and re-layouts  6.71 us
    all_to_all x1, starting transfers between devices, shards(): lax.all_to_all(mixed, 'dp', split_axis=0, concat_axis=0, tiled=True, axis...  3.47 us
  transfers between devices with their start and end apart: 28, of which 14 were waited for; matrix products, arithmetic and copies ran while one was open for 0% of the time, Pallas kernels for 18%

profile of v6, /device:TPU:1, one launch (start us, length us, event | category | flops | bytes accessed | tf_op | source)
XLA Modules:
  0.0 123.5 jit_solution(17605649473407820612)
XLA Ops:
  0.6 2.2 %collective-permute-start.1 = (bf16[128,2048]{1,0:T(8,128)(2,1)}, bf16[128,2048]{1,0:T(8,128)(2,1)S(1)}, u32[]{:S(2)}, u32[]{:S(2)}) collective-permute-start(bf16[128,2048]{1,0:T(8,128)(2,1)} %bitcast.3), channel_id=1, source_target_pairs={{0,4},{1,5},{2,6},{3,7},{4,8},{5,9},{6,10},{7,11},{8,12},{9,13},{1... | collective-permute-start | bytes 1572872 | tf_op jit(solution)/shard_map/weight/below/ppermute | solution.py:66
  8.4 1.7 %collective-permute-start.4 = (bf16[128,1024]{1,0:T(8,128)(2,1)S(1)}, bf16[128,1024]{1,0:T(8,128)(2,1)S(1)}, u32[]{:S(2)}, u32[]{:S(2)}) collective-permute-start(bf16[128,1024]{1,0:T(8,128)(2,1)S(1)} %get-tuple-element.53), channel_id=1, source_target_pairs={{0,1},{1,0},{2,3},{3,2},{4,5},{5,4},{6,7},{7,6},{8,9},{9,8},{10,11... | collective-permute-start | bytes 786440 | tf_op jit(solution)/shard_map/ppermute | solution.py:66
  18.6 9.2 %collective-permute-start.11 = (bf16[256,1024]{1,0:T(8,128)(2,1)S(1)}, bf16[256,1024]{1,0:T(8,128)(2,1)S(1)}, u32[]{:S(2)}, u32[]{:S(2)}) collective-permute-start(bf16[256,1024]{1,0:T(8,128)(2,1)S(1)} %join.1.refs_1_.refs_3_), channel_id=1, source_target_pairs={{0,240},{16,224},{32,208},{48,192},{64,176},{80,160},{96,144},{112... | collective-permute-start | bytes 1572872 | tf_op jit(solution)/shard_map/panel/ppermute | solution.py:53
  27.8 2.8 %collective-permute-start = (bf16[8,128,128]{2,1,0:T(8,128)(2,1)S(1)}, bf16[8,128,128]{2,1,0:T(8,128)(2,1)S(1)}, u32[]{:S(2)}, u32[]{:S(2)}) collective-permute-start(bf16[8,128,128]{2,1,0:T(8,128)(2,1)S(1)} %get-tuple-element.51), channel_id=1, source_target_pairs={{0,1},{1,0},{2,3},{3,2},{4,5},{5,4},{6,7},{7,6},{8,9},{9,8},{10,11... | collective-permute-start | bytes 786440 | tf_op jit(solution)/shard_map/acts/ppermute | solution.py:66
  30.7 2.4 %collective-permute-done.5.refs_0_.refs_2_.refs_6_ = bf16[192,2048]{1,0:T(8,128)(2,1)S(1)} collective-permute-done((bf16[192,2048]{1,0:T(8,128)(2,1)S(1)}, bf16[192,2048]{1,0:T(8,128)(2,1)S(1)}, u32[]{:S(2)}, u32[]{:S(2)}) %collective-permute-start.5) | collective-permute-done | bytes 786464 | tf_op jit(solution)/shard_map/weight/up/ppermute | solution.py:66
  35.4 1.6 %collective-permute-start.8 = (bf16[64,2048]{1,0:T(8,128)(2,1)S(1)}, bf16[64,2048]{1,0:T(8,128)(2,1)S(1)}, u32[]{:S(2)}, u32[]{:S(2)}) collective-permute-start(bf16[64,2048]{1,0:T(8,128)(2,1)S(1)} %get-tuple-element.58), channel_id=1, source_target_pairs={{0,12},{1,13},{2,14},{3,15},{4,0},{5,1},{6,2},{7,3},{8,4},{9,5},{1... | collective-permute-start | bytes 786440 | tf_op jit(solution)/shard_map/weight/far_down/ppermute | solution.py:66
  38.1 3.0 %collective-permute-done.7.refs_4_.refs_8_ = bf16[64,2048]{1,0:T(8,128)(2,1)S(1)} collective-permute-done((bf16[64,2048]{1,0:T(8,128)(2,1)S(1)}, bf16[64,2048]{1,0:T(8,128)(2,1)S(1)}, u32[]{:S(2)}, u32[]{:S(2)}) %collective-permute-start.7) | collective-permute-done | bytes 262176 | tf_op jit(solution)/shard_map/weight/far_up/ppermute | solution.py:66
  42.0 8.9 %collective-permute-done.11.refs_0_ = bf16[256,1024]{1,0:T(8,128)(2,1)S(1)} collective-permute-done((bf16[256,1024]{1,0:T(8,128)(2,1)S(1)}, bf16[256,1024]{1,0:T(8,128)(2,1)S(1)}, u32[]{:S(2)}, u32[]{:S(2)}) %collective-permute-start.11) | collective-permute-done | bytes 524320 | tf_op jit(solution)/shard_map/panel/ppermute | solution.py:53
  50.9 2.2 %backward.1 = (f32[128,2176]{1,0:T(8,128)S(1)}, bf16[128,2304]{1,0:T(8,128)(2,1)S(1)}, f32[8,128]{1,0:T(8,128)}) custom-call(bf16[256,1024]{1,0:T(8,128)(2,1)S(1)} %collective-permute-done.11.refs_0_, f32[1,2048]{1,0:T(1,128)S(1)} %copy-done.12, bf16[128,2048]{1,0:T(8,128)(2,1)S(1)} %bitcast.7, bf16[128,2048]{1,0:T(8,128)(2,1)S(1)} %collective-permute-done.1.refs_0_.refs_3_, ...), custom_call_target="tpu_custom_call" | custom-call | flops 1140850688 | bytes 6434816 | tf_op jit(solution)/shard_map/backward/pallas_call | solution.py:38
  54.3 1.9 %collective-permute-done.12.refs_1_ = bf16[128,1024]{1,0:T(8,128)(2,1)S(1)} collective-permute-done((bf16[128,1024]{1,0:T(8,128)(2,1)S(1)}, bf16[128,1024]{1,0:T(8,128)(2,1)S(1)}, u32[]{:S(2)}, u32[]{:S(2)}) %collective-permute-start.12) | collective-permute-done | bytes 262176 | tf_op jit(solution)/shard_map/restore/ppermute | solution.py:66
  58.0 2.7 %collective-permute-start.19 = (bf16[128,2048]{1,0:T(8,128)(2,1)S(1)}, bf16[128,2048]{1,0:T(8,128)(2,1)S(1)}, u32[]{:S(2)}, u32[]{:S(2)}) collective-permute-start(bf16[128,2048]{1,0:T(8,128)(2,1)S(1)} %delta.1.refs_0_.refs_1_), channel_id=1, source_target_pairs={{0,12},{1,13},{2,14},{3,15},{4,0},{5,1},{6,2},{7,3},{8,4},{9,5},{1... | collective-permute-start | bytes 1572872 | tf_op jit(solution)/shard_map/delta/above/ppermute | solution.py:66
  61.0 2.1 %out.1 = (bf16[128,2048]{1,0:T(8,128)(2,1)}, f32[8,128]{1,0:T(8,128)S(1)}) custom-call(f32[128,2048]{1,0:T(8,128)S(1)} %get-tuple-element.61.refs_0_, bf16[128,2048]{1,0:T(8,128)(2,1)S(1)} %collective-permute-done.9.refs_1_, bf16[128,2048]{1,0:T(8,128)(2,1)} %bitcast.refs_0_.refs_2_), custom_call_target="tpu_custom_call" | custom-call | bytes 2625536 | tf_op jit(solution)/shard_map/out/pallas_call | solution.py:38
  65.6 6.9 %collective-permute-done.18.refs_0_.refs_2_ = bf16[128,2048]{1,0:T(8,128)(2,1)S(1)} collective-permute-done((bf16[128,2048]{1,0:T(8,128)(2,1)S(1)}, bf16[128,2048]{1,0:T(8,128)(2,1)S(1)}, u32[]{:S(2)}, u32[]{:S(2)}) %collective-permute-start.18) | collective-permute-done | bytes 524320 | tf_op jit(solution)/shard_map/delta/below/ppermute | solution.py:66
  74.7 2.7 %collective-permute-start.22 = (bf16[192,2048]{1,0:T(8,128)(2,1)}, bf16[192,2048]{1,0:T(8,128)(2,1)S(1)}, u32[]{:S(2)}, u32[]{:S(2)}) collective-permute-start(bf16[192,2048]{1,0:T(8,128)(2,1)} %get-tuple-element.77), channel_id=1, source_target_pairs={{0,12},{1,13},{2,14},{3,15},{4,0},{5,1},{6,2},{7,3},{8,4},{9,5},{1... | collective-permute-start | bytes 2359304 | tf_op jit(solution)/shard_map/delta/down/ppermute | solution.py:66
  77.7 5.7 %collective-permute-start.25 = (bf16[128,2048]{1,0:T(8,128)(2,1)}, bf16[128,2048]{1,0:T(8,128)(2,1)}, u32[]{:S(2)}, u32[]{:S(2)}) collective-permute-start(bf16[128,2048]{1,0:T(8,128)(2,1)} %bitcast.refs_0_.refs_2_), channel_id=1, source_target_pairs={{0,240},{16,224},{32,208},{48,192},{64,176},{80,160},{96,144},{112... | collective-permute-start | bytes 1572872 | tf_op jit(solution)/shard_map/stash/ppermute | solution.py:53
  86.4 3.5 %all-to-all-start = ((bf16[4,2,2,128,128]{4,3,2,1,0:T(8,128)(2,1)}), bf16[4,2,2,128,128]{4,3,2,1,0:T(8,128)(2,1)S(1)}, u32[]{:S(2)}, u32[]{:S(2)}) async-start(bf16[4,2,2,128,128]{4,3,2,1,0:T(8,128)(2,1)} %copy-done.10), calls=%async_computation | async-start | bytes 1048576 | tf_op jit(solution)/shard_map/all_to_all | solution.py:478
  89.8 3.6 %collective-permute-done.21.refs_0_.refs_5_ = bf16[192,2048]{1,0:T(8,128)(2,1)S(1)} collective-permute-done((bf16[192,2048]{1,0:T(8,128)(2,1)}, bf16[192,2048]{1,0:T(8,128)(2,1)S(1)}, u32[]{:S(2)}, u32[]{:S(2)}) %collective-permute-start.21) | collective-permute-done | bytes 786464 | tf_op jit(solution)/shard_map/delta/up/ppermute | solution.py:66
  94.3 2.6 %collective-permute-start.24 = (bf16[64,2048]{1,0:T(8,128)(2,1)}, bf16[64,2048]{1,0:T(8,128)(2,1)}, u32[]{:S(2)}, u32[]{:S(2)}) collective-permute-start(bf16[64,2048]{1,0:T(8,128)(2,1)} %get-tuple-element.79), channel_id=1, source_target_pairs={{0,12},{1,13},{2,14},{3,15},{4,0},{5,1},{6,2},{7,3},{8,4},{9,5},{1... | collective-permute-start | bytes 786440 | tf_op jit(solution)/shard_map/delta/far_down/ppermute | solution.py:66
  97.0 2.6 %all-to-all-done.refs_0_ = bf16[4,2,2,128,128]{4,3,2,1,0:T(8,128)(2,1)S(1)} async-done(((bf16[4,2,2,128,128]{4,3,2,1,0:T(8,128)(2,1)}), bf16[4,2,2,128,128]{4,3,2,1,0:T(8,128)(2,1)S(1)}, u32[]{:S(2)}, u32[]{:S(2)}) %all-to-all-start) | async-done | bytes 524320 | tf_op jit(solution)/shard_map/all_to_all | solution.py:478
  104.3 2.8 %collective-permute-done.25.refs_2_ = bf16[128,2048]{1,0:T(8,128)(2,1)} collective-permute-done((bf16[128,2048]{1,0:T(8,128)(2,1)}, bf16[128,2048]{1,0:T(8,128)(2,1)}, u32[]{:S(2)}, u32[]{:S(2)}) %collective-permute-start.25) | collective-permute-done | bytes 524320 | tf_op jit(solution)/shard_map/stash/ppermute | solution.py:53
  107.0 1.9 %park.1 = (bf16[1,3,128,2048]{3,2,1,0:T(8,128)(2,1)}, f32[8,128]{1,0:T(8,128)S(1)}) custom-call(s32[16]{0:T(128)S(1)} %copy-done.14, bf16[1,3,128,2048]{3,2,1,0:T(8,128)(2,1)} %get-tuple-element.83.refs_1_, bf16[128,2048]{1,0:T(8,128)(2,1)} %collective-permute-done.25.refs_2_, f32[8,128]{1,0:T(8,128)S(1)} %get-tuple-element.84.refs_3_), custom_call_target="tpu_custom_call", output_to_operand_aliasing={{0}: (1, {})} | custom-call | bytes 3674176 | tf_op jit(solution)/shard_map/park/pallas_call | solution.py:38
  108.9 8.2 %collective-permute-done.16.refs_6_.refs_1_ = bf16[128,2048]{1,0:T(8,128)(2,1)} collective-permute-done((bf16[128,2048]{1,0:T(8,128)(2,1)}, bf16[128,2048]{1,0:T(8,128)(2,1)}, u32[]{:S(2)}, u32[]{:S(2)}) %collective-permute-start.16) | collective-permute-done | bytes 524320 | tf_op jit(solution)/shard_map/next_grads/ppermute | solution.py:58
  117.1 1.6 %outer_far.1 = (f32[128,2048]{1,0:T(8,128)S(1)}, bf16[128,2048]{1,0:T(8,128)(2,1)S(1)}, f32[8,128]{1,0:T(8,128)S(1)}) custom-call(bf16[4,2,2,128,128]{4,3,2,1,0:T(8,128)(2,1)S(1)} %all-to-all-done.refs_0_, bf16[64,2048]{1,0:T(8,128)(2,1)} %collective-permute-done.23.refs_1_, bf16[64,2048]{1,0:T(8,128)(2,1)} %collective-permute-done.24.refs_2_, ...), custom_call_target="tpu_custom_call" | custom-call | flops 134217728 | bytes 4722688 | tf_op jit(solution)/shard_map/outer_far/pallas_call | solution.py:38
  120.0 2.2 %emit.1 = (bf16[1,128,2048]{2,1,0:T(8,128)(2,1)}, bf16[1,128,2048]{2,1,0:T(8,128)(2,1)}, f32[8,128]{1,0:T(8,128)S(1)}) custom-call(bf16[128,2048]{1,0:T(8,128)(2,1)} %collective-permute-done.10.refs_0_, bf16[128,2048]{1,0:T(8,128)(2,1)} %collective-permute-done.16.refs_6_.refs_1_, f32[8,128]{1,0:T(8,128)S(1)} %get-tuple-element.86.refs_2_), custom_call_target="tpu_custom_call" | custom-call | bytes 2101248 | tf_op jit(solution)/shard_map/emit/pallas_call | solution.py:38
  (85 shorter events, 37.7 us)
Async XLA Ops:
  0.6 13.5 %collective-permute-start.1 = (bf16[128,2048]{1,0:T(8,128)(2,1)}, bf16[128,2048]{1,0:T(8,128)(2,1)S(1)}, u32[]{:S(2)}, u32[]{:S(2)}) collective-permute-start(bf16[128,2048]{1,0:T(8,128)(2,1)} %bitcast.3), channel_id=1, source_target_pairs={{0,4},{1,5},{2,6},{3,7},{4,8},{5,9},{6,10},{7,11},{8,12},{9,13},{1... | collective-permute-start | bytes 1572872 | tf_op jit(solution)/shard_map/weight/below/ppermute | solution.py:66
  2.8 12.4 %collective-permute-start.2 = (bf16[128,2048]{1,0:T(8,128)(2,1)}, bf16[128,2048]{1,0:T(8,128)(2,1)S(1)}, u32[]{:S(2)}, u32[]{:S(2)}) collective-permute-start(bf16[128,2048]{1,0:T(8,128)(2,1)} %bitcast.4), channel_id=1, source_target_pairs={{0,12},{1,13},{2,14},{3,15},{4,0},{5,1},{6,2},{7,3},{8,4},{9,5},{1... | collective-permute-start | bytes 1572872 | tf_op jit(solution)/shard_map/weight/above/ppermute | solution.py:66
  4.4 11.4 %collective-permute-start.3 = (bf16[128,2048]{1,0:T(8,128)(2,1)}, bf16[128,2048]{1,0:T(8,128)(2,1)S(1)}, u32[]{:S(2)}, u32[]{:S(2)}) collective-permute-start(bf16[128,2048]{1,0:T(8,128)(2,1)} %bitcast.5), channel_id=1, source_target_pairs={{0,2},{1,3},{2,0},{3,1},{4,6},{5,7},{6,4},{7,5},{8,10},{9,11},{10,... | collective-permute-start | bytes 1572872 | tf_op jit(solution)/shard_map/weight/pair/ppermute | solution.py:66
  15.9 17.2 %collective-permute-start.5 = (bf16[192,2048]{1,0:T(8,128)(2,1)S(1)}, bf16[192,2048]{1,0:T(8,128)(2,1)S(1)}, u32[]{:S(2)}, u32[]{:S(2)}) collective-permute-start(bf16[192,2048]{1,0:T(8,128)(2,1)S(1)} %get-tuple-element.55), channel_id=1, source_target_pairs={{0,4},{1,5},{2,6},{3,7},{4,8},{5,9},{6,10},{7,11},{8,12},{9,13},{1... | collective-permute-start | bytes 2359304 | tf_op jit(solution)/shard_map/weight/up/ppermute | solution.py:66
  17.0 16.7 %collective-permute-start.6 = (bf16[192,2048]{1,0:T(8,128)(2,1)S(1)}, bf16[192,2048]{1,0:T(8,128)(2,1)S(1)}, u32[]{:S(2)}, u32[]{:S(2)}) collective-permute-start(bf16[192,2048]{1,0:T(8,128)(2,1)S(1)} %get-tuple-element.56), channel_id=1, source_target_pairs={{0,12},{1,13},{2,14},{3,15},{4,0},{5,1},{6,2},{7,3},{8,4},{9,5},{1... | collective-permute-start | bytes 2359304 | tf_op jit(solution)/shard_map/weight/down/ppermute | solution.py:66
  18.6 32.3 %collective-permute-start.11 = (bf16[256,1024]{1,0:T(8,128)(2,1)S(1)}, bf16[256,1024]{1,0:T(8,128)(2,1)S(1)}, u32[]{:S(2)}, u32[]{:S(2)}) collective-permute-start(bf16[256,1024]{1,0:T(8,128)(2,1)S(1)} %join.1.refs_1_.refs_3_), channel_id=1, source_target_pairs={{0,240},{16,224},{32,208},{48,192},{64,176},{80,160},{96,144},{112... | collective-permute-start | bytes 1572872 | tf_op jit(solution)/shard_map/panel/ppermute | solution.py:53
  27.8 9.2 %collective-permute-start = (bf16[8,128,128]{2,1,0:T(8,128)(2,1)S(1)}, bf16[8,128,128]{2,1,0:T(8,128)(2,1)S(1)}, u32[]{:S(2)}, u32[]{:S(2)}) collective-permute-start(bf16[8,128,128]{2,1,0:T(8,128)(2,1)S(1)} %get-tuple-element.51), channel_id=1, source_target_pairs={{0,1},{1,0},{2,3},{3,2},{4,5},{5,4},{6,7},{7,6},{8,9},{9,8},{10,11... | collective-permute-start | bytes 786440 | tf_op jit(solution)/shard_map/acts/ppermute | solution.py:66
  34.4 6.7 %collective-permute-start.7 = (bf16[64,2048]{1,0:T(8,128)(2,1)S(1)}, bf16[64,2048]{1,0:T(8,128)(2,1)S(1)}, u32[]{:S(2)}, u32[]{:S(2)}) collective-permute-start(bf16[64,2048]{1,0:T(8,128)(2,1)S(1)} %get-tuple-element.57), channel_id=1, source_target_pairs={{0,4},{1,5},{2,6},{3,7},{4,8},{5,9},{6,10},{7,11},{8,12},{9,13},{1... | collective-permute-start | bytes 786440 | tf_op jit(solution)/shard_map/weight/far_up/ppermute | solution.py:66
  35.4 5.7 %collective-permute-start.8 = (bf16[64,2048]{1,0:T(8,128)(2,1)S(1)}, bf16[64,2048]{1,0:T(8,128)(2,1)S(1)}, u32[]{:S(2)}, u32[]{:S(2)}) collective-permute-start(bf16[64,2048]{1,0:T(8,128)(2,1)S(1)} %get-tuple-element.58), channel_id=1, source_target_pairs={{0,12},{1,13},{2,14},{3,15},{4,0},{5,1},{6,2},{7,3},{8,4},{9,5},{1... | collective-permute-start | bytes 786440 | tf_op jit(solution)/shard_map/weight/far_down/ppermute | solution.py:66
  56.7 4.4 %collective-permute-start.9 = (bf16[128,2048]{1,0:T(8,128)(2,1)S(1)}, bf16[128,2048]{1,0:T(8,128)(2,1)S(1)}, u32[]{:S(2)}, u32[]{:S(2)}) collective-permute-start(bf16[128,2048]{1,0:T(8,128)(2,1)S(1)} %get-tuple-element.62), channel_id=1, source_target_pairs={{0,1},{1,0},{2,3},{3,2},{4,5},{5,4},{6,7},{7,6},{8,9},{9,8},{10,11... | collective-permute-start | bytes 1572872 | tf_op jit(solution)/shard_map/pre_acts/ppermute | solution.py:66
  57.7 5.5 %collective-permute-start.14 = (bf16[128,2048]{1,0:T(8,128)(2,1)S(1)}, bf16[128,2048]{1,0:T(8,128)(2,1)S(1)}, u32[]{:S(2)}, u32[]{:S(2)}) collective-permute-start(bf16[128,2048]{1,0:T(8,128)(2,1)S(1)} %delta.1.refs_0_.refs_1_), channel_id=1, source_target_pairs={{0,1},{1,0},{2,3},{3,2},{4,5},{5,4},{6,7},{7,6},{8,9},{9,8},{10,11... | collective-permute-start | bytes 1572872 | tf_op jit(solution)/shard_map/delta_other/ppermute | solution.py:66
  57.9 14.6 %collective-permute-start.18 = (bf16[128,2048]{1,0:T(8,128)(2,1)S(1)}, bf16[128,2048]{1,0:T(8,128)(2,1)S(1)}, u32[]{:S(2)}, u32[]{:S(2)}) collective-permute-start(bf16[128,2048]{1,0:T(8,128)(2,1)S(1)} %delta.1.refs_0_.refs_1_), channel_id=1, source_target_pairs={{0,4},{1,5},{2,6},{3,7},{4,8},{5,9},{6,10},{7,11},{8,12},{9,13},{1... | collective-permute-start | bytes 1572872 | tf_op jit(solution)/shard_map/delta/below/ppermute | solution.py:66
  58.0 14.5 %collective-permute-start.19 = (bf16[128,2048]{1,0:T(8,128)(2,1)S(1)}, bf16[128,2048]{1,0:T(8,128)(2,1)S(1)}, u32[]{:S(2)}, u32[]{:S(2)}) collective-permute-start(bf16[128,2048]{1,0:T(8,128)(2,1)S(1)} %delta.1.refs_0_.refs_1_), channel_id=1, source_target_pairs={{0,12},{1,13},{2,14},{3,15},{4,0},{5,1},{6,2},{7,3},{8,4},{9,5},{1... | collective-permute-start | bytes 1572872 | tf_op jit(solution)/shard_map/delta/above/ppermute | solution.py:66
  60.7 12.6 %collective-permute-start.20 = (bf16[128,2048]{1,0:T(8,128)(2,1)S(1)}, bf16[128,2048]{1,0:T(8,128)(2,1)S(1)}, u32[]{:S(2)}, u32[]{:S(2)}) collective-permute-start(bf16[128,2048]{1,0:T(8,128)(2,1)S(1)} %delta.1.refs_0_.refs_1_), channel_id=1, source_target_pairs={{0,2},{1,3},{2,0},{3,1},{4,6},{5,7},{6,4},{7,5},{8,10},{9,11},{10,... | collective-permute-start | bytes 1572872 | tf_op jit(solution)/shard_map/delta/pair/ppermute | solution.py:66
  64.4 19.0 %collective-permute-start.15 = (f32[8,128,128]{2,1,0:T(8,128)S(1)}, f32[8,128,128]{2,1,0:T(8,128)S(1)}, u32[]{:S(2)}, u32[]{:S(2)}) collective-permute-start(f32[8,128,128]{2,1,0:T(8,128)S(1)} %get-tuple-element.71), channel_id=1, source_target_pairs={{0,1},{1,0},{2,3},{3,2},{4,5},{5,4},{6,7},{7,6},{8,9},{9,8},{10,11... | collective-permute-start | bytes 1572872 | tf_op jit(solution)/shard_map/back/ppermute | solution.py:66
  74.7 18.8 %collective-permute-start.21 = (bf16[192,2048]{1,0:T(8,128)(2,1)}, bf16[192,2048]{1,0:T(8,128)(2,1)S(1)}, u32[]{:S(2)}, u32[]{:S(2)}) collective-permute-start(bf16[192,2048]{1,0:T(8,128)(2,1)} %get-tuple-element.76), channel_id=1, source_target_pairs={{0,4},{1,5},{2,6},{3,7},{4,8},{5,9},{6,10},{7,11},{8,12},{9,13},{1... | collective-permute-start | bytes 2359304 | tf_op jit(solution)/shard_map/delta/up/ppermute | solution.py:66
  74.7 18.8 %collective-permute-start.22 = (bf16[192,2048]{1,0:T(8,128)(2,1)}, bf16[192,2048]{1,0:T(8,128)(2,1)S(1)}, u32[]{:S(2)}, u32[]{:S(2)}) collective-permute-start(bf16[192,2048]{1,0:T(8,128)(2,1)} %get-tuple-element.77), channel_id=1, source_target_pairs={{0,12},{1,13},{2,14},{3,15},{4,0},{5,1},{6,2},{7,3},{8,4},{9,5},{1... | collective-permute-start | bytes 2359304 | tf_op jit(solution)/shard_map/delta/down/ppermute | solution.py:66
  77.4 7.6 %collective-permute-start.17 = (bf16[4,2,128,128]{3,2,1,0:T(8,128)(2,1)S(1)}, bf16[4,2,128,128]{3,2,1,0:T(8,128)(2,1)S(1)}, u32[]{:S(2)}, u32[]{:S(2)}) collective-permute-start(bf16[4,2,128,128]{3,2,1,0:T(8,128)(2,1)S(1)} %get-tuple-element.73), channel_id=1, source_target_pairs={{0,2},{1,3},{2,0},{3,1},{4,6},{5,7},{6,4},{7,5},{8,10},{9,11},{10,... | collective-permute-start | bytes 786440 | tf_op jit(solution)/shard_map/pair_units/ppermute | solution.py:66
  77.7 29.3 %collective-permute-start.25 = (bf16[128,2048]{1,0:T(8,128)(2,1)}, bf16[128,2048]{1,0:T(8,128)(2,1)}, u32[]{:S(2)}, u32[]{:S(2)}) collective-permute-start(bf16[128,2048]{1,0:T(8,128)(2,1)} %bitcast.refs_0_.refs_2_), channel_id=1, source_target_pairs={{0,240},{16,224},{32,208},{48,192},{64,176},{80,160},{96,144},{112... | collective-permute-start | bytes 1572872 | tf_op jit(solution)/shard_map/stash/ppermute | solution.py:53
  84.9 32.3 %collective-permute-start.16 = (bf16[128,2048]{1,0:T(8,128)(2,1)}, bf16[128,2048]{1,0:T(8,128)(2,1)}, u32[]{:S(2)}, u32[]{:S(2)}) collective-permute-start(bf16[128,2048]{1,0:T(8,128)(2,1)} %get-tuple-element.72), channel_id=1, source_target_pairs={{16,0},{32,16},{48,32},{64,48},{80,64},{96,80},{112,96},{128,112},... | collective-permute-start | bytes 1572872 | tf_op jit(solution)/shard_map/next_grads/ppermute | solution.py:58
  86.4 13.2 %all-to-all-start = ((bf16[4,2,2,128,128]{4,3,2,1,0:T(8,128)(2,1)}), bf16[4,2,2,128,128]{4,3,2,1,0:T(8,128)(2,1)S(1)}, u32[]{:S(2)}, u32[]{:S(2)}) async-start(bf16[4,2,2,128,128]{4,3,2,1,0:T(8,128)(2,1)} %copy-done.10), calls=%async_computation | async-start | bytes 1048576 | tf_op jit(solution)/shard_map/all_to_all | solution.py:478
  94.3 22.8 %collective-permute-start.23 = (bf16[64,2048]{1,0:T(8,128)(2,1)}, bf16[64,2048]{1,0:T(8,128)(2,1)}, u32[]{:S(2)}, u32[]{:S(2)}) collective-permute-start(bf16[64,2048]{1,0:T(8,128)(2,1)} %get-tuple-element.78), channel_id=1, source_target_pairs={{0,4},{1,5},{2,6},{3,7},{4,8},{5,9},{6,10},{7,11},{8,12},{9,13},{1... | collective-permute-start | bytes 786440 | tf_op jit(solution)/shard_map/delta/far_up/ppermute | solution.py:66
  94.3 22.8 %collective-permute-start.24 = (bf16[64,2048]{1,0:T(8,128)(2,1)}, bf16[64,2048]{1,0:T(8,128)(2,1)}, u32[]{:S(2)}, u32[]{:S(2)}) collective-permute-start(bf16[64,2048]{1,0:T(8,128)(2,1)} %get-tuple-element.79), channel_id=1, source_target_pairs={{0,12},{1,13},{2,14},{3,15},{4,0},{5,1},{6,2},{7,3},{8,4},{9,5},{1... | collective-permute-start | bytes 786440 | tf_op jit(solution)/shard_map/delta/far_down/ppermute | solution.py:66
  97.0 23.0 %collective-permute-start.10 = (bf16[128,2048]{1,0:T(8,128)(2,1)}, bf16[128,2048]{1,0:T(8,128)(2,1)}, u32[]{:S(2)}, u32[]{:S(2)}) collective-permute-start(bf16[128,2048]{1,0:T(8,128)(2,1)} %get-tuple-element.63), channel_id=1, source_target_pairs={{240,0},{0,16},{16,32},{32,48},{48,64},{64,80},{80,96},{96,112},{1... | collective-permute-start | bytes 1572872 | tf_op jit(solution)/shard_map/next_acts/ppermute | solution.py:58
  (19 other events, 101.2 us)
